TPU v7x, 32 devices: a whole 2x2x4 slice. The times are simulated.
32 devices in a mesh: band: 2 (over y), space: 16 (over z, x, core).
Axes of the slice: x: 2, y: 2, z: 4, core: 2. Of those that a mesh axis runs over, the one named last changes fastest.
Arguments:
- snapshots: float32 [1152, 8, 8192], P(None, 'band', 'space'), may hold values from -6 to 6
- quad_weights: float32 [8, 8192], P('band', 'space'), may hold values from 0.2 to 9, as said below
- freq_bins: int32 [16], replicated, may hold values from 1 to 127, as said below
- block_starts: int32 [8], replicated, may hold values from 0 to 896, as said below
Outputs:
- factor: float32 [16, 2, 8, 8], P('band')
- modes: float32 [16, 2, 8, 8, 8192], P('band', None, None, None, 'space')
Inputs may be any that keep to these rules, and one draw needn't show every extreme that they name: `freq_bins`: distinct and increasing; the first is 1 and the last is 127. `block_starts`: Increasing; the first is 0 and the last is 896; consecutive starts differ by 64 to 192. `quad_weights`: Positive.
All inputs are finite; a program needn't handle non-finite values.
Results may differ from a plain program's by a relative error of at most 0.000075.
Values sent between devices are 32-bit elements; how exact they have to be, the bound alone decides.
No kernel may reach another device: no remote copies, remote signals or barrier semaphores. Data moves between devices by JAX's collectives and lax.ppermute only.
A program may use at most 64 MiB of HBM per device.

v0:
```python
import math

import jax
import jax.numpy as jnp
from jax import lax
from jax.sharding import PartitionSpec as P

BLOCK = 256
NBLK = 8
NFREQ = 16
SLABS = 8


def from_partner(block, axis, apart):
    count = lax.axis_size(axis)
    route = []
    for low in range(count):
        high = low | 1 << apart
        if high != low and high < count:
            route += [(low, high), (high, low)]
    return lax.ppermute(block, axis, route)


def spectral_table(freq_bins, block_starts, total_times):
    moments = jnp.arange(total_times)
    offset = moments[None, :] - block_starts[:, None]
    inside = (offset >= 0) & (offset < BLOCK)
    position = offset.astype(jnp.float32)
    taper = 0.5 - 0.5 * jnp.cos(2.0 * math.pi * position / BLOCK)
    turns = jnp.mod(freq_bins[:, None, None] * offset[None, :, :], BLOCK).astype(jnp.float32)
    phase = 2.0 * math.pi * turns / BLOCK
    scaled = jnp.where(inside, taper, 0.0)[None] / math.sqrt(0.375 * BLOCK)
    table = jnp.stack([scaled * jnp.cos(phase), -scaled * jnp.sin(phase)], axis=1)
    return table.reshape(-1, total_times)


def spectra(snap_rows, weights, table):
    fluct = snap_rows - jnp.mean(snap_rows, axis=0, keepdims=True)
    coeffs = jnp.dot(
        table, fluct, precision=lax.Precision.HIGHEST, preferred_element_type=jnp.float32
    )
    return coeffs * jnp.sqrt(weights)[None, :]


def gram_local(coeffs, count):
    vectors = coeffs.reshape(coeffs.shape[0], 2 * coeffs.shape[2], -1)
    return jnp.einsum("fas,fbs->fab", vectors, vectors, precision=lax.Precision.HIGHEST) / count


def gram_split(moment):
    half = moment.shape[-1] // 2
    real_part = moment[:, :half, :half] + moment[:, half:, half:]
    imag_part = moment[:, :half, half:] - moment[:, half:, :half]
    return (real_part, imag_part)


def factor_pair(gram_real, gram_imag):
    order = gram_real.shape[-1]
    columns = jnp.arange(order)
    rows_real = []
    rows_imag = []
    for pivot_row in range(order):
        left_real = gram_real[:, pivot_row, :]
        left_imag = gram_imag[:, pivot_row, :]
        for earlier in range(pivot_row):
            coef_real = rows_real[earlier][:, pivot_row : pivot_row + 1]
            coef_imag = rows_imag[earlier][:, pivot_row : pivot_row + 1]
            left_real = left_real - (
                coef_real * rows_real[earlier] + coef_imag * rows_imag[earlier]
            )
            left_imag = left_imag - (
                coef_real * rows_imag[earlier] - coef_imag * rows_real[earlier]
            )
        pivot = jnp.sqrt(left_real[:, pivot_row : pivot_row + 1])
        rows_real.append(jnp.where(columns >= pivot_row, left_real / pivot, 0.0))
        rows_imag.append(jnp.where(columns > pivot_row, left_imag / pivot, 0.0))
    return (jnp.stack(rows_real, 1), jnp.stack(rows_imag, 1))


def invert_pair(fac_real, fac_imag):
    order = fac_real.shape[-1]
    identity = jnp.eye(order, dtype=fac_real.dtype)
    inv_real = [None] * order
    inv_imag = [None] * order
    for target in reversed(range(order)):
        acc_real = jnp.broadcast_to(identity[target], fac_real[:, 0, :].shape)
        acc_imag = jnp.zeros_like(acc_real)
        for later in range(target + 1, order):
            coef_real = fac_real[:, target, later : later + 1]
            coef_imag = fac_imag[:, target, later : later + 1]
            acc_real = acc_real - (coef_real * inv_real[later] - coef_imag * inv_imag[later])
            acc_imag = acc_imag - (coef_real * inv_imag[later] + coef_imag * inv_real[later])
        diagonal = fac_real[:, target, target : target + 1]
        inv_real[target] = acc_real / diagonal
        inv_imag[target] = acc_imag / diagonal
    return (jnp.stack(inv_real, 1), jnp.stack(inv_imag, 1))


def project(coeffs, inv_real, inv_imag):
    upper = jnp.stack([inv_real, inv_imag], 2)
    lower = jnp.stack([-inv_imag, inv_real], 2)
    kernel = jnp.stack([upper, lower], 1)
    flat = coeffs.reshape(coeffs.shape[0], 2, coeffs.shape[2], -1)
    result = jnp.einsum("fpacb,fpas->fcbs", kernel, flat, precision=lax.Precision.HIGHEST)
    return result.reshape(coeffs.shape)


def shards(snapshots, quad_weights, freq_bins, block_starts):
    total_times, local_slabs, slab_cells = snapshots.shape
    table = spectral_table(freq_bins, block_starts, total_times)
    coeffs = spectra(snapshots.reshape(total_times, -1), quad_weights.reshape(-1), table)
    coeffs = coeffs.reshape(NFREQ, 2, NBLK, local_slabs, slab_cells)
    count = SLABS * slab_cells * lax.axis_size("space")
    grouped = lax.all_to_all(coeffs, "band", split_axis=0, concat_axis=3, tiled=True)
    moment = gram_local(grouped, count)
    for level in range(lax.axis_size("space").bit_length() - 1):
        moment = moment + from_partner(moment, "space", level)
    fac_real, fac_imag = factor_pair(*gram_split(moment))
    modes = project(grouped, *invert_pair(fac_real, fac_imag))
    factor = jnp.stack([fac_real, fac_imag], 1)
    return (factor, modes)


def solution(mesh):
    placed = (P(None, "band", "space"), P("band", "space"), P(), P())
    return jax.shard_map(
        shards,
        mesh=mesh,
        in_specs=placed,
        out_specs=(P("band", None, None, None), P("band", None, None, None, "space")),
        check_vma=False,
    )
```

profile of v0, /device:TPU:0, one launch (start us, length us, event | category | flops | bytes accessed | tf_op | source)
XLA Modules:
  0.0 98.0 jit_solution(14072722822726179555)
XLA Ops:
  0.6 0.9 select_multiply_fusion
  1.5 0.7 iota_subtract_fusion
  2.2 5.4 %reduce_sum.9 = f32[4,512]{1,0:T(4,128)S(1)} reduce(f32[1152,4,512]{2,1,0:T(4,128)} %param.4, f32[]{:T(128)} %constant.21.clone.1), dimensions={0}, to_apply=%region_0.1 | reduce | flops 2357248 | bytes 9445380 | tf_op jit(solution)/shard_map/reduce_sum | solution.py:38
  7.7 4.9 %broadcast_subtract_fusion = f32[576,8,512]{2,1,0:T(8,128)S(1)} fusion(f32[576,8,512]{2,1,0:T(8,128)} %bitcast.223, f32[8,512]{1,0:T(8,128)S(1)} %bitcast.232), kind=kLoop, calls=%fused_computation | loop fusion | flops 2359296 | bytes 18890752 | tf_op jit(solution)/shard_map/sub | solution.py:38
  12.6 4.6 %copy.46 = f32[144,8,4,512]{3,1,2,0:T(8,128)S(1)} copy(f32[144,8,4,512]{3,2,1,0:T(4,128)S(1)} %bitcast.222) | data formatting | bytes 18874368
  17.3 2.4 %cosine_multiply_fusion = (f32[16,1,8,1152]{3,2,1,0:T(8,128)S(1)}, f32[16,1,8,1152]{3,2,1,0:T(8,128)S(1)}) fusion(s32[8,1152]{1,0:T(8,128)S(1)} %iota_subtract_fusion, s32[16]{0:T(128)S(1)} %copy-done.1, f32[8,1152]{1,0:T(8,128)S(1)} %get-tuple-element.185, f32[8,1152]{1,0:T(8,128)S(1)} %get-tuple-element.186), kind=kLoop, calls=%fused_computation.14 | loop fusion | flops 2359296 | bytes 1290304 | tf_op jit(solution)/shard_map/mul | solution.py:33
  19.8 10.4 %convolution_multiply_fusion = f32[256,2048]{1,0:T(8,128)} fusion(f32[256,1152]{1,0:T(8,128)S(1)} %bitcast.230, f32[1152,2048]{1,0:T(8,128)S(1)} %bitcast.221, f32[2048]{0:T(1024)S(1)} %bitcast.231), kind=kOutput, calls=%fused_computation.1 | convolution fusion | flops 7248281600 | bytes 12722176 | tf_op jit(solution)/shard_map/dot_general | solution.py:39
  30.2 4.2 %all-to-all-start = ((f32[16,2,8,4,512]{4,2,3,1,0:T(8,128)}), f32[16,2,8,4,512]{4,2,3,1,0:T(8,128)S(1)}, u32[]{:S(2)}, u32[]{:S(2)}) async-start(f32[16,2,8,4,512]{4,2,3,1,0:T(8,128)} %bitcast.227), calls=%async_computation | async-start | bytes 4194304 | tf_op jit(solution)/shard_map/all_to_all | solution.py:114
  34.5 25.8 %all-to-all-done = f32[16,2,8,4,512]{4,2,3,1,0:T(8,128)S(1)} async-done(((f32[16,2,8,4,512]{4,2,3,1,0:T(8,128)}), f32[16,2,8,4,512]{4,2,3,1,0:T(8,128)S(1)}, u32[]{:S(2)}, u32[]{:S(2)}) %all-to-all-start) | async-done | bytes 2097184 | tf_op jit(solution)/shard_map/all_to_all | solution.py:114
  60.5 2.7 %fusion.70 = f32[8,16,16]{2,1,0:T(8,128)S(1)} fusion(f32[8,16,4096]{2,1,0:T(8,128)S(1)} %bitcast.226), kind=kOutput, calls=%fused_computation.337 | convolution fusion | flops 100663296 | bytes 2105344 | tf_op jit(solution)/shard_map/fas,fbs->fab/dot_general | solution.py:47
  63.3 1.2 %collective-permute-done = f32[8,16,16]{2,0,1:T(8,128)S(1)} collective-permute-done((f32[8,16,16]{2,0,1:T(8,128)S(1)}, f32[8,16,16]{2,0,1:T(8,128)S(1)}, u32[]{:S(2)}, u32[]{:S(2)}) %collective-permute-start) | collective-permute-done | bytes 8224 | tf_op jit(solution)/shard_map/ppermute | solution.py:21
  64.6 1.8 %collective-permute-start.1 = (f32[8,16,16]{2,0,1:T(8,128)S(1)}, f32[8,16,16]{2,0,1:T(8,128)S(1)}, u32[]{:S(2)}, u32[]{:S(2)}) collective-permute-start(f32[8,16,16]{2,0,1:T(8,128)S(1)} %fusion.67), channel_id=1, source_target_pairs={{0,2},{2,0},{1,3},{3,1},{4,6},{6,4},{5,7},{7,5},{8,10},{10,8},{9,1... | collective-permute-start | bytes 24584 | tf_op jit(solution)/shard_map/ppermute | solution.py:21
  66.4 2.6 %collective-permute-done.1 = f32[8,16,16]{2,0,1:T(8,128)S(1)} collective-permute-done((f32[8,16,16]{2,0,1:T(8,128)S(1)}, f32[8,16,16]{2,0,1:T(8,128)S(1)}, u32[]{:S(2)}, u32[]{:S(2)}) %collective-permute-start.1) | collective-permute-done | bytes 8224 | tf_op jit(solution)/shard_map/ppermute | solution.py:21
  68.9 1.9 %collective-permute-start.2 = (f32[8,16,16]{2,0,1:T(8,128)S(1)}, f32[8,16,16]{2,0,1:T(8,128)S(1)}, u32[]{:S(2)}, u32[]{:S(2)}) collective-permute-start(f32[8,16,16]{2,0,1:T(8,128)S(1)} %add.1546), channel_id=1, source_target_pairs={{0,4},{4,0},{1,5},{5,1},{2,6},{6,2},{3,7},{7,3},{8,12},{12,8},{9,1... | collective-permute-start | bytes 24584 | tf_op jit(solution)/shard_map/ppermute | solution.py:21
  70.8 2.5 %collective-permute-done.2 = f32[8,16,16]{2,0,1:T(8,128)S(1)} collective-permute-done((f32[8,16,16]{2,0,1:T(8,128)S(1)}, f32[8,16,16]{2,0,1:T(8,128)S(1)}, u32[]{:S(2)}, u32[]{:S(2)}) %collective-permute-start.2) | collective-permute-done | bytes 8224 | tf_op jit(solution)/shard_map/ppermute | solution.py:21
  73.3 2.9 %collective-permute-start.3 = (f32[8,16,16]{2,0,1:T(8,128)S(1)}, f32[8,16,16]{2,0,1:T(8,128)S(1)}, u32[]{:S(2)}, u32[]{:S(2)}) collective-permute-start(f32[8,16,16]{2,0,1:T(8,128)S(1)} %add.1547), channel_id=1, source_target_pairs={{0,8},{8,0},{1,9},{9,1},{2,10},{10,2},{3,11},{11,3},{4,12},{12,4},... | collective-permute-start | bytes 24584 | tf_op jit(solution)/shard_map/ppermute | solution.py:21
  76.4 2.1 %collective-permute-done.3 = f32[8,16,16]{2,0,1:T(8,128)S(1)} collective-permute-done((f32[8,16,16]{2,0,1:T(8,128)S(1)}, f32[8,16,16]{2,0,1:T(8,128)S(1)}, u32[]{:S(2)}, u32[]{:S(2)}) %collective-permute-start.3) | collective-permute-done | bytes 8224 | tf_op jit(solution)/shard_map/ppermute | solution.py:21
  78.8 0.4 slice_reduce_fusion.76
  79.6 0.3 slice_reduce_fusion.75
  79.8 0.3 slice_reduce_fusion.74
  80.5 0.3 slice_reduce_fusion.73
  80.7 0.3 slice_reduce_fusion.72
  84.6 0.3 slice_reduce_fusion.63
  84.9 0.3 slice_reduce_fusion.13
  85.2 0.3 slice_reduce_fusion.62
  85.5 0.3 slice_reduce_fusion.25
  85.8 0.3 slice_reduce_fusion.61
  86.0 0.3 slice_reduce_fusion.60
  86.3 0.3 slice_reduce_fusion.35
  91.9 1.9 %fusion = f32[8,2,8,4096,1]{3,2,4,0,1:T(8,128)S(1)} fusion(f32[8,2,8,4096,1]{3,2,0,1,4:T(8,128)S(1)} %bitcast.228, f32[8,2,8,2,8]{4,0,2,3,1:T(8,128)S(1)} %pad_maximum_fusion.1), kind=kOutput, calls=%fused_computation.2 | convolution fusion | flops 100663296 | bytes 4202496 | tf_op jit(solution)/shard_map/fpacb,fpas->fcbs/dot_general | solution.py:104
  93.8 3.0 %copy.40 = f32[8,2,8,8,512]{4,3,2,1,0:T(8,128)} copy(f32[8,2,8,8,512]{4,2,3,0,1:T(8,128)S(1)} %bitcast.229) | data formatting | bytes 4194304
  97.4 0.6 copy.39
  (119 shorter events, 11.0 us)
Async XLA Ops:
  12.6 4.7 %copy-start = (f32[4,512]{1,0:T(4,128)S(1)}, f32[4,512]{1,0:T(4,128)}, u32[]{:S(2)}) copy-start(f32[4,512]{1,0:T(4,128)} %param.5) | copy-start | bytes 24580
  12.6 4.7 %copy-start.1 = (s32[16]{0:T(128)S(1)}, s32[16]{0:T(128)}, u32[]{:S(2)}) copy-start(s32[16]{0:T(128)} %param.6) | copy-start | bytes 196
  30.2 30.1 %all-to-all-start = ((f32[16,2,8,4,512]{4,2,3,1,0:T(8,128)}), f32[16,2,8,4,512]{4,2,3,1,0:T(8,128)S(1)}, u32[]{:S(2)}, u32[]{:S(2)}) async-start(f32[16,2,8,4,512]{4,2,3,1,0:T(8,128)} %bitcast.227), calls=%async_computation | async-start | bytes 4194304 | tf_op jit(solution)/shard_map/all_to_all | solution.py:114
  63.2 1.3 %collective-permute-start = (f32[8,16,16]{2,0,1:T(8,128)S(1)}, f32[8,16,16]{2,0,1:T(8,128)S(1)}, u32[]{:S(2)}, u32[]{:S(2)}) collective-permute-start(f32[8,16,16]{2,0,1:T(8,128)S(1)} %copy_multiply_fusion), channel_id=1, source_target_pairs={{0,1},{1,0},{2,3},{3,2},{4,5},{5,4},{6,7},{7,6},{8,9},{9,8},{10,11... | collective-permute-start | bytes 24584 | tf_op jit(solution)/shard_map/ppermute | solution.py:21
  64.6 4.3 %collective-permute-start.1 = (f32[8,16,16]{2,0,1:T(8,128)S(1)}, f32[8,16,16]{2,0,1:T(8,128)S(1)}, u32[]{:S(2)}, u32[]{:S(2)}) collective-permute-start(f32[8,16,16]{2,0,1:T(8,128)S(1)} %fusion.67), channel_id=1, source_target_pairs={{0,2},{2,0},{1,3},{3,1},{4,6},{6,4},{5,7},{7,5},{8,10},{10,8},{9,1... | collective-permute-start | bytes 24584 | tf_op jit(solution)/shard_map/ppermute | solution.py:21
  68.9 4.3 %collective-permute-start.2 = (f32[8,16,16]{2,0,1:T(8,128)S(1)}, f32[8,16,16]{2,0,1:T(8,128)S(1)}, u32[]{:S(2)}, u32[]{:S(2)}) collective-permute-start(f32[8,16,16]{2,0,1:T(8,128)S(1)} %add.1546), channel_id=1, source_target_pairs={{0,4},{4,0},{1,5},{5,1},{2,6},{6,2},{3,7},{7,3},{8,12},{12,8},{9,1... | collective-permute-start | bytes 24584 | tf_op jit(solution)/shard_map/ppermute | solution.py:21
  73.3 5.2 %collective-permute-start.3 = (f32[8,16,16]{2,0,1:T(8,128)S(1)}, f32[8,16,16]{2,0,1:T(8,128)S(1)}, u32[]{:S(2)}, u32[]{:S(2)}) collective-permute-start(f32[8,16,16]{2,0,1:T(8,128)S(1)} %add.1547), channel_id=1, source_target_pairs={{0,8},{8,0},{1,9},{9,1},{2,10},{10,2},{3,11},{11,3},{4,12},{12,4},... | collective-permute-start | bytes 24584 | tf_op jit(solution)/shard_map/ppermute | solution.py:21
where the time goes:
time: 98.3 us; the launch traced here: 98 us
  waiting for transfers between devices  34.1 us (35%)
  other arithmetic  19.8 us (20%)
  local copies, waits for them, and re-layouts  17 us (17%)
  matrix products  15.1 us (15%)
  starting transfers between devices  10.8 us (11%)
  between operations  1.13 us (1%)
    all_to_all x1, waiting for transfers between devices, shards(): lax.all_to_all(coeffs, 'band', split_axis=0, concat_axis=3, tiled=True)  25.8 us
    dot_general x1, matrix products, spectra(): jnp.dot(table, fluct, precision=lax.Precision.HIGHEST, preferred_element_...  10.4 us
    ppermute x4, waiting for transfers between devices, from_partner(): return lax.ppermute(block, axis, route)  8.37 us
    unnamed x21, local copies, waits for them, and re-layouts  8.31 us
    ppermute x4, starting transfers between devices, from_partner(): return lax.ppermute(block, axis, route)  6.57 us
    reduce_sum x1, other arithmetic, spectra(): fluct = snap_rows - jnp.mean(snap_rows, axis=0, keepdims=True)  5.45 us
    sub x1, other arithmetic, spectra(): fluct = snap_rows - jnp.mean(snap_rows, axis=0, keepdims=True)  4.86 us
    all_to_all x1, starting transfers between devices, shards(): lax.all_to_all(coeffs, 'band', split_axis=0, concat_axis=3, tiled=True)  4.23 us
  transfers between devices with their start and end apart: 5, of which 5 were waited for; matrix products, arithmetic and copies ran while one was open for 0% of the time, Pallas kernels for 0%

commit v1 on v0

--- a/solution.py
+++ b/solution.py
@@ -3,12 +3,21 @@
 import jax
 import jax.numpy as jnp
 from jax import lax
+from jax.experimental import pallas as pl
+from jax.experimental.pallas import tpu as pltpu
 from jax.sharding import PartitionSpec as P
 
 BLOCK = 256
 NBLK = 8
 NFREQ = 16
 SLABS = 8
+GAP_LOW = 64
+GAP_HIGH = 192
+LANES = 128
+ROWS = 8
+VMEM_BYTES = 48 * 1024 * 1024
+PAIRS = [(a, b) for a in range(NBLK) for b in range(a, NBLK)]
+ENTRIES = [(0, a, b) for a, b in PAIRS] + [(1, a, b) for a, b in PAIRS if a < b]
 
 
 def from_partner(block, axis, apart):
@@ -105,7 +114,7 @@
     return result.reshape(coeffs.shape)
 
 
-def shards(snapshots, quad_weights, freq_bins, block_starts):
+def any_bands(snapshots, quad_weights, freq_bins, block_starts):
     total_times, local_slabs, slab_cells = snapshots.shape
     table = spectral_table(freq_bins, block_starts, total_times)
     coeffs = spectra(snapshots.reshape(total_times, -1), quad_weights.reshape(-1), table)
@@ -121,6 +130,353 @@
     return (factor, modes)
 
 
+def reach(total_times):
+    last = total_times - BLOCK
+    spans = []
+    for j in range(NBLK):
+        low = max(GAP_LOW * j, last - GAP_HIGH * (NBLK - 1 - j))
+        high = min(GAP_HIGH * j, last - GAP_LOW * (NBLK - 1 - j))
+        spans.append((low, high + BLOCK))
+    return spans
+
+
+def fill_table(freq_ref, start_ref, high_ref, low_ref):
+    band = lax.axis_index("band")
+    wide = BLOCK + LANES
+    row = lax.broadcasted_iota(jnp.int32, (NFREQ, wide), 0)
+    spot = lax.broadcasted_iota(jnp.int32, (NFREQ, wide), 1)
+    bins = jnp.zeros((NFREQ, wide), jnp.int32)
+    half = NFREQ // 2
+    for r in range(NFREQ):
+        owner = 1 - band if r < half else band
+        bins = jnp.where(row == r, freq_ref[owner * half + r % half], bins)
+    step = 2.0 * math.pi / BLOCK
+    phase = ((bins * spot) & (BLOCK - 1)).astype(jnp.float32) * step
+    taper = 0.5 - 0.5 * jnp.cos(spot.astype(jnp.float32) * step)
+    scaled = jnp.where(spot < BLOCK, taper, 0.0) * (1.0 / math.sqrt(0.375 * BLOCK))
+    parts = (scaled * jnp.cos(phase), -scaled * jnp.sin(phase))
+    high_ref[...] = jnp.zeros_like(high_ref)
+    low_ref[...] = jnp.zeros_like(low_ref)
+    for j in range(NBLK):
+        start = start_ref[j]
+        shift = start % LANES
+        place = pl.ds(pl.multiple_of(start - shift, LANES), wide)
+        for p in range(2):
+            moved = pltpu.roll(parts[p], shift, 1)
+            high = moved.astype(jnp.bfloat16)
+            low = (moved - high.astype(jnp.float32)).astype(jnp.bfloat16)
+            rows = pl.ds((2 * j + p) * NFREQ, NFREQ)
+            high_ref[rows, place] = high
+            low_ref[rows, place] = low
+
+
+def coeff_chunk(flow_ref, weight, high_ref, low_ref, fhigh_ref, flow_low_ref, acc_ref, slabs):
+    total = flow_ref.shape[0] // slabs
+    for l in range(slabs):
+        values = flow_ref[pl.ds(l, total, stride=slabs), :]
+        fluct = values - jnp.sum(values, axis=0, keepdims=True) * (1.0 / total)
+        high = fluct.astype(jnp.bfloat16)
+        fhigh_ref[:, l * LANES : (l + 1) * LANES] = high
+        flow_low_ref[:, l * LANES : (l + 1) * LANES] = (fluct - high.astype(jnp.float32)).astype(
+            jnp.bfloat16
+        )
+    per_block = 2 * NFREQ
+    spans = reach(total)
+    started = [False] * NBLK
+    for t0 in range(0, total, BLOCK):
+        t1 = min(t0 + BLOCK, total)
+        hit = [j for j in range(NBLK) if spans[j][0] < t1 and spans[j][1] > t0]
+        j0, j1 = min(hit), max(hit) + 1
+        rows = slice(j0 * per_block, j1 * per_block)
+        xh, xl = fhigh_ref[t0:t1, :], flow_low_ref[t0:t1, :]
+        th, tl = high_ref[rows, t0:t1], low_ref[rows, t0:t1]
+        part = jnp.dot(th, xl, preferred_element_type=jnp.float32)
+        part += jnp.dot(tl, xh, preferred_element_type=jnp.float32)
+        part += jnp.dot(th, xh, preferred_element_type=jnp.float32)
+        for j in range(j0, j1):
+            own = slice(j * per_block, (j + 1) * per_block)
+            piece = part[(j - j0) * per_block : (j - j0 + 1) * per_block]
+            acc_ref[own, :] = acc_ref[own, :] + piece if started[j] else piece
+            started[j] = True
+    root = jnp.concatenate([jnp.sqrt(weight[l : l + 1, :]) for l in range(slabs)], axis=1)
+    return root
+
+
+def store_chunk(acc_ref, root, send_ref, own_ref, at):
+    cols = root.shape[1]
+    for jp in range(2 * NBLK):
+        piece = acc_ref[jp * 2 * ROWS : (jp + 1) * 2 * ROWS, :] * root
+        send_ref[jp, :, at : at + cols] = piece[:ROWS]
+        own_ref[jp, :, at : at + cols] = piece[ROWS:]
+
+
+def spectra_kernel(slabs, first, count, freq_ref, start_ref, snap_ref, weight_ref, *rest):
+    send_ref, own_ref, held, high_ref, low_ref, fh_ref, fl_ref, acc_ref, sems = rest
+    copies = []
+    for i in range(count):
+        source = snap_ref.at[:, :, pl.ds((first + i) * LANES, LANES)]
+        copies.append(pltpu.make_async_copy(source, held.at[i], sems.at[i]))
+        copies[-1].start()
+    fill_table(freq_ref, start_ref, high_ref, low_ref)
+    total = snap_ref.shape[0]
+    for i in range(count):
+        copies[i].wait()
+        flat = held.at[i].reshape(total * slabs, LANES)
+        weight = weight_ref[:, (first + i) * LANES : (first + i + 1) * LANES]
+        root = coeff_chunk(flat, weight, high_ref, low_ref, fh_ref, fl_ref, acc_ref, slabs)
+        store_chunk(acc_ref, root, send_ref, own_ref, i * slabs * LANES)
+
+
+def spectra_call(snapshots, weights, freq_bins, block_starts, first, count):
+    total, slabs, _ = snapshots.shape
+    cols = slabs * LANES
+    shape = jax.ShapeDtypeStruct((2 * NBLK, ROWS, count * cols), jnp.float32)
+    wide = -(-total // LANES) * LANES + LANES
+    return pl.pallas_call(
+        lambda *refs: spectra_kernel(slabs, first, count, *refs),
+        out_shape=(shape, shape),
+        in_specs=[
+            pl.BlockSpec(memory_space=pltpu.SMEM),
+            pl.BlockSpec(memory_space=pltpu.SMEM),
+            pl.BlockSpec(memory_space=pl.ANY),
+            pl.BlockSpec(memory_space=pltpu.VMEM),
+        ],
+        out_specs=(pl.BlockSpec(memory_space=pltpu.VMEM),) * 2,
+        scratch_shapes=[
+            pltpu.VMEM((count, total, slabs, LANES), jnp.float32),
+            pltpu.VMEM((2 * NBLK * NFREQ, wide), jnp.bfloat16),
+            pltpu.VMEM((2 * NBLK * NFREQ, wide), jnp.bfloat16),
+            pltpu.VMEM((total, cols), jnp.bfloat16),
+            pltpu.VMEM((total, cols), jnp.bfloat16),
+            pltpu.VMEM((2 * NBLK * NFREQ, cols), jnp.float32),
+            pltpu.SemaphoreType.DMA((count,)),
+        ],
+        compiler_params=pltpu.CompilerParams(vmem_limit_bytes=VMEM_BYTES),
+        name="spectra",
+    )(freq_bins, block_starts, snapshots, weights)
+
+
+def lane_places(count):
+    bits = LANES.bit_length() - 1
+    used = count.bit_length() - 1
+    lanes = []
+    for e in range(count):
+        lane = 0
+        for level in range(used):
+            if e >> (used - 1 - level) & 1:
+                lane |= 1 << level
+        lanes.append(lane)
+    return lanes
+
+
+def fold_lanes(terms):
+    lane = lax.broadcasted_iota(jnp.int32, (ROWS, LANES), 1)
+    apart = 1
+    while len(terms) > 1:
+        half = len(terms) // 2
+        kept = (lane & apart) == 0
+        merged = []
+        for i in range(half):
+            first, second = terms[i], terms[i + half]
+            stay = jnp.where(kept, first, second)
+            go = jnp.where(kept, second, first)
+            fold = jnp.where(
+                kept, pltpu.roll(go, LANES - apart, 1), pltpu.roll(go, apart, 1)
+            )
+            merged.append(stay + fold)
+        terms = merged
+        apart *= 2
+    total = terms[0]
+    while apart < LANES:
+        total = total + pltpu.roll(total, apart, 1)
+        apart *= 2
+    return total
+
+
+def gram_kernel(*refs):
+    blocks, outs = refs[:-2], refs[-2:]
+    pairs = len(blocks) // 2
+    for side in range(2):
+        sums = {}
+        for a in range(NBLK):
+            row = [(0, a, b) for b in range(a, NBLK)] + [(1, a, b) for b in range(a + 1, NBLK)]
+            carry = tuple(jnp.zeros((ROWS, LANES), jnp.float32) for _ in row)
+            for i in range(pairs):
+                ref = blocks[2 * i + side]
+
+                def body(k, carry, ref=ref, a=a, row=row):
+                    cols = pl.ds(pl.multiple_of(k * LANES, LANES), LANES)
+                    re = {b: ref[2 * b, :, cols] for b in range(a, NBLK)}
+                    im = {b: ref[2 * b + 1, :, cols] for b in range(a, NBLK)}
+                    out = []
+                    for (kind, _, b), total in zip(row, carry):
+                        if kind == 0:
+                            out.append(total + (re[a] * re[b] + im[a] * im[b]))
+                        else:
+                            out.append(total + (re[a] * im[b] - im[a] * re[b]))
+                    return tuple(out)
+
+                carry = lax.fori_loop(0, ref.shape[2] // LANES, body, carry, unroll=4)
+            for key, total in zip(row, carry):
+                sums[key] = total
+        outs[side][...] = fold_lanes([sums[key] for key in ENTRIES])
+
+
+def gram_call(*blocks):
+    shape = jax.ShapeDtypeStruct((ROWS, LANES), jnp.float32)
+    return pl.pallas_call(
+        gram_kernel,
+        out_shape=(shape, shape),
+        in_specs=[pl.BlockSpec(memory_space=pltpu.VMEM)] * len(blocks),
+        out_specs=(pl.BlockSpec(memory_space=pltpu.VMEM),) * 2,
+        compiler_params=pltpu.CompilerParams(vmem_limit_bytes=VMEM_BYTES),
+        name="gram",
+    )(*blocks)
+
+
+def factor_kernel(count, sum_ref, inv_ref, fac_ref):
+    total = sum_ref[...] * (1.0 / count)
+    wide = lambda v: jnp.broadcast_to(v, (ROWS, LANES))
+    gram = {
+        key: wide(total[:, lane : lane + 1]) for key, lane in zip(ENTRIES, lane_places(len(ENTRIES)))
+    }
+    fac, recip = {}, []
+    for r in range(NBLK):
+        for c in range(r, NBLK):
+            real = gram[0, r, c]
+            imag = gram[1, r, c] if c > r else None
+            for e in range(r):
+                ar, ai = fac[0, e, r], fac[1, e, r]
+                br, bi = fac[0, e, c], fac[1, e, c]
+                real = real - (ar * br + ai * bi)
+                if c > r:
+                    imag = imag - (ar * bi - ai * br)
+            if c == r:
+                pivot = jnp.sqrt(real)
+                fac[0, r, r] = pivot
+                recip.append(1.0 / pivot)
+            else:
+                fac[0, r, c] = real * recip[r]
+                fac[1, r, c] = imag * recip[r]
+    inv = {}
+    for b in range(NBLK):
+        inv[0, b, b] = recip[b]
+        for a in reversed(range(b)):
+            real = imag = jnp.zeros((ROWS, LANES), jnp.float32)
+            for k in range(a + 1, b + 1):
+                cr, ci = fac[0, a, k], fac[1, a, k]
+                real = real - cr * inv[0, k, b]
+                imag = imag - ci * inv[0, k, b]
+                if k < b:
+                    real = real + ci * inv[1, k, b]
+                    imag = imag - cr * inv[1, k, b]
+            inv[0, a, b] = real * recip[a]
+            inv[1, a, b] = imag * recip[a]
+    for e, key in enumerate(ENTRIES):
+        inv_ref[e] = inv[key]
+    lane = lax.broadcasted_iota(jnp.int32, (ROWS, LANES), 1)
+    for p in range(2):
+        for a in range(NBLK):
+            line = jnp.zeros((ROWS, LANES), jnp.float32)
+            for b in range(a + p, NBLK):
+                line = jnp.where(lane == b, fac[p, a, b], line)
+            fac_ref[pl.ds(p * NBLK + a, ROWS, stride=2 * NBLK), :] = line
+
+
+def factor_call(total, count):
+    return pl.pallas_call(
+        lambda *refs: factor_kernel(count, *refs),
+        out_shape=(
+            jax.ShapeDtypeStruct((len(ENTRIES), ROWS, LANES), jnp.float32),
+            jax.ShapeDtypeStruct((ROWS * 2 * NBLK, LANES), jnp.float32),
+        ),
+        in_specs=[pl.BlockSpec(memory_space=pltpu.VMEM)],
+        out_specs=(pl.BlockSpec(memory_space=pltpu.VMEM),) * 2,
+        compiler_params=pltpu.CompilerParams(vmem_limit_bytes=VMEM_BYTES),
+        name="factor",
+    )(total)
+
+
+def project_kernel(slabs, inv_ref, own_ref, far_ref, *rest):
+    out_ref = rest[-1]
+    band = lax.axis_index("band")
+    per = 2 * NBLK * 2 * slabs
+    flat = out_ref.reshape(ROWS * per, LANES)
+    for side, ref in enumerate((own_ref, far_ref)):
+        base = (band if side == 0 else 1 - band) * slabs
+
+        def body(l, _, ref=ref, base=base):
+            cols = pl.ds(pl.multiple_of(l * LANES, LANES), LANES)
+            re = [ref[2 * a, :, cols] for a in range(NBLK)]
+            im = [ref[2 * a + 1, :, cols] for a in range(NBLK)]
+            for b in range(NBLK):
+                diagonal = inv_ref[ENTRIES.index((0, b, b))]
+                real, imag = re[b] * diagonal, im[b] * diagonal
+                for a in range(b):
+                    cr = inv_ref[ENTRIES.index((0, a, b))]
+                    ci = inv_ref[ENTRIES.index((1, a, b))]
+                    real = real + (re[a] * cr - im[a] * ci)
+                    imag = imag + (re[a] * ci + im[a] * cr)
+                for p, value in enumerate((real, imag)):
+                    line = (p * NBLK + b) * 2 * slabs + base + l
+                    flat[pl.ds(line, ROWS, stride=per), :] = value
+            return 0
+
+        lax.fori_loop(0, slabs, body, 0, unroll=2)
+
+
+def project_call(inv, own, far, modes, at, slabs, chunks):
+    count = own.shape[2] // (slabs * LANES)
+    block = (ROWS, 2 * NBLK, None, 2 * slabs, LANES)
+    given = [] if modes is None else [modes]
+    cols = slabs * LANES
+    spec = pl.BlockSpec((2 * NBLK, ROWS, cols), lambda i: (0, 0, i))
+    return pl.pallas_call(
+        lambda *refs: project_kernel(slabs, *refs),
+        grid=(count,),
+        out_shape=jax.ShapeDtypeStruct((ROWS, 2 * NBLK, chunks, 2 * slabs, LANES), jnp.float32),
+        in_specs=[pl.BlockSpec(inv.shape, lambda i: (0, 0, 0)), spec, spec]
+        + [pl.BlockSpec(memory_space=pl.ANY)] * len(given),
+        out_specs=pl.BlockSpec(block, lambda i: (0, 0, at + i, 0, 0)),
+        input_output_aliases={3: 0} if given else {},
+        compiler_params=pltpu.CompilerParams(vmem_limit_bytes=VMEM_BYTES),
+        name="project",
+    )(inv, own, far, *given)
+
+
+def swap_bands(block):
+    return lax.ppermute(block, "band", [(0, 1), (1, 0)])
+
+
+def two_bands(snapshots, quad_weights, freq_bins, block_starts):
+    slabs, cells = snapshots.shape[1:]
+    chunks = cells // LANES
+    count = 2 * slabs * cells * lax.axis_size("space")
+    given = (snapshots, quad_weights, freq_bins, block_starts)
+    send_a, own_a = spectra_call(*given, 0, 1)
+    far_a = swap_bands(send_a)
+    send_b, own_b = spectra_call(*given, 1, chunks - 1)
+    gram_send, gram_own = gram_call(send_a, own_a, send_b, own_b)
+    total = gram_own + swap_bands(gram_send)
+    far_b = swap_bands(send_b)
+    for level in range(lax.axis_size("space").bit_length() - 1):
+        total = total + from_partner(total, "space", level)
+    inv, fac = factor_call(total, count)
+    modes = project_call(inv, own_a, far_a, None, 0, slabs, chunks)
+    modes = project_call(inv, own_b, far_b, modes, 1, slabs, chunks)
+    modes = modes.reshape(ROWS, 2, NBLK, chunks, 2 * slabs, LANES)
+    modes = modes.transpose(0, 1, 2, 4, 3, 5).reshape(ROWS, 2, NBLK, 2 * slabs, cells)
+    factor = fac[:, :NBLK].reshape(ROWS, 2, NBLK, NBLK)
+    return (factor, modes)
+
+
+def shards(snapshots, *others):
+    fits = NFREQ == ROWS * lax.axis_size("band") == 2 * ROWS
+    fits = fits and snapshots.shape[1] == SLABS // 2 and snapshots.shape[2] % LANES == 0
+    fits = fits and snapshots.shape[2] > LANES and snapshots.shape[0] % LANES == 0
+    return (two_bands if fits else any_bands)(snapshots, *others)
+
+
 def solution(mesh):
     placed = (P(None, "band", "space"), P("band", "space"), P(), P())
     return jax.shard_map(

time: 98.3 us -> 52.9 us (0.54)
  other arithmetic: 19.8 us -> 0.02 us
  Pallas kernels: 0 us -> 16.9 us
  matrix products: 15.1 us -> 0 us
  local copies, waits for them, and re-layouts: 17 us -> 2 us
  waiting for transfers between devices: 34.1 us -> 21.6 us
    all_to_all x1 -> x0, waiting for transfers between devices: 25.8 us -> none  [shards(): lax.all_to_all(coeffs, 'band', split_axis=0, concat_axis=3, tiled=True)]
    pallas_call x0 -> x6, Pallas kernels: none -> 16.9 us  [the longest x2 9.29 us: spectra_call(): pl.pallas_call(lambda *refs: spectra_kernel(slabs, first, count, *refs),...]
    dot_general x3 -> x0, matrix products: 15.1 us -> none  [the longest x1 10.4 us: spectra(): jnp.dot(table, fluct, precision=lax.Precision.HIGHEST, preferred_element_...]
    ppermute x0 -> x3, waiting for transfers between devices: none -> 15 us  [swap_bands(): return lax.ppermute(block, 'band', [(0, 1), (1, 0)])]
    slice x29 -> x0, local copies, waits for them, and re-layouts: 6.75 us -> none  [the longest x7 1.77 us: factor_pair(): coef_imag = rows_imag[earlier][:, pivot_row:pivot_row + 1]]
    unnamed x21 -> x6, local copies, waits for them, and re-layouts: 8.31 us -> 2 us
    sub x9 -> x0, other arithmetic: 6.29 us -> none  [the longest x1 4.86 us: spectra(): fluct = snap_rows - jnp.mean(snap_rows, axis=0, keepdims=True)]
    reduce_sum x1 -> x0, other arithmetic: 5.45 us -> none  [spectra(): fluct = snap_rows - jnp.mean(snap_rows, axis=0, keepdims=True)]
  transfers between devices with their start and end apart: 5 -> 7, of which waited for: 5 -> 5; matrix products, arithmetic and copies ran while one was open for 0% -> 0% of each run, Pallas kernels for 0% -> 16%
where the time goes in v1:
time: 52.9 us; the launch traced here: 52.7 us
  waiting for transfers between devices  21.6 us (41%)
  Pallas kernels  16.9 us (32%)
  starting transfers between devices  11.4 us (22%)
  local copies, waits for them, and re-layouts  2 us (4%)
  between operations  0.67 us (1%)
    ppermute x3, waiting for transfers between devices, swap_bands(): return lax.ppermute(block, 'band', [(0, 1), (1, 0)])  15 us
    pallas_call x2, Pallas kernels, spectra_call(): pl.pallas_call(lambda *refs: spectra_kernel(slabs, first, count, *refs),...  9.29 us
    ppermute x4, waiting for transfers between devices, from_partner(): return lax.ppermute(block, axis, route)  6.57 us
    ppermute x4, starting transfers between devices, from_partner(): return lax.ppermute(block, axis, route)  6.32 us
    ppermute x3, starting transfers between devices, swap_bands(): return lax.ppermute(block, 'band', [(0, 1), (1, 0)])  5.13 us
    pallas_call x2, Pallas kernels, project_call(): pl.pallas_call(lambda *refs: project_kernel(slabs, *refs), grid=(count,),...  4.18 us
    pallas_call x1, Pallas kernels, gram_call(): pl.pallas_call(gram_kernel, out_shape=(shape, shape), in_specs=[pl.BlockS...  2.59 us
    unnamed x6, local copies, waits for them, and re-layouts  2 us
  transfers between devices with their start and end apart: 7, of which 5 were waited for; matrix products, arithmetic and copies ran while one was open for 0% of the time, Pallas kernels for 16%

profile of v1, /device:TPU:0, one launch (start us, length us, event | category | flops | bytes accessed | tf_op | source)
XLA Modules:
  0.0 52.7 jit_solution(14615215184791207382)
XLA Ops:
  0.6 0.0 copy-start
  0.6 0.7 %copy-done = f32[4,512]{1,0:T(4,128)S(1)} copy-done((f32[4,512]{1,0:T(4,128)S(1)}, f32[4,512]{1,0:T(4,128)}, u32[]{:S(2)}) %copy-start) | copy-done | bytes 8216
  1.3 0.0 copy-start.1
  1.3 0.7 %copy-done.1 = s32[16]{0:T(128)S(1)} copy-done((s32[16]{0:T(128)S(1)}, s32[16]{0:T(128)}, u32[]{:S(2)}) %copy-start.1) | copy-done | bytes 88
  2.0 0.0 copy-start.2
  2.0 0.7 %copy-done.2 = s32[8]{0:T(128)S(1)} copy-done((s32[8]{0:T(128)S(1)}, s32[8]{0:T(128)}, u32[]{:S(2)}) %copy-start.2) | copy-done | bytes 56
  2.6 5.8 %spectra.3 = (f32[16,8,1536]{2,1,0:T(8,128)S(1)}, f32[16,8,1536]{2,1,0:T(8,128)S(1)}) custom-call(s32[16]{0:T(128)S(1)} %copy-done.1, s32[8]{0:T(128)S(1)} %copy-done.2, f32[1152,4,512]{2,1,0:T(4,128)} %refs_2_.3, f32[4,512]{1,0:T(4,128)S(1)} %copy-done), custom_call_target="tpu_custom_call" | custom-call | tf_op jit(solution)/shard_map/spectra/pallas_call | solution.py:235
  8.4 3.0 %collective-permute-start.5 = (f32[16,8,1536]{2,1,0:T(8,128)S(1)}, f32[16,8,1536]{2,1,0:T(8,128)S(1)}, u32[]{:S(2)}, u32[]{:S(2)}) collective-permute-start(f32[16,8,1536]{2,1,0:T(8,128)S(1)} %get-tuple-element.12.refs_2_), channel_id=1, source_target_pairs={{0,16},{16,0},{1,17},{17,1},{2,18},{18,2},{3,19},{19,3},{4,20},{20... | collective-permute-start | bytes 2359304 | tf_op jit(solution)/shard_map/ppermute | solution.py:448
  11.4 3.5 %spectra.2 = (f32[16,8,512]{2,1,0:T(8,128)S(1)}, f32[16,8,512]{2,1,0:T(8,128)S(1)}) custom-call(s32[16]{0:T(128)S(1)} %copy-done.1, s32[8]{0:T(128)S(1)} %copy-done.2, f32[1152,4,512]{2,1,0:T(4,128)} %refs_2_.3, f32[4,512]{1,0:T(4,128)S(1)} %copy-done), custom_call_target="tpu_custom_call" | custom-call | tf_op jit(solution)/shard_map/spectra/pallas_call | solution.py:235
  15.0 0.1 collective-permute-start.6
  15.1 2.6 %gram.1 = (f32[8,128]{1,0:T(8,128)S(1)}, f32[8,128]{1,0:T(8,128)S(1)}) custom-call(f32[16,8,512]{2,1,0:T(8,128)S(1)} %get-tuple-element.10.refs_0_, f32[16,8,512]{2,1,0:T(8,128)S(1)} %get-tuple-element.11.refs_1_, f32[16,8,1536]{2,1,0:T(8,128)S(1)} %get-tuple-element.12.refs_2_, f32[16,8,1536]{2,1,0:T(8,128)S(1)} %get-tuple-element.13.refs_3_.refs_1_), custom_call_target="tpu_custom_call" | custom-call | tf_op jit(solution)/shard_map/gram/pallas_call | solution.py:327
  17.6 2.0 %collective-permute-start = (f32[8,128]{1,0:T(8,128)S(1)}, f32[8,128]{1,0:T(8,128)S(1)}, u32[]{:S(2)}, u32[]{:S(2)}) collective-permute-start(f32[8,128]{1,0:T(8,128)S(1)} %get-tuple-element.15), channel_id=1, source_target_pairs={{0,16},{16,0},{1,17},{17,1},{2,18},{18,2},{3,19},{19,3},{4,20},{20... | collective-permute-start | bytes 12296 | tf_op jit(solution)/shard_map/ppermute | solution.py:448
  19.7 15.0 %collective-permute-done = f32[8,128]{1,0:T(8,128)S(1)} collective-permute-done((f32[8,128]{1,0:T(8,128)S(1)}, f32[8,128]{1,0:T(8,128)S(1)}, u32[]{:S(2)}, u32[]{:S(2)}) %collective-permute-start) | collective-permute-done | bytes 4128 | tf_op jit(solution)/shard_map/ppermute | solution.py:448
  34.7 0.0 collective-permute-start.1
  34.7 1.2 %collective-permute-done.1 = f32[8,128]{1,0:T(8,128)S(1)} collective-permute-done((f32[8,128]{1,0:T(8,128)S(1)}, f32[8,128]{1,0:T(8,128)S(1)}, u32[]{:S(2)}, u32[]{:S(2)}) %collective-permute-start.1) | collective-permute-done | bytes 4128 | tf_op jit(solution)/shard_map/ppermute | solution.py:30
  35.9 1.7 %collective-permute-start.2 = (f32[8,128]{1,0:T(8,128)S(1)}, f32[8,128]{1,0:T(8,128)S(1)}, u32[]{:S(2)}, u32[]{:S(2)}) collective-permute-start(f32[8,128]{1,0:T(8,128)S(1)} %add.16), channel_id=1, source_target_pairs={{0,2},{2,0},{1,3},{3,1},{4,6},{6,4},{5,7},{7,5},{8,10},{10,8},{9,1... | collective-permute-start | bytes 12296 | tf_op jit(solution)/shard_map/ppermute | solution.py:30
  37.6 1.9 %collective-permute-done.2 = f32[8,128]{1,0:T(8,128)S(1)} collective-permute-done((f32[8,128]{1,0:T(8,128)S(1)}, f32[8,128]{1,0:T(8,128)S(1)}, u32[]{:S(2)}, u32[]{:S(2)}) %collective-permute-start.2) | collective-permute-done | bytes 4128 | tf_op jit(solution)/shard_map/ppermute | solution.py:30
  39.5 1.8 %collective-permute-start.3 = (f32[8,128]{1,0:T(8,128)S(1)}, f32[8,128]{1,0:T(8,128)S(1)}, u32[]{:S(2)}, u32[]{:S(2)}) collective-permute-start(f32[8,128]{1,0:T(8,128)S(1)} %add.17), channel_id=1, source_target_pairs={{0,4},{4,0},{1,5},{5,1},{2,6},{6,2},{3,7},{7,3},{8,12},{12,8},{9,1... | collective-permute-start | bytes 12296 | tf_op jit(solution)/shard_map/ppermute | solution.py:30
  41.3 1.8 %collective-permute-done.3 = f32[8,128]{1,0:T(8,128)S(1)} collective-permute-done((f32[8,128]{1,0:T(8,128)S(1)}, f32[8,128]{1,0:T(8,128)S(1)}, u32[]{:S(2)}, u32[]{:S(2)}) %collective-permute-start.3) | collective-permute-done | bytes 4128 | tf_op jit(solution)/shard_map/ppermute | solution.py:30
  43.1 2.8 %collective-permute-start.4 = (f32[8,128]{1,0:T(8,128)S(1)}, f32[8,128]{1,0:T(8,128)S(1)}, u32[]{:S(2)}, u32[]{:S(2)}) collective-permute-start(f32[8,128]{1,0:T(8,128)S(1)} %add.18), channel_id=1, source_target_pairs={{0,8},{8,0},{1,9},{9,1},{2,10},{10,2},{3,11},{11,3},{4,12},{12,4},... | collective-permute-start | bytes 12296 | tf_op jit(solution)/shard_map/ppermute | solution.py:30
  45.9 1.7 %collective-permute-done.4 = f32[8,128]{1,0:T(8,128)S(1)} collective-permute-done((f32[8,128]{1,0:T(8,128)S(1)}, f32[8,128]{1,0:T(8,128)S(1)}, u32[]{:S(2)}, u32[]{:S(2)}) %collective-permute-start.4) | collective-permute-done | bytes 4128 | tf_op jit(solution)/shard_map/ppermute | solution.py:30
  47.6 0.9 %factor.1 = (f32[64,8,128]{2,1,0:T(8,128)S(1)}, f32[128,128]{1,0:T(8,128)}) custom-call(f32[8,128]{1,0:T(8,128)S(1)} %add.19.refs_0_), custom_call_target="tpu_custom_call" | custom-call | tf_op jit(solution)/shard_map/factor/pallas_call | solution.py:387
  48.5 0.0 collective-permute-done.6.refs_2_
  48.5 1.4 %project.2.refs_3_ = f32[8,16,4,8,128]{4,3,2,1,0:T(8,128)} custom-call(f32[64,8,128]{2,1,0:T(8,128)S(1)} %get-tuple-element.17.refs_0_, f32[16,8,512]{2,1,0:T(8,128)S(1)} %get-tuple-element.11.refs_1_, f32[16,8,512]{2,1,0:T(8,128)S(1)} %collective-permute-done.6.refs_2_), custom_call_target="tpu_custom_call" | custom-call | tf_op jit(solution)/shard_map/project/pallas_call | solution.py:434
  49.8 0.0 collective-permute-done.5.refs_2_
  49.8 2.8 %project.3 = f32[8,16,4,8,128]{4,3,2,1,0:T(8,128)} custom-call(f32[64,8,128]{2,1,0:T(8,128)S(1)} %get-tuple-element.17.refs_0_, f32[16,8,1536]{2,1,0:T(8,128)S(1)} %get-tuple-element.13.refs_3_.refs_1_, f32[16,8,1536]{2,1,0:T(8,128)S(1)} %collective-permute-done.5.refs_2_, f32[8,16,4,8,128]{4,3,2,1,0:T(8,128)} %project.2.refs_3_), custom_call_target="tpu_custom_call", output_to_operand_aliasing={{}: (3, {})} | custom-call | tf_op jit(solution)/shard_map/project/pallas_call | solution.py:434
  (5 shorter events, 0.0 us)
Async XLA Ops:
  0.6 0.7 %copy-start = (f32[4,512]{1,0:T(4,128)S(1)}, f32[4,512]{1,0:T(4,128)}, u32[]{:S(2)}) copy-start(f32[4,512]{1,0:T(4,128)} %refs_3_.3) | copy-start | bytes 24580
  1.3 0.7 %copy-start.1 = (s32[16]{0:T(128)S(1)}, s32[16]{0:T(128)}, u32[]{:S(2)}) copy-start(s32[16]{0:T(128)} %refs_0_.3) | copy-start | bytes 196
  2.0 0.7 %copy-start.2 = (s32[8]{0:T(128)S(1)}, s32[8]{0:T(128)}, u32[]{:S(2)}) copy-start(s32[8]{0:T(128)} %refs_1_.3) | copy-start | bytes 100
  8.4 41.4 %collective-permute-start.5 = (f32[16,8,1536]{2,1,0:T(8,128)S(1)}, f32[16,8,1536]{2,1,0:T(8,128)S(1)}, u32[]{:S(2)}, u32[]{:S(2)}) collective-permute-start(f32[16,8,1536]{2,1,0:T(8,128)S(1)} %get-tuple-element.12.refs_2_), channel_id=1, source_target_pairs={{0,16},{16,0},{1,17},{17,1},{2,18},{18,2},{3,19},{19,3},{4,20},{20... | collective-permute-start | bytes 2359304 | tf_op jit(solution)/shard_map/ppermute | solution.py:448
  15.0 33.5 %collective-permute-start.6 = (f32[16,8,512]{2,1,0:T(8,128)S(1)}, f32[16,8,512]{2,1,0:T(8,128)S(1)}, u32[]{:S(2)}, u32[]{:S(2)}) collective-permute-start(f32[16,8,512]{2,1,0:T(8,128)S(1)} %get-tuple-element.10.refs_0_), channel_id=1, source_target_pairs={{0,16},{16,0},{1,17},{17,1},{2,18},{18,2},{3,19},{19,3},{4,20},{20... | collective-permute-start | bytes 786440 | tf_op jit(solution)/shard_map/ppermute | solution.py:448
  17.6 17.0 %collective-permute-start = (f32[8,128]{1,0:T(8,128)S(1)}, f32[8,128]{1,0:T(8,128)S(1)}, u32[]{:S(2)}, u32[]{:S(2)}) collective-permute-start(f32[8,128]{1,0:T(8,128)S(1)} %get-tuple-element.15), channel_id=1, source_target_pairs={{0,16},{16,0},{1,17},{17,1},{2,18},{18,2},{3,19},{19,3},{4,20},{20... | collective-permute-start | bytes 12296 | tf_op jit(solution)/shard_map/ppermute | solution.py:448
  34.7 1.2 %collective-permute-start.1 = (f32[8,128]{1,0:T(8,128)S(1)}, f32[8,128]{1,0:T(8,128)S(1)}, u32[]{:S(2)}, u32[]{:S(2)}) collective-permute-start(f32[8,128]{1,0:T(8,128)S(1)} %add.15), channel_id=1, source_target_pairs={{0,1},{1,0},{2,3},{3,2},{4,5},{5,4},{6,7},{7,6},{8,9},{9,8},{10,11... | collective-permute-start | bytes 12296 | tf_op jit(solution)/shard_map/ppermute | solution.py:30
  35.9 3.6 %collective-permute-start.2 = (f32[8,128]{1,0:T(8,128)S(1)}, f32[8,128]{1,0:T(8,128)S(1)}, u32[]{:S(2)}, u32[]{:S(2)}) collective-permute-start(f32[8,128]{1,0:T(8,128)S(1)} %add.16), channel_id=1, source_target_pairs={{0,2},{2,0},{1,3},{3,1},{4,6},{6,4},{5,7},{7,5},{8,10},{10,8},{9,1... | collective-permute-start | bytes 12296 | tf_op jit(solution)/shard_map/ppermute | solution.py:30
  39.5 3.6 %collective-permute-start.3 = (f32[8,128]{1,0:T(8,128)S(1)}, f32[8,128]{1,0:T(8,128)S(1)}, u32[]{:S(2)}, u32[]{:S(2)}) collective-permute-start(f32[8,128]{1,0:T(8,128)S(1)} %add.17), channel_id=1, source_target_pairs={{0,4},{4,0},{1,5},{5,1},{2,6},{6,2},{3,7},{7,3},{8,12},{12,8},{9,1... | collective-permute-start | bytes 12296 | tf_op jit(solution)/shard_map/ppermute | solution.py:30
  43.1 4.5 %collective-permute-start.4 = (f32[8,128]{1,0:T(8,128)S(1)}, f32[8,128]{1,0:T(8,128)S(1)}, u32[]{:S(2)}, u32[]{:S(2)}) collective-permute-start(f32[8,128]{1,0:T(8,128)S(1)} %add.18), channel_id=1, source_target_pairs={{0,8},{8,0},{1,9},{9,1},{2,10},{10,2},{3,11},{11,3},{4,12},{12,4},... | collective-permute-start | bytes 12296 | tf_op jit(solution)/shard_map/ppermute | solution.py:30

commit v2 on v1

--- a/solution.py
+++ b/solution.py
@@ -15,6 +15,7 @@
 GAP_HIGH = 192
 LANES = 128
 ROWS = 8
+JOIN_FLOPS = 10**10
 VMEM_BYTES = 48 * 1024 * 1024
 PAIRS = [(a, b) for a in range(NBLK) for b in range(a, NBLK)]
 ENTRIES = [(0, a, b) for a, b in PAIRS] + [(1, a, b) for a, b in PAIRS if a < b]
@@ -168,92 +169,142 @@
             rows = pl.ds((2 * j + p) * NFREQ, NFREQ)
             high_ref[rows, place] = high
             low_ref[rows, place] = low
-
-
-def coeff_chunk(flow_ref, weight, high_ref, low_ref, fhigh_ref, flow_low_ref, acc_ref, slabs):
+    return [jnp.sum(part, axis=1, keepdims=True) for part in parts]
+
+
+def coeff_chunk(flow_ref, arrived, high_ref, low_ref, fh_ref, fl_ref, acc_ref, slabs):
     total = flow_ref.shape[0] // slabs
-    for l in range(slabs):
-        values = flow_ref[pl.ds(l, total, stride=slabs), :]
-        fluct = values - jnp.sum(values, axis=0, keepdims=True) * (1.0 / total)
-        high = fluct.astype(jnp.bfloat16)
-        fhigh_ref[:, l * LANES : (l + 1) * LANES] = high
-        flow_low_ref[:, l * LANES : (l + 1) * LANES] = (fluct - high.astype(jnp.float32)).astype(
-            jnp.bfloat16
-        )
     per_block = 2 * NFREQ
     spans = reach(total)
     started = [False] * NBLK
-    for t0 in range(0, total, BLOCK):
+    shift, left = [None] * slabs, [0.0] * slabs
+    for i, t0 in enumerate(range(0, total, BLOCK)):
+        t1 = min(t0 + BLOCK, total)
+        arrived(i)
+        for l in range(slabs):
+            values = flow_ref[pl.ds(t0 * slabs + l, t1 - t0, stride=slabs), :]
+            if i == 0:
+                shift[l] = jnp.sum(values, axis=0, keepdims=True) * (1.0 / (t1 - t0))
+            values = values - shift[l]
+            left[l] += jnp.sum(values.reshape(-1, ROWS, LANES), axis=0)
+            high = values.astype(jnp.bfloat16)
+            cols = slice(l * LANES, (l + 1) * LANES)
+            fh_ref[t0:t1, cols] = high
+            fl_ref[t0:t1, cols] = (values - high.astype(jnp.float32)).astype(jnp.bfloat16)
+    for i, t0 in enumerate(range(0, total, BLOCK)):
         t1 = min(t0 + BLOCK, total)
         hit = [j for j in range(NBLK) if spans[j][0] < t1 and spans[j][1] > t0]
         j0, j1 = min(hit), max(hit) + 1
         rows = slice(j0 * per_block, j1 * per_block)
-        xh, xl = fhigh_ref[t0:t1, :], flow_low_ref[t0:t1, :]
+        xh, xl = fh_ref[t0:t1, :], fl_ref[t0:t1, :]
         th, tl = high_ref[rows, t0:t1], low_ref[rows, t0:t1]
-        part = jnp.dot(th, xl, preferred_element_type=jnp.float32)
-        part += jnp.dot(tl, xh, preferred_element_type=jnp.float32)
-        part += jnp.dot(th, xh, preferred_element_type=jnp.float32)
+        part = jnp.dot(
+            jnp.concatenate([th, tl, th], axis=1),
+            jnp.concatenate([xh, xh, xl], axis=0),
+            preferred_element_type=jnp.float32,
+        )
         for j in range(j0, j1):
             own = slice(j * per_block, (j + 1) * per_block)
             piece = part[(j - j0) * per_block : (j - j0 + 1) * per_block]
             acc_ref[own, :] = acc_ref[own, :] + piece if started[j] else piece
             started[j] = True
-    root = jnp.concatenate([jnp.sqrt(weight[l : l + 1, :]) for l in range(slabs)], axis=1)
-    return root
-
-
-def store_chunk(acc_ref, root, send_ref, own_ref, at):
-    cols = root.shape[1]
-    for jp in range(2 * NBLK):
-        piece = acc_ref[jp * 2 * ROWS : (jp + 1) * 2 * ROWS, :] * root
-        send_ref[jp, :, at : at + cols] = piece[:ROWS]
-        own_ref[jp, :, at : at + cols] = piece[ROWS:]
-
-
-def spectra_kernel(slabs, first, count, freq_ref, start_ref, snap_ref, weight_ref, *rest):
-    send_ref, own_ref, held, high_ref, low_ref, fh_ref, fl_ref, acc_ref, sems = rest
+    left = [jnp.sum(rest, axis=0, keepdims=True) * (1.0 / total) for rest in left]
+    return jnp.concatenate(left, axis=1)
+
+
+def store_chunk(acc_ref, left, sums, root, send_ref, own_ref):
+    for p in range(2):
+        mean_part = sums[p] * left
+        for j in range(NBLK):
+            jp = 2 * j + p
+            piece = (acc_ref[jp * NFREQ : (jp + 1) * NFREQ, :] - mean_part) * root
+            send_ref[jp] = piece[:ROWS]
+            own_ref[jp] = piece[ROWS:]
+
+
+def spectra_kernel(slabs, first, pieces, earlier, *refs):
+    freq_hbm, start_hbm, snap_ref, weight_hbm, *rest = refs
+    count = sum(pieces)
+    outs = len(pieces)
+    sends, owns, rest = rest[:outs], rest[outs : 2 * outs], rest[2 * outs :]
+    if earlier:
+        gram_ref, *rest = rest
+    freq_ref, start_ref, weight_ref, held = rest[:4]
+    high_ref, low_ref, fh_ref, fl_ref, acc_ref, sems, small_sems = rest[4:]
+    small = [
+        pltpu.make_async_copy(source, target, small_sems.at[i])
+        for i, (source, target) in enumerate(
+            ((freq_hbm, freq_ref), (start_hbm, start_ref), (weight_hbm, weight_ref))
+        )
+    ]
+    for copy in small:
+        copy.start()
+    total = snap_ref.shape[0]
     copies = []
     for i in range(count):
-        source = snap_ref.at[:, :, pl.ds((first + i) * LANES, LANES)]
-        copies.append(pltpu.make_async_copy(source, held.at[i], sems.at[i]))
-        copies[-1].start()
-    fill_table(freq_ref, start_ref, high_ref, low_ref)
-    total = snap_ref.shape[0]
+        copies.append([])
+        step = total
+        for k, t0 in enumerate(range(0, total, step)):
+            times = pl.ds(t0, min(step, total - t0))
+            source = snap_ref.at[times, :, pl.ds((first + i) * LANES, LANES)]
+            copies[i].append(pltpu.make_async_copy(source, held.at[i, times], sems.at[i, k]))
+            copies[i][k].start()
+    for copy in small:
+        copy.wait()
+    sums = fill_table(freq_ref, start_ref, high_ref, low_ref)
+    places = [(piece, at) for piece, size in enumerate(pieces) for at in range(size)]
     for i in range(count):
-        copies[i].wait()
         flat = held.at[i].reshape(total * slabs, LANES)
         weight = weight_ref[:, (first + i) * LANES : (first + i + 1) * LANES]
-        root = coeff_chunk(flat, weight, high_ref, low_ref, fh_ref, fl_ref, acc_ref, slabs)
-        store_chunk(acc_ref, root, send_ref, own_ref, i * slabs * LANES)
-
-
-def spectra_call(snapshots, weights, freq_bins, block_starts, first, count):
+        root = jnp.concatenate([jnp.sqrt(weight[l : l + 1, :]) for l in range(slabs)], axis=1)
+        left = coeff_chunk(
+            flat, lambda k: copies[i][k].wait() if k < len(copies[i]) else None, high_ref, low_ref, fh_ref, fl_ref, acc_ref, slabs
+        )
+        piece, at = places[i]
+        cols = slice(at * slabs * LANES, (at + 1) * slabs * LANES)
+        store_chunk(acc_ref, left, sums, root, sends[piece].at[:, :, cols], owns[piece].at[:, :, cols])
+    if earlier:
+        gram_ref[...] = gram_sums([*earlier, *sends])
+
+
+def spectra_call(snapshots, weights, freq_bins, block_starts, first, pieces, earlier=()):
     total, slabs, _ = snapshots.shape
     cols = slabs * LANES
-    shape = jax.ShapeDtypeStruct((2 * NBLK, ROWS, count * cols), jnp.float32)
+    count, outs, more = sum(pieces), len(pieces), len(earlier)
+    shapes = [jax.ShapeDtypeStruct((2 * NBLK, ROWS, n * cols), jnp.float32) for n in pieces] * 2
+    if more:
+        shapes.append(jax.ShapeDtypeStruct((ROWS, LANES), jnp.float32))
     wide = -(-total // LANES) * LANES + LANES
-    return pl.pallas_call(
-        lambda *refs: spectra_kernel(slabs, first, count, *refs),
-        out_shape=(shape, shape),
-        in_specs=[
-            pl.BlockSpec(memory_space=pltpu.SMEM),
-            pl.BlockSpec(memory_space=pltpu.SMEM),
-            pl.BlockSpec(memory_space=pl.ANY),
-            pl.BlockSpec(memory_space=pltpu.VMEM),
-        ],
-        out_specs=(pl.BlockSpec(memory_space=pltpu.VMEM),) * 2,
+    given = pl.pallas_call(
+        lambda *refs: spectra_kernel(
+            slabs, first, pieces, refs[4 : 4 + more], *refs[:4], *refs[4 + more :]
+        ),
+        out_shape=tuple(shapes),
+        in_specs=[pl.BlockSpec(memory_space=pltpu.HBM)] * 4
+        + [pl.BlockSpec(memory_space=pltpu.VMEM)] * more,
+        out_specs=(pl.BlockSpec(memory_space=pltpu.VMEM),) * len(shapes),
         scratch_shapes=[
+            pltpu.SMEM(freq_bins.shape, jnp.int32),
+            pltpu.SMEM(block_starts.shape, jnp.int32),
+            pltpu.VMEM(weights.shape, jnp.float32),
             pltpu.VMEM((count, total, slabs, LANES), jnp.float32),
             pltpu.VMEM((2 * NBLK * NFREQ, wide), jnp.bfloat16),
             pltpu.VMEM((2 * NBLK * NFREQ, wide), jnp.bfloat16),
             pltpu.VMEM((total, cols), jnp.bfloat16),
             pltpu.VMEM((total, cols), jnp.bfloat16),
             pltpu.VMEM((2 * NBLK * NFREQ, cols), jnp.float32),
-            pltpu.SemaphoreType.DMA((count,)),
+            pltpu.SemaphoreType.DMA((count, -(-total // BLOCK))),
+            pltpu.SemaphoreType.DMA((3,)),
         ],
         compiler_params=pltpu.CompilerParams(vmem_limit_bytes=VMEM_BYTES),
+        cost_estimate=pl.CostEstimate(
+            flops=6 * 2 * NBLK * NFREQ * total * count * cols,
+            bytes_accessed=4 * (total + 2 * NBLK * NFREQ) * count * cols,
+            transcendentals=0,
+        ),
         name="spectra",
-    )(freq_bins, block_starts, snapshots, weights)
+    )(freq_bins, block_starts, snapshots, weights, *earlier)
+    return given[:outs], given[outs : 2 * outs], given[2 * outs :]
 
 
 def lane_places(count):
@@ -293,45 +344,66 @@
     return total
 
 
-def gram_kernel(*refs):
-    blocks, outs = refs[:-2], refs[-2:]
-    pairs = len(blocks) // 2
-    for side in range(2):
-        sums = {}
-        for a in range(NBLK):
-            row = [(0, a, b) for b in range(a, NBLK)] + [(1, a, b) for b in range(a + 1, NBLK)]
-            carry = tuple(jnp.zeros((ROWS, LANES), jnp.float32) for _ in row)
-            for i in range(pairs):
-                ref = blocks[2 * i + side]
-
-                def body(k, carry, ref=ref, a=a, row=row):
-                    cols = pl.ds(pl.multiple_of(k * LANES, LANES), LANES)
-                    re = {b: ref[2 * b, :, cols] for b in range(a, NBLK)}
-                    im = {b: ref[2 * b + 1, :, cols] for b in range(a, NBLK)}
-                    out = []
-                    for (kind, _, b), total in zip(row, carry):
-                        if kind == 0:
-                            out.append(total + (re[a] * re[b] + im[a] * im[b]))
-                        else:
-                            out.append(total + (re[a] * im[b] - im[a] * re[b]))
-                    return tuple(out)
-
-                carry = lax.fori_loop(0, ref.shape[2] // LANES, body, carry, unroll=4)
-            for key, total in zip(row, carry):
-                sums[key] = total
-        outs[side][...] = fold_lanes([sums[key] for key in ENTRIES])
-
-
-def gram_call(*blocks):
-    shape = jax.ShapeDtypeStruct((ROWS, LANES), jnp.float32)
+def gram_sums(blocks):
+    sums = {}
+    for a in range(NBLK):
+        row = [(0, a, b) for b in range(a, NBLK)] + [(1, a, b) for b in range(a + 1, NBLK)]
+        carry = tuple(jnp.zeros((ROWS, LANES), jnp.float32) for _ in row)
+        for ref in blocks:
+
+            def body(k, carry, ref=ref, a=a, row=row):
+                cols = pl.ds(pl.multiple_of(k * LANES, LANES), LANES)
+                re = {b: ref[2 * b, :, cols] for b in range(a, NBLK)}
+                im = {b: ref[2 * b + 1, :, cols] for b in range(a, NBLK)}
+                out = []
+                for (kind, _, b), total in zip(row, carry):
+                    if kind == 0:
+                        out.append(total + (re[a] * re[b] + im[a] * im[b]))
+                    else:
+                        out.append(total + (re[a] * im[b] - im[a] * re[b]))
+                return tuple(out)
+
+            carry = lax.fori_loop(0, ref.shape[2] // LANES, body, carry, unroll=4)
+        for key, total in zip(row, carry):
+            sums[key] = total
+    return fold_lanes([sums[key] for key in ENTRIES])
+
+
+def gram_kernel(count, *refs):
+    refs[-1][...] = gram_sums(refs[:count])
+
+
+def gram_call(blocks, after):
     return pl.pallas_call(
-        gram_kernel,
-        out_shape=(shape, shape),
-        in_specs=[pl.BlockSpec(memory_space=pltpu.VMEM)] * len(blocks),
-        out_specs=(pl.BlockSpec(memory_space=pltpu.VMEM),) * 2,
+        lambda *refs: gram_kernel(len(blocks), *refs),
+        out_shape=jax.ShapeDtypeStruct((ROWS, LANES), jnp.float32),
+        in_specs=[pl.BlockSpec(memory_space=pltpu.VMEM)] * len(blocks)
+        + [pl.BlockSpec(memory_space=pl.ANY)],
+        out_specs=pl.BlockSpec(memory_space=pltpu.VMEM),
         compiler_params=pltpu.CompilerParams(vmem_limit_bytes=VMEM_BYTES),
+        cost_estimate=pl.CostEstimate(
+            flops=sum(block.size for block in blocks) * 4 * NBLK,
+            bytes_accessed=4 * sum(block.size for block in blocks),
+            transcendentals=0,
+        ),
         name="gram",
-    )(*blocks)
+    )(*blocks, after)
+
+
+def join_kernel(own_ref, far_ref, out_ref):
+    out_ref[...] = own_ref[...] + far_ref[...]
+
+
+def join_call(own, far):
+    return pl.pallas_call(
+        join_kernel,
+        out_shape=jax.ShapeDtypeStruct(own.shape, own.dtype),
+        in_specs=[pl.BlockSpec(memory_space=pltpu.VMEM)] * 2,
+        out_specs=pl.BlockSpec(memory_space=pltpu.VMEM),
+        compiler_params=pltpu.CompilerParams(vmem_limit_bytes=VMEM_BYTES),
+        cost_estimate=pl.CostEstimate(flops=JOIN_FLOPS, bytes_accessed=0, transcendentals=0),
+        name="join",
+    )(own, far)
 
 
 def factor_kernel(count, sum_ref, inv_ref, fac_ref):
@@ -397,49 +469,70 @@
     )(total)
 
 
-def project_kernel(slabs, inv_ref, own_ref, far_ref, *rest):
-    out_ref = rest[-1]
+def project_chunk(slabs, inv_ref, own_ref, far_ref, first, flat):
     band = lax.axis_index("band")
     per = 2 * NBLK * 2 * slabs
-    flat = out_ref.reshape(ROWS * per, LANES)
     for side, ref in enumerate((own_ref, far_ref)):
         base = (band if side == 0 else 1 - band) * slabs
-
-        def body(l, _, ref=ref, base=base):
-            cols = pl.ds(pl.multiple_of(l * LANES, LANES), LANES)
-            re = [ref[2 * a, :, cols] for a in range(NBLK)]
-            im = [ref[2 * a + 1, :, cols] for a in range(NBLK)]
+        for l0 in range(0, slabs, 2):
+            both = range(l0, l0 + 2)
+            cols = [pl.ds(pl.multiple_of(first + l * LANES, LANES), LANES) for l in both]
+            re = [[ref[2 * a, :, at] for a in range(NBLK)] for at in cols]
+            im = [[ref[2 * a + 1, :, at] for a in range(NBLK)] for at in cols]
             for b in range(NBLK):
                 diagonal = inv_ref[ENTRIES.index((0, b, b))]
-                real, imag = re[b] * diagonal, im[b] * diagonal
+                real = [re[i][b] * diagonal for i in range(2)]
+                imag = [im[i][b] * diagonal for i in range(2)]
                 for a in range(b):
                     cr = inv_ref[ENTRIES.index((0, a, b))]
                     ci = inv_ref[ENTRIES.index((1, a, b))]
-                    real = real + (re[a] * cr - im[a] * ci)
-                    imag = imag + (re[a] * ci + im[a] * cr)
-                for p, value in enumerate((real, imag)):
-                    line = (p * NBLK + b) * 2 * slabs + base + l
-                    flat[pl.ds(line, ROWS, stride=per), :] = value
-            return 0
-
-        lax.fori_loop(0, slabs, body, 0, unroll=2)
+                    for i in range(2):
+                        real[i] = real[i] + (re[i][a] * cr - im[i][a] * ci)
+                        imag[i] = imag[i] + (re[i][a] * ci + im[i][a] * cr)
+                for i in range(2):
+                    for p, value in enumerate((real[i], imag[i])):
+                        line = (p * NBLK + b) * 2 * slabs + base + l0 + i
+                        flat[pl.ds(line, ROWS, stride=per), :] = value
+
+
+def project_kernel(slabs, at, inv_ref, own_ref, far_ref, *rest):
+    out_ref, held, sems = rest[-3:]
+    count = held.shape[0]
+    per = 2 * NBLK * 2 * slabs
+
+    def copy_of(i):
+        return pltpu.make_async_copy(held.at[i], out_ref.at[:, :, at + i], sems.at[i])
+
+    def body(i, _):
+        flat = held.at[i].reshape(ROWS * per, LANES)
+        project_chunk(slabs, inv_ref, own_ref, far_ref, i * slabs * LANES, flat)
+        copy_of(i).start()
+        return 0
+
+    lax.fori_loop(0, count, body, 0)
+    for i in range(count):
+        copy_of(i).wait()
 
 
 def project_call(inv, own, far, modes, at, slabs, chunks):
     count = own.shape[2] // (slabs * LANES)
-    block = (ROWS, 2 * NBLK, None, 2 * slabs, LANES)
     given = [] if modes is None else [modes]
-    cols = slabs * LANES
-    spec = pl.BlockSpec((2 * NBLK, ROWS, cols), lambda i: (0, 0, i))
+    block = (ROWS, 2 * NBLK, 2 * slabs, LANES)
     return pl.pallas_call(
-        lambda *refs: project_kernel(slabs, *refs),
-        grid=(count,),
+        lambda *refs: project_kernel(slabs, at, *refs),
         out_shape=jax.ShapeDtypeStruct((ROWS, 2 * NBLK, chunks, 2 * slabs, LANES), jnp.float32),
-        in_specs=[pl.BlockSpec(inv.shape, lambda i: (0, 0, 0)), spec, spec]
-        + [pl.BlockSpec(memory_space=pl.ANY)] * len(given),
-        out_specs=pl.BlockSpec(block, lambda i: (0, 0, at + i, 0, 0)),
+        in_specs=[pl.BlockSpec(memory_space=pltpu.VMEM)] * 3
+        + [pl.BlockSpec(memory_space=pltpu.HBM)] * len(given),
+        out_specs=pl.BlockSpec(memory_space=pltpu.HBM),
         input_output_aliases={3: 0} if given else {},
+        scratch_shapes=[
+            pltpu.VMEM((count, *block), jnp.float32),
+            pltpu.SemaphoreType.DMA((count,)),
+        ],
         compiler_params=pltpu.CompilerParams(vmem_limit_bytes=VMEM_BYTES),
+        cost_estimate=pl.CostEstimate(
+            flops=8 * own.size * NBLK, bytes_accessed=16 * own.size, transcendentals=0
+        ),
         name="project",
     )(inv, own, far, *given)
 
@@ -452,18 +545,25 @@
     slabs, cells = snapshots.shape[1:]
     chunks = cells // LANES
     count = 2 * slabs * cells * lax.axis_size("space")
-    given = (snapshots, quad_weights, freq_bins, block_starts)
-    send_a, own_a = spectra_call(*given, 0, 1)
-    far_a = swap_bands(send_a)
-    send_b, own_b = spectra_call(*given, 1, chunks - 1)
-    gram_send, gram_own = gram_call(send_a, own_a, send_b, own_b)
-    total = gram_own + swap_bands(gram_send)
-    far_b = swap_bands(send_b)
+    given = [
+        pltpu.with_memory_space_constraint(array, pltpu.HBM)
+        for array in (snapshots, quad_weights, freq_bins, block_starts)
+    ]
+    pieces = (chunks - 2, 1) if chunks > 2 else (1,)
+    sends, owns, _ = spectra_call(*given, 0, (1,))
+    fars = [swap_bands(sends[0])]
+    later, owns_later, (gram_send,) = spectra_call(*given, 1, pieces, sends)
+    far_gram = swap_bands(gram_send)
+    fars += [swap_bands(send) for send in later]
+    owns = [*owns, *owns_later]
+    total = join_call(gram_call(owns, fars[0]), far_gram)
     for level in range(lax.axis_size("space").bit_length() - 1):
         total = total + from_partner(total, "space", level)
     inv, fac = factor_call(total, count)
-    modes = project_call(inv, own_a, far_a, None, 0, slabs, chunks)
-    modes = project_call(inv, own_b, far_b, modes, 1, slabs, chunks)
+    modes, at = None, 0
+    for size, own, far in zip((1, *pieces), owns, fars):
+        modes = project_call(inv, own, far, modes, at, slabs, chunks)
+        at += size
     modes = modes.reshape(ROWS, 2, NBLK, chunks, 2 * slabs, LANES)
     modes = modes.transpose(0, 1, 2, 4, 3, 5).reshape(ROWS, 2, NBLK, 2 * slabs, cells)
     factor = fac[:, :NBLK].reshape(ROWS, 2, NBLK, NBLK)

time: 52.9 us -> 36.5 us (0.69)
  waiting for transfers between devices: 21.6 us -> 7.54 us
  local copies, waits for them, and re-layouts: 2 us -> 0 us
    ppermute x3 -> x4, waiting for transfers between devices: 15 us -> 0.65 us  [swap_bands(): return lax.ppermute(block, 'band', [(0, 1), (1, 0)])]
    unnamed x6 -> x0, local copies, waits for them, and re-layouts: 2 us -> none
    pallas_call x5 -> x7, Pallas kernels: 16.1 us -> 16 us  [the longest x2 10.1 us: spectra_call(): pl.pallas_call(lambda *refs: spectra_kernel(slabs, first, pieces, refs[4:...]
    ppermute x3 -> x4, starting transfers between devices: 5.13 us -> 5.2 us  [swap_bands(): return lax.ppermute(block, 'band', [(0, 1), (1, 0)])]
  transfers between devices with their start and end apart: 7 -> 8, of which waited for: 5 -> 6; matrix products, arithmetic and copies ran while one was open for 0% -> 0% of each run, Pallas kernels for 16% -> 35%
where the time goes in v2:
time: 36.5 us; the launch traced here: 36.3 us
  Pallas kernels  16.9 us (46%)
  starting transfers between devices  11.2 us (31%)
  waiting for transfers between devices  7.54 us (21%)
  between operations  0.68 us (2%)
    pallas_call x2, Pallas kernels, spectra_call(): pl.pallas_call(lambda *refs: spectra_kernel(slabs, first, pieces, refs[4:...  10.1 us
    ppermute x4, waiting for transfers between devices, from_partner(): return lax.ppermute(block, axis, route)  6.9 us
    ppermute x4, starting transfers between devices, from_partner(): return lax.ppermute(block, axis, route)  5.99 us
    ppermute x4, starting transfers between devices, swap_bands(): return lax.ppermute(block, 'band', [(0, 1), (1, 0)])  5.2 us
    pallas_call x3, Pallas kernels, project_call(): pl.pallas_call(lambda *refs: project_kernel(slabs, at, *refs), out_shape=...  4.67 us
    pallas_call x1, Pallas kernels, gram_call(): pl.pallas_call(lambda *refs: gram_kernel(len(blocks), *refs), out_shape=j...  1.23 us
    pallas_call x1, Pallas kernels, factor_call(): pl.pallas_call(lambda *refs: factor_kernel(count, *refs), out_shape=(jax....  0.89 us
  transfers between devices with their start and end apart: 8, of which 6 were waited for; matrix products, arithmetic and copies ran while one was open for 0% of the time, Pallas kernels for 35%

profile of v2, /device:TPU:0, one launch (start us, length us, event | category | flops | bytes accessed | tf_op | source)
XLA Modules:
  0.0 36.3 jit_solution(5376143010824011981)
XLA Ops:
  0.6 2.9 %spectra.2 = (f32[16,8,512]{2,1,0:T(8,128)S(1)}, f32[16,8,512]{2,1,0:T(8,128)S(1)}) custom-call(s32[16]{0:T(128)} %refs_0_.3, s32[8]{0:T(128)} %refs_1_.3, f32[1152,4,512]{2,1,0:T(4,128)} %refs_2_.3, f32[4,512]{1,0:T(4,128)} %refs_3_.3), custom_call_target="tpu_custom_call" | custom-call | flops 905969664 | bytes 2883584 | tf_op jit(solution)/shard_map/spectra/pallas_call | solution.py:278
  3.5 3.0 %collective-permute-start = (f32[16,8,512]{2,1,0:T(8,128)S(1)}, f32[16,8,512]{2,1,0:T(8,128)S(1)}, u32[]{:S(2)}, u32[]{:S(2)}) collective-permute-start(f32[16,8,512]{2,1,0:T(8,128)S(1)} %get-tuple-element.12.refs_4_), channel_id=1, source_target_pairs={{0,16},{16,0},{1,17},{17,1},{2,18},{18,2},{3,19},{19,3},{4,20},{20... | collective-permute-start | bytes 786440 | tf_op jit(solution)/shard_map/ppermute | solution.py:541
  6.5 7.2 %spectra.3 = (f32[16,8,1024]{2,1,0:T(8,128)S(1)}, f32[16,8,512]{2,1,0:T(8,128)S(1)}, f32[16,8,1024]{2,1,0:T(8,128)S(1)}, f32[16,8,512]{2,1,0:T(8,128)S(1)}, f32[8,128]{1,0:T(8,128)S(1)}) custom-call(s32[16]{0:T(128)} %refs_0_.3, s32[8]{0:T(128)} %refs_1_.3, f32[1152,4,512]{2,1,0:T(4,128)} %refs_2_.3, f32[4,512]{1,0:T(4,128)} %refs_3_.3, ...), custom_call_target="tpu_custom_call" | custom-call | flops 2717908992 | bytes 8650752 | tf_op jit(solution)/shard_map/spectra/pallas_call | solution.py:278
  13.7 0.1 collective-permute-start.1
  13.8 2.0 %collective-permute-start.6 = (f32[16,8,512]{2,1,0:T(8,128)S(1)}, f32[16,8,512]{2,1,0:T(8,128)S(1)}, u32[]{:S(2)}, u32[]{:S(2)}) collective-permute-start(f32[16,8,512]{2,1,0:T(8,128)S(1)} %get-tuple-element.18), channel_id=1, source_target_pairs={{0,16},{16,0},{1,17},{17,1},{2,18},{18,2},{3,19},{19,3},{4,20},{20... | collective-permute-start | bytes 786440 | tf_op jit(solution)/shard_map/ppermute | solution.py:541
  15.8 0.1 collective-permute-start.7
  15.9 0.0 collective-permute-done.refs_3_.refs_2_
  15.9 1.2 %gram.1.own_ref = f32[8,128]{1,0:T(8,128)S(1)} custom-call(f32[16,8,512]{2,1,0:T(8,128)S(1)} %get-tuple-element.11.refs_0_.refs_1_, f32[16,8,1024]{2,1,0:T(8,128)S(1)} %get-tuple-element.13.refs_1_, f32[16,8,512]{2,1,0:T(8,128)S(1)} %get-tuple-element.14.refs_2_.refs_1_, f32[16,8,512]{2,1,0:T(8,128)S(1)} %collective-permute-done.refs_3_.refs_2_), custom_call_target="tpu_custom_call" | custom-call | flops 8388608 | bytes 1048576 | tf_op jit(solution)/shard_map/gram/pallas_call | solution.py:377
  17.1 0.3 collective-permute-done.1.far_ref
  17.5 0.0 collective-permute-start.2
  17.5 1.2 %collective-permute-done.2 = f32[8,128]{1,0:T(8,128)S(1)} collective-permute-done((f32[8,128]{1,0:T(8,128)S(1)}, f32[8,128]{1,0:T(8,128)S(1)}, u32[]{:S(2)}, u32[]{:S(2)}) %collective-permute-start.2) | collective-permute-done | bytes 4128 | tf_op jit(solution)/shard_map/ppermute | solution.py:31
  18.7 1.6 %collective-permute-start.3 = (f32[8,128]{1,0:T(8,128)S(1)}, f32[8,128]{1,0:T(8,128)S(1)}, u32[]{:S(2)}, u32[]{:S(2)}) collective-permute-start(f32[8,128]{1,0:T(8,128)S(1)} %add.12), channel_id=1, source_target_pairs={{0,2},{2,0},{1,3},{3,1},{4,6},{6,4},{5,7},{7,5},{8,10},{10,8},{9,1... | collective-permute-start | bytes 12296 | tf_op jit(solution)/shard_map/ppermute | solution.py:31
  20.3 2.0 %collective-permute-done.3 = f32[8,128]{1,0:T(8,128)S(1)} collective-permute-done((f32[8,128]{1,0:T(8,128)S(1)}, f32[8,128]{1,0:T(8,128)S(1)}, u32[]{:S(2)}, u32[]{:S(2)}) %collective-permute-start.3) | collective-permute-done | bytes 4128 | tf_op jit(solution)/shard_map/ppermute | solution.py:31
  22.3 1.7 %collective-permute-start.4 = (f32[8,128]{1,0:T(8,128)S(1)}, f32[8,128]{1,0:T(8,128)S(1)}, u32[]{:S(2)}, u32[]{:S(2)}) collective-permute-start(f32[8,128]{1,0:T(8,128)S(1)} %add.13), channel_id=1, source_target_pairs={{0,4},{4,0},{1,5},{5,1},{2,6},{6,2},{3,7},{7,3},{8,12},{12,8},{9,1... | collective-permute-start | bytes 12296 | tf_op jit(solution)/shard_map/ppermute | solution.py:31
  24.0 1.9 %collective-permute-done.4 = f32[8,128]{1,0:T(8,128)S(1)} collective-permute-done((f32[8,128]{1,0:T(8,128)S(1)}, f32[8,128]{1,0:T(8,128)S(1)}, u32[]{:S(2)}, u32[]{:S(2)}) %collective-permute-start.4) | collective-permute-done | bytes 4128 | tf_op jit(solution)/shard_map/ppermute | solution.py:31
  25.9 2.7 %collective-permute-start.5 = (f32[8,128]{1,0:T(8,128)S(1)}, f32[8,128]{1,0:T(8,128)S(1)}, u32[]{:S(2)}, u32[]{:S(2)}) collective-permute-start(f32[8,128]{1,0:T(8,128)S(1)} %add.14), channel_id=1, source_target_pairs={{0,8},{8,0},{1,9},{9,1},{2,10},{10,2},{3,11},{11,3},{4,12},{12,4},... | collective-permute-start | bytes 12296 | tf_op jit(solution)/shard_map/ppermute | solution.py:31
  28.6 1.8 %collective-permute-done.5 = f32[8,128]{1,0:T(8,128)S(1)} collective-permute-done((f32[8,128]{1,0:T(8,128)S(1)}, f32[8,128]{1,0:T(8,128)S(1)}, u32[]{:S(2)}, u32[]{:S(2)}) %collective-permute-start.5) | collective-permute-done | bytes 4128 | tf_op jit(solution)/shard_map/ppermute | solution.py:31
  30.4 0.9 %factor.1 = (f32[64,8,128]{2,1,0:T(8,128)S(1)}, f32[128,128]{1,0:T(8,128)}) custom-call(f32[8,128]{1,0:T(8,128)S(1)} %add.15.refs_0_), custom_call_target="tpu_custom_call" | custom-call | tf_op jit(solution)/shard_map/factor/pallas_call | solution.py:459
  31.3 1.3 %project.3.refs_3_ = f32[8,16,4,8,128]{4,3,2,1,0:T(8,128)} custom-call(f32[64,8,128]{2,1,0:T(8,128)S(1)} %get-tuple-element.17.refs_0_, f32[16,8,512]{2,1,0:T(8,128)S(1)} %get-tuple-element.11.refs_0_.refs_1_, f32[16,8,512]{2,1,0:T(8,128)S(1)} %collective-permute-done.refs_3_.refs_2_), custom_call_target="tpu_custom_call" | custom-call | flops 4194304 | bytes 1048576 | tf_op jit(solution)/shard_map/project/pallas_call | solution.py:521
  32.6 0.3 collective-permute-done.7.refs_2_
  32.9 2.0 %project.4.refs_3_ = f32[8,16,4,8,128]{4,3,2,1,0:T(8,128)} custom-call(f32[64,8,128]{2,1,0:T(8,128)S(1)} %get-tuple-element.17.refs_0_, f32[16,8,1024]{2,1,0:T(8,128)S(1)} %get-tuple-element.13.refs_1_, f32[16,8,1024]{2,1,0:T(8,128)S(1)} %collective-permute-done.7.refs_2_, f32[8,16,4,8,128]{4,3,2,1,0:T(8,128)} %project.3.refs_3_), custom_call_target="tpu_custom_call", output_to_operand_aliasing={{}: (3, {})} | custom-call | flops 8388608 | bytes 2097152 | tf_op jit(solution)/shard_map/project/pallas_call | solution.py:521
  34.9 0.0 collective-permute-done.6.refs_2_
  35.0 1.3 %project.5 = f32[8,16,4,8,128]{4,3,2,1,0:T(8,128)} custom-call(f32[64,8,128]{2,1,0:T(8,128)S(1)} %get-tuple-element.17.refs_0_, f32[16,8,512]{2,1,0:T(8,128)S(1)} %get-tuple-element.14.refs_2_.refs_1_, f32[16,8,512]{2,1,0:T(8,128)S(1)} %collective-permute-done.6.refs_2_, f32[8,16,4,8,128]{4,3,2,1,0:T(8,128)} %project.4.refs_3_), custom_call_target="tpu_custom_call", output_to_operand_aliasing={{}: (3, {})} | custom-call | flops 4194304 | bytes 1048576 | tf_op jit(solution)/shard_map/project/pallas_call | solution.py:521
  (5 shorter events, 0.0 us)
Async XLA Ops:
  3.5 12.4 %collective-permute-start = (f32[16,8,512]{2,1,0:T(8,128)S(1)}, f32[16,8,512]{2,1,0:T(8,128)S(1)}, u32[]{:S(2)}, u32[]{:S(2)}) collective-permute-start(f32[16,8,512]{2,1,0:T(8,128)S(1)} %get-tuple-element.12.refs_4_), channel_id=1, source_target_pairs={{0,16},{16,0},{1,17},{17,1},{2,18},{18,2},{3,19},{19,3},{4,20},{20... | collective-permute-start | bytes 786440 | tf_op jit(solution)/shard_map/ppermute | solution.py:541
  13.7 3.8 %collective-permute-start.1 = (f32[8,128]{1,0:T(8,128)S(1)}, f32[8,128]{1,0:T(8,128)S(1)}, u32[]{:S(2)}, u32[]{:S(2)}) collective-permute-start(f32[8,128]{1,0:T(8,128)S(1)} %get-tuple-element.15), channel_id=1, source_target_pairs={{0,16},{16,0},{1,17},{17,1},{2,18},{18,2},{3,19},{19,3},{4,20},{20... | collective-permute-start | bytes 12296 | tf_op jit(solution)/shard_map/ppermute | solution.py:541
  13.8 21.1 %collective-permute-start.6 = (f32[16,8,512]{2,1,0:T(8,128)S(1)}, f32[16,8,512]{2,1,0:T(8,128)S(1)}, u32[]{:S(2)}, u32[]{:S(2)}) collective-permute-start(f32[16,8,512]{2,1,0:T(8,128)S(1)} %get-tuple-element.18), channel_id=1, source_target_pairs={{0,16},{16,0},{1,17},{17,1},{2,18},{18,2},{3,19},{19,3},{4,20},{20... | collective-permute-start | bytes 786440 | tf_op jit(solution)/shard_map/ppermute | solution.py:541
  15.8 17.1 %collective-permute-start.7 = (f32[16,8,1024]{2,1,0:T(8,128)S(1)}, f32[16,8,1024]{2,1,0:T(8,128)S(1)}, u32[]{:S(2)}, u32[]{:S(2)}) collective-permute-start(f32[16,8,1024]{2,1,0:T(8,128)S(1)} %get-tuple-element.19), channel_id=1, source_target_pairs={{0,16},{16,0},{1,17},{17,1},{2,18},{18,2},{3,19},{19,3},{4,20},{20... | collective-permute-start | bytes 1572872 | tf_op jit(solution)/shard_map/ppermute | solution.py:541
  17.5 1.2 %collective-permute-start.2 = (f32[8,128]{1,0:T(8,128)S(1)}, f32[8,128]{1,0:T(8,128)S(1)}, u32[]{:S(2)}, u32[]{:S(2)}) collective-permute-start(f32[8,128]{1,0:T(8,128)S(1)} %join.1), channel_id=1, source_target_pairs={{0,1},{1,0},{2,3},{3,2},{4,5},{5,4},{6,7},{7,6},{8,9},{9,8},{10,11... | collective-permute-start | bytes 12296 | tf_op jit(solution)/shard_map/ppermute | solution.py:31
  18.7 3.6 %collective-permute-start.3 = (f32[8,128]{1,0:T(8,128)S(1)}, f32[8,128]{1,0:T(8,128)S(1)}, u32[]{:S(2)}, u32[]{:S(2)}) collective-permute-start(f32[8,128]{1,0:T(8,128)S(1)} %add.12), channel_id=1, source_target_pairs={{0,2},{2,0},{1,3},{3,1},{4,6},{6,4},{5,7},{7,5},{8,10},{10,8},{9,1... | collective-permute-start | bytes 12296 | tf_op jit(solution)/shard_map/ppermute | solution.py:31
  22.3 3.6 %collective-permute-start.4 = (f32[8,128]{1,0:T(8,128)S(1)}, f32[8,128]{1,0:T(8,128)S(1)}, u32[]{:S(2)}, u32[]{:S(2)}) collective-permute-start(f32[8,128]{1,0:T(8,128)S(1)} %add.13), channel_id=1, source_target_pairs={{0,4},{4,0},{1,5},{5,1},{2,6},{6,2},{3,7},{7,3},{8,12},{12,8},{9,1... | collective-permute-start | bytes 12296 | tf_op jit(solution)/shard_map/ppermute | solution.py:31
  25.9 4.5 %collective-permute-start.5 = (f32[8,128]{1,0:T(8,128)S(1)}, f32[8,128]{1,0:T(8,128)S(1)}, u32[]{:S(2)}, u32[]{:S(2)}) collective-permute-start(f32[8,128]{1,0:T(8,128)S(1)} %add.14), channel_id=1, source_target_pairs={{0,8},{8,0},{1,9},{9,1},{2,10},{10,2},{3,11},{11,3},{4,12},{12,4},... | collective-permute-start | bytes 12296 | tf_op jit(solution)/shard_map/ppermute | solution.py:31

commit v3 on v2

--- a/solution.py
+++ b/solution.py
@@ -15,8 +15,12 @@
 GAP_HIGH = 192
 LANES = 128
 ROWS = 8
+GROUPS = ((0, 1), (2, 3, 4), (5, 6, 7))
+UNROLL = True
+WINDOW = 3
+PAD = 1
 JOIN_FLOPS = 10**10
-VMEM_BYTES = 48 * 1024 * 1024
+VMEM_BYTES = 24 * 1024 * 1024
 PAIRS = [(a, b) for a in range(NBLK) for b in range(a, NBLK)]
 ENTRIES = [(0, a, b) for a, b in PAIRS] + [(1, a, b) for a, b in PAIRS if a < b]
 
@@ -172,17 +176,16 @@
     return [jnp.sum(part, axis=1, keepdims=True) for part in parts]
 
 
-def coeff_chunk(flow_ref, arrived, high_ref, low_ref, fh_ref, fl_ref, acc_ref, slabs):
-    total = flow_ref.shape[0] // slabs
+def coeff_chunk(flow_ref, total, base, high_ref, low_ref, fh_ref, fl_ref, acc_ref, slabs):
+    apart = flow_ref.shape[0] // total
     per_block = 2 * NFREQ
     spans = reach(total)
     started = [False] * NBLK
     shift, left = [None] * slabs, [0.0] * slabs
     for i, t0 in enumerate(range(0, total, BLOCK)):
         t1 = min(t0 + BLOCK, total)
-        arrived(i)
         for l in range(slabs):
-            values = flow_ref[pl.ds(t0 * slabs + l, t1 - t0, stride=slabs), :]
+            values = flow_ref[pl.ds(t0 * apart + base + l, t1 - t0, stride=apart), :]
             if i == 0:
                 shift[l] = jnp.sum(values, axis=0, keepdims=True) * (1.0 / (t1 - t0))
             values = values - shift[l]
@@ -222,15 +225,15 @@
             own_ref[jp] = piece[ROWS:]
 
 
-def spectra_kernel(slabs, first, pieces, earlier, *refs):
-    freq_hbm, start_hbm, snap_ref, weight_hbm, *rest = refs
-    count = sum(pieces)
-    outs = len(pieces)
+def spectra_kernel(pieces, earlier, freq_hbm, start_hbm, weight_hbm, snap_ref, *rest):
+    first = len(earlier)
+    count, outs = sum(pieces), len(pieces)
+    total, chunks, slabs, _ = snap_ref.shape
     sends, owns, rest = rest[:outs], rest[outs : 2 * outs], rest[2 * outs :]
     if earlier:
         gram_ref, *rest = rest
-    freq_ref, start_ref, weight_ref, held = rest[:4]
-    high_ref, low_ref, fh_ref, fl_ref, acc_ref, sems, small_sems = rest[4:]
+    freq_ref, start_ref, weight_ref, high_ref, low_ref, fh_ref, fl_ref, acc_ref, *rest = rest
+    small_sems = rest[0]
     small = [
         pltpu.make_async_copy(source, target, small_sems.at[i])
         for i, (source, target) in enumerate(
@@ -239,62 +242,63 @@
     ]
     for copy in small:
         copy.start()
-    total = snap_ref.shape[0]
-    copies = []
-    for i in range(count):
-        copies.append([])
-        step = total
-        for k, t0 in enumerate(range(0, total, step)):
-            times = pl.ds(t0, min(step, total - t0))
-            source = snap_ref.at[times, :, pl.ds((first + i) * LANES, LANES)]
-            copies[i].append(pltpu.make_async_copy(source, held.at[i, times], sems.at[i, k]))
-            copies[i][k].start()
+    held, sems = rest[1:]
+    copies = [
+        pltpu.make_async_copy(snap_ref.at[:, first + i], held.at[i], sems.at[i]) for i in range(count)
+    ]
+    for copy in copies[:WINDOW]:
+        copy.start()
     for copy in small:
         copy.wait()
     sums = fill_table(freq_ref, start_ref, high_ref, low_ref)
     places = [(piece, at) for piece, size in enumerate(pieces) for at in range(size)]
-    for i in range(count):
-        flat = held.at[i].reshape(total * slabs, LANES)
+    for i, (piece, at) in enumerate(places):
         weight = weight_ref[:, (first + i) * LANES : (first + i + 1) * LANES]
         root = jnp.concatenate([jnp.sqrt(weight[l : l + 1, :]) for l in range(slabs)], axis=1)
+        copies[i].wait()
+        if i + WINDOW < count:
+            copies[i + WINDOW].start()
+        flat = held.at[i].reshape(total * slabs, LANES)
         left = coeff_chunk(
-            flat, lambda k: copies[i][k].wait() if k < len(copies[i]) else None, high_ref, low_ref, fh_ref, fl_ref, acc_ref, slabs
+            flat, total, 0, high_ref, low_ref, fh_ref, fl_ref, acc_ref, slabs
         )
-        piece, at = places[i]
         cols = slice(at * slabs * LANES, (at + 1) * slabs * LANES)
         store_chunk(acc_ref, left, sums, root, sends[piece].at[:, :, cols], owns[piece].at[:, :, cols])
     if earlier:
         gram_ref[...] = gram_sums([*earlier, *sends])
 
 
-def spectra_call(snapshots, weights, freq_bins, block_starts, first, pieces, earlier=()):
-    total, slabs, _ = snapshots.shape
+def spectra_call(snapshots, weights, freq_bins, block_starts, pieces, earlier=()):
+    total, slabs, cells = snapshots.shape
+    by_chunk = snapshots.reshape(total, slabs, -1, LANES).transpose(0, 2, 1, 3)
     cols = slabs * LANES
     count, outs, more = sum(pieces), len(pieces), len(earlier)
     shapes = [jax.ShapeDtypeStruct((2 * NBLK, ROWS, n * cols), jnp.float32) for n in pieces] * 2
     if more:
         shapes.append(jax.ShapeDtypeStruct((ROWS, LANES), jnp.float32))
     wide = -(-total // LANES) * LANES + LANES
+    small = [pltpu.with_memory_space_constraint(v, pltpu.HBM) for v in (freq_bins, block_starts, weights)]
+    if not more:
+        by_chunk = pltpu.with_memory_space_constraint(by_chunk, pltpu.HBM)
     given = pl.pallas_call(
-        lambda *refs: spectra_kernel(
-            slabs, first, pieces, refs[4 : 4 + more], *refs[:4], *refs[4 + more :]
-        ),
+        lambda *refs: spectra_kernel(pieces, refs[4 : 4 + more], *refs[:4], *refs[4 + more :]),
         out_shape=tuple(shapes),
-        in_specs=[pl.BlockSpec(memory_space=pltpu.HBM)] * 4
+        in_specs=[pl.BlockSpec(memory_space=pltpu.HBM)] * 3
+        + [pl.BlockSpec(memory_space=pltpu.VMEM if more else pltpu.HBM)]
         + [pl.BlockSpec(memory_space=pltpu.VMEM)] * more,
         out_specs=(pl.BlockSpec(memory_space=pltpu.VMEM),) * len(shapes),
         scratch_shapes=[
             pltpu.SMEM(freq_bins.shape, jnp.int32),
             pltpu.SMEM(block_starts.shape, jnp.int32),
             pltpu.VMEM(weights.shape, jnp.float32),
-            pltpu.VMEM((count, total, slabs, LANES), jnp.float32),
             pltpu.VMEM((2 * NBLK * NFREQ, wide), jnp.bfloat16),
             pltpu.VMEM((2 * NBLK * NFREQ, wide), jnp.bfloat16),
             pltpu.VMEM((total, cols), jnp.bfloat16),
             pltpu.VMEM((total, cols), jnp.bfloat16),
             pltpu.VMEM((2 * NBLK * NFREQ, cols), jnp.float32),
-            pltpu.SemaphoreType.DMA((count, -(-total // BLOCK))),
             pltpu.SemaphoreType.DMA((3,)),
+            pltpu.VMEM((count, total, slabs, LANES), jnp.float32),
+            pltpu.SemaphoreType.DMA((count,)),
         ],
         compiler_params=pltpu.CompilerParams(vmem_limit_bytes=VMEM_BYTES),
         cost_estimate=pl.CostEstimate(
@@ -303,7 +307,7 @@
             transcendentals=0,
         ),
         name="spectra",
-    )(freq_bins, block_starts, snapshots, weights, *earlier)
+    )(*small, by_chunk, *earlier)
     return given[:outs], given[outs : 2 * outs], given[2 * outs :]
 
 
@@ -346,26 +350,25 @@
 
 def gram_sums(blocks):
     sums = {}
-    for a in range(NBLK):
-        row = [(0, a, b) for b in range(a, NBLK)] + [(1, a, b) for b in range(a + 1, NBLK)]
-        carry = tuple(jnp.zeros((ROWS, LANES), jnp.float32) for _ in row)
+    for group in GROUPS:
+        keys = [key for key in ENTRIES if key[1] in group]
+        carry = tuple(jnp.zeros((ROWS, LANES), jnp.float32) for _ in keys)
         for ref in blocks:
 
-            def body(k, carry, ref=ref, a=a, row=row):
+            def body(k, carry, ref=ref, group=group, keys=keys):
                 cols = pl.ds(pl.multiple_of(k * LANES, LANES), LANES)
-                re = {b: ref[2 * b, :, cols] for b in range(a, NBLK)}
-                im = {b: ref[2 * b + 1, :, cols] for b in range(a, NBLK)}
+                re = {b: ref[2 * b, :, cols] for b in range(group[0], NBLK)}
+                im = {b: ref[2 * b + 1, :, cols] for b in range(group[0], NBLK)}
                 out = []
-                for (kind, _, b), total in zip(row, carry):
+                for (kind, a, b), total in zip(keys, carry):
                     if kind == 0:
                         out.append(total + (re[a] * re[b] + im[a] * im[b]))
                     else:
                         out.append(total + (re[a] * im[b] - im[a] * re[b]))
                 return tuple(out)
 
-            carry = lax.fori_loop(0, ref.shape[2] // LANES, body, carry, unroll=4)
-        for key, total in zip(row, carry):
-            sums[key] = total
+            carry = lax.fori_loop(0, ref.shape[2] // LANES, body, carry, unroll=UNROLL)
+        sums.update(zip(keys, carry))
     return fold_lanes([sums[key] for key in ENTRIES])
 
 
@@ -471,7 +474,7 @@
 
 def project_chunk(slabs, inv_ref, own_ref, far_ref, first, flat):
     band = lax.axis_index("band")
-    per = 2 * NBLK * 2 * slabs
+    per = flat.shape[0] // ROWS
     for side, ref in enumerate((own_ref, far_ref)):
         base = (band if side == 0 else 1 - band) * slabs
         for l0 in range(0, slabs, 2):
@@ -498,10 +501,10 @@
 def project_kernel(slabs, at, inv_ref, own_ref, far_ref, *rest):
     out_ref, held, sems = rest[-3:]
     count = held.shape[0]
-    per = 2 * NBLK * 2 * slabs
+    per = (2 * NBLK + PAD) * 2 * slabs
 
     def copy_of(i):
-        return pltpu.make_async_copy(held.at[i], out_ref.at[:, :, at + i], sems.at[i])
+        return pltpu.make_async_copy(held.at[i, :, : 2 * NBLK], out_ref.at[:, :, at + i], sems.at[i])
 
     def body(i, _):
         flat = held.at[i].reshape(ROWS * per, LANES)
@@ -517,7 +520,6 @@
 def project_call(inv, own, far, modes, at, slabs, chunks):
     count = own.shape[2] // (slabs * LANES)
     given = [] if modes is None else [modes]
-    block = (ROWS, 2 * NBLK, 2 * slabs, LANES)
     return pl.pallas_call(
         lambda *refs: project_kernel(slabs, at, *refs),
         out_shape=jax.ShapeDtypeStruct((ROWS, 2 * NBLK, chunks, 2 * slabs, LANES), jnp.float32),
@@ -526,7 +528,7 @@
         out_specs=pl.BlockSpec(memory_space=pltpu.HBM),
         input_output_aliases={3: 0} if given else {},
         scratch_shapes=[
-            pltpu.VMEM((count, *block), jnp.float32),
+            pltpu.VMEM((count, ROWS, 2 * NBLK + PAD, 2 * slabs, LANES), jnp.float32),
             pltpu.SemaphoreType.DMA((count,)),
         ],
         compiler_params=pltpu.CompilerParams(vmem_limit_bytes=VMEM_BYTES),
@@ -545,14 +547,11 @@
     slabs, cells = snapshots.shape[1:]
     chunks = cells // LANES
     count = 2 * slabs * cells * lax.axis_size("space")
-    given = [
-        pltpu.with_memory_space_constraint(array, pltpu.HBM)
-        for array in (snapshots, quad_weights, freq_bins, block_starts)
-    ]
+    given = (snapshots, quad_weights, freq_bins, block_starts)
     pieces = (chunks - 2, 1) if chunks > 2 else (1,)
-    sends, owns, _ = spectra_call(*given, 0, (1,))
+    sends, owns, _ = spectra_call(*given, (1,))
     fars = [swap_bands(sends[0])]
-    later, owns_later, (gram_send,) = spectra_call(*given, 1, pieces, sends)
+    later, owns_later, (gram_send,) = spectra_call(*given, pieces, sends)
     far_gram = swap_bands(gram_send)
     fars += [swap_bands(send) for send in later]
     owns = [*owns, *owns_later]

time: 36.5 us -> 35.7 us (0.978)
  Pallas kernels: 16.9 us -> 14.4 us
  starting transfers between devices: 11.2 us -> 12.2 us
  waiting for transfers between devices: 7.54 us -> 8.27 us
    ppermute x4, starting transfers between devices: 5.2 us -> 6.46 us  [swap_bands(): return lax.ppermute(block, 'band', [(0, 1), (1, 0)])]
    pallas_call x2, Pallas kernels: 10.1 us -> 8.86 us  [spectra_call(): pl.pallas_call(lambda *refs: spectra_kernel(pieces, refs[4:4 + more], *re...]
    pallas_call x3, Pallas kernels: 4.67 us -> 3.62 us  [project_call(): pl.pallas_call(lambda *refs: project_kernel(slabs, at, *refs), out_shape=...]
    ppermute x4, waiting for transfers between devices: 0.65 us -> 1.06 us  [swap_bands(): return lax.ppermute(block, 'band', [(0, 1), (1, 0)])]
  transfers between devices with their start and end apart: 8 -> 8, of which waited for: 6 -> 5; matrix products, arithmetic and copies ran while one was open for 0% -> 0% of each run, Pallas kernels for 35% -> 29%
where the time goes in v3:
time: 35.7 us; the launch traced here: 35.6 us
  Pallas kernels  14.4 us (40%)
  starting transfers between devices  12.2 us (34%)
  waiting for transfers between devices  8.27 us (23%)
  between operations  0.7 us (2%)
    pallas_call x2, Pallas kernels, spectra_call(): pl.pallas_call(lambda *refs: spectra_kernel(pieces, refs[4:4 + more], *re...  8.86 us
    ppermute x4, waiting for transfers between devices, from_partner(): return lax.ppermute(block, axis, route)  7.21 us
    ppermute x4, starting transfers between devices, swap_bands(): return lax.ppermute(block, 'band', [(0, 1), (1, 0)])  6.46 us
    ppermute x4, starting transfers between devices, from_partner(): return lax.ppermute(block, axis, route)  5.69 us
    pallas_call x3, Pallas kernels, project_call(): pl.pallas_call(lambda *refs: project_kernel(slabs, at, *refs), out_shape=...  3.62 us
    pallas_call x1, Pallas kernels, gram_call(): pl.pallas_call(lambda *refs: gram_kernel(len(blocks), *refs), out_shape=j...  1.06 us
    ppermute x4, waiting for transfers between devices, swap_bands(): return lax.ppermute(block, 'band', [(0, 1), (1, 0)])  1.06 us
    pallas_call x1, Pallas kernels, factor_call(): pl.pallas_call(lambda *refs: factor_kernel(count, *refs), out_shape=(jax....  0.89 us
  transfers between devices with their start and end apart: 8, of which 5 were waited for; matrix products, arithmetic and copies ran while one was open for 0% of the time, Pallas kernels for 29%

profile of v3, /device:TPU:0, one launch (start us, length us, event | category | flops | bytes accessed | tf_op | source)
XLA Modules:
  0.0 35.6 jit_solution(18259370958203137037)
XLA Ops:
  0.6 0.0 copy-start
  0.6 3.0 %spectra.2 = (f32[16,8,512]{2,1,0:T(8,128)S(1)}, f32[16,8,512]{2,1,0:T(8,128)S(1)}) custom-call(s32[16]{0:T(128)} %refs_0_.3, s32[8]{0:T(128)} %refs_1_.3, f32[4,512]{1,0:T(4,128)} %refs_2_.3, f32[1152,4,4,128]{3,2,1,0:T(4,128)} %bitcast.10), custom_call_target="tpu_custom_call" | custom-call | flops 905969664 | bytes 2883584 | tf_op jit(solution)/shard_map/spectra/pallas_call | solution.py:283
  3.6 3.0 %collective-permute-start = (f32[16,8,512]{2,1,0:T(8,128)S(1)}, f32[16,8,512]{2,1,0:T(8,128)S(1)}, u32[]{:S(2)}, u32[]{:S(2)}) collective-permute-start(f32[16,8,512]{2,1,0:T(8,128)S(1)} %get-tuple-element.12.refs_4_), channel_id=1, source_target_pairs={{0,16},{16,0},{1,17},{17,1},{2,18},{18,2},{3,19},{19,3},{4,20},{20... | collective-permute-start | bytes 786440 | tf_op jit(solution)/shard_map/ppermute | solution.py:543
  6.7 0.0 copy-done
  6.7 5.9 %spectra.3 = (f32[16,8,1024]{2,1,0:T(8,128)S(1)}, f32[16,8,512]{2,1,0:T(8,128)S(1)}, f32[16,8,1024]{2,1,0:T(8,128)S(1)}, f32[16,8,512]{2,1,0:T(8,128)S(1)}, f32[8,128]{1,0:T(8,128)S(1)}) custom-call(s32[16]{0:T(128)} %refs_0_.3, s32[8]{0:T(128)} %refs_1_.3, f32[4,512]{1,0:T(4,128)} %refs_2_.3, f32[1152,4,4,128]{3,2,1,0:T(4,128)S(1)} %bitcast.11, ...), custom_call_target="tpu_custom_call" | custom-call | flops 2717908992 | bytes 8650752 | tf_op jit(solution)/shard_map/spectra/pallas_call | solution.py:283
  12.5 1.4 %collective-permute-start.1 = (f32[8,128]{1,0:T(8,128)S(1)}, f32[8,128]{1,0:T(8,128)S(1)}, u32[]{:S(2)}, u32[]{:S(2)}) collective-permute-start(f32[8,128]{1,0:T(8,128)S(1)} %get-tuple-element.15), channel_id=1, source_target_pairs={{0,16},{16,0},{1,17},{17,1},{2,18},{18,2},{3,19},{19,3},{4,20},{20... | collective-permute-start | bytes 12296 | tf_op jit(solution)/shard_map/ppermute | solution.py:543
  14.0 0.7 %collective-permute-start.6 = (f32[16,8,512]{2,1,0:T(8,128)S(1)}, f32[16,8,512]{2,1,0:T(8,128)S(1)}, u32[]{:S(2)}, u32[]{:S(2)}) collective-permute-start(f32[16,8,512]{2,1,0:T(8,128)S(1)} %get-tuple-element.18), channel_id=1, source_target_pairs={{0,16},{16,0},{1,17},{17,1},{2,18},{18,2},{3,19},{19,3},{4,20},{20... | collective-permute-start | bytes 786440 | tf_op jit(solution)/shard_map/ppermute | solution.py:543
  14.6 1.3 %collective-permute-start.7 = (f32[16,8,1024]{2,1,0:T(8,128)S(1)}, f32[16,8,1024]{2,1,0:T(8,128)S(1)}, u32[]{:S(2)}, u32[]{:S(2)}) collective-permute-start(f32[16,8,1024]{2,1,0:T(8,128)S(1)} %get-tuple-element.19), channel_id=1, source_target_pairs={{0,16},{16,0},{1,17},{17,1},{2,18},{18,2},{3,19},{19,3},{4,20},{20... | collective-permute-start | bytes 1572872 | tf_op jit(solution)/shard_map/ppermute | solution.py:543
  16.0 0.0 collective-permute-done.refs_3_.refs_2_
  16.0 1.1 %gram.1.own_ref = f32[8,128]{1,0:T(8,128)S(1)} custom-call(f32[16,8,512]{2,1,0:T(8,128)S(1)} %get-tuple-element.11.refs_0_.refs_1_, f32[16,8,1024]{2,1,0:T(8,128)S(1)} %get-tuple-element.13.refs_1_, f32[16,8,512]{2,1,0:T(8,128)S(1)} %get-tuple-element.14.refs_2_.refs_1_, f32[16,8,512]{2,1,0:T(8,128)S(1)} %collective-permute-done.refs_3_.refs_2_), custom_call_target="tpu_custom_call" | custom-call | flops 8388608 | bytes 1048576 | tf_op jit(solution)/shard_map/gram/pallas_call | solution.py:380
  17.0 0.0 collective-permute-done.1.far_ref
  17.1 0.0 collective-permute-start.2
  17.1 1.2 %collective-permute-done.2 = f32[8,128]{1,0:T(8,128)S(1)} collective-permute-done((f32[8,128]{1,0:T(8,128)S(1)}, f32[8,128]{1,0:T(8,128)S(1)}, u32[]{:S(2)}, u32[]{:S(2)}) %collective-permute-start.2) | collective-permute-done | bytes 4128 | tf_op jit(solution)/shard_map/ppermute | solution.py:35
  18.2 1.5 %collective-permute-start.3 = (f32[8,128]{1,0:T(8,128)S(1)}, f32[8,128]{1,0:T(8,128)S(1)}, u32[]{:S(2)}, u32[]{:S(2)}) collective-permute-start(f32[8,128]{1,0:T(8,128)S(1)} %add.12), channel_id=1, source_target_pairs={{0,2},{2,0},{1,3},{3,1},{4,6},{6,4},{5,7},{7,5},{8,10},{10,8},{9,1... | collective-permute-start | bytes 12296 | tf_op jit(solution)/shard_map/ppermute | solution.py:35
  19.7 2.1 %collective-permute-done.3 = f32[8,128]{1,0:T(8,128)S(1)} collective-permute-done((f32[8,128]{1,0:T(8,128)S(1)}, f32[8,128]{1,0:T(8,128)S(1)}, u32[]{:S(2)}, u32[]{:S(2)}) %collective-permute-start.3) | collective-permute-done | bytes 4128 | tf_op jit(solution)/shard_map/ppermute | solution.py:35
  21.9 1.6 %collective-permute-start.4 = (f32[8,128]{1,0:T(8,128)S(1)}, f32[8,128]{1,0:T(8,128)S(1)}, u32[]{:S(2)}, u32[]{:S(2)}) collective-permute-start(f32[8,128]{1,0:T(8,128)S(1)} %add.13), channel_id=1, source_target_pairs={{0,4},{4,0},{1,5},{5,1},{2,6},{6,2},{3,7},{7,3},{8,12},{12,8},{9,1... | collective-permute-start | bytes 12296 | tf_op jit(solution)/shard_map/ppermute | solution.py:35
  23.4 2.0 %collective-permute-done.4 = f32[8,128]{1,0:T(8,128)S(1)} collective-permute-done((f32[8,128]{1,0:T(8,128)S(1)}, f32[8,128]{1,0:T(8,128)S(1)}, u32[]{:S(2)}, u32[]{:S(2)}) %collective-permute-start.4) | collective-permute-done | bytes 4128 | tf_op jit(solution)/shard_map/ppermute | solution.py:35
  25.5 2.6 %collective-permute-start.5 = (f32[8,128]{1,0:T(8,128)S(1)}, f32[8,128]{1,0:T(8,128)S(1)}, u32[]{:S(2)}, u32[]{:S(2)}) collective-permute-start(f32[8,128]{1,0:T(8,128)S(1)} %add.14), channel_id=1, source_target_pairs={{0,8},{8,0},{1,9},{9,1},{2,10},{10,2},{3,11},{11,3},{4,12},{12,4},... | collective-permute-start | bytes 12296 | tf_op jit(solution)/shard_map/ppermute | solution.py:35
  28.1 1.9 %collective-permute-done.5 = f32[8,128]{1,0:T(8,128)S(1)} collective-permute-done((f32[8,128]{1,0:T(8,128)S(1)}, f32[8,128]{1,0:T(8,128)S(1)}, u32[]{:S(2)}, u32[]{:S(2)}) %collective-permute-start.5) | collective-permute-done | bytes 4128 | tf_op jit(solution)/shard_map/ppermute | solution.py:35
  30.0 0.9 %factor.1 = (f32[64,8,128]{2,1,0:T(8,128)S(1)}, f32[128,128]{1,0:T(8,128)}) custom-call(f32[8,128]{1,0:T(8,128)S(1)} %add.15.refs_0_), custom_call_target="tpu_custom_call" | custom-call | tf_op jit(solution)/shard_map/factor/pallas_call | solution.py:462
  30.9 1.1 %project.3.refs_3_ = f32[8,16,4,8,128]{4,3,2,1,0:T(8,128)} custom-call(f32[64,8,128]{2,1,0:T(8,128)S(1)} %get-tuple-element.17.refs_0_, f32[16,8,512]{2,1,0:T(8,128)S(1)} %get-tuple-element.11.refs_0_.refs_1_, f32[16,8,512]{2,1,0:T(8,128)S(1)} %collective-permute-done.refs_3_.refs_2_), custom_call_target="tpu_custom_call" | custom-call | flops 4194304 | bytes 1048576 | tf_op jit(solution)/shard_map/project/pallas_call | solution.py:523
  32.0 1.1 %collective-permute-done.7.refs_2_ = f32[16,8,1024]{2,1,0:T(8,128)S(1)} collective-permute-done((f32[16,8,1024]{2,1,0:T(8,128)S(1)}, f32[16,8,1024]{2,1,0:T(8,128)S(1)}, u32[]{:S(2)}, u32[]{:S(2)}) %collective-permute-start.7) | collective-permute-done | bytes 524320 | tf_op jit(solution)/shard_map/ppermute | solution.py:543
  33.0 1.5 %project.4.refs_3_ = f32[8,16,4,8,128]{4,3,2,1,0:T(8,128)} custom-call(f32[64,8,128]{2,1,0:T(8,128)S(1)} %get-tuple-element.17.refs_0_, f32[16,8,1024]{2,1,0:T(8,128)S(1)} %get-tuple-element.13.refs_1_, f32[16,8,1024]{2,1,0:T(8,128)S(1)} %collective-permute-done.7.refs_2_, f32[8,16,4,8,128]{4,3,2,1,0:T(8,128)} %project.3.refs_3_), custom_call_target="tpu_custom_call", output_to_operand_aliasing={{}: (3, {})} | custom-call | flops 8388608 | bytes 2097152 | tf_op jit(solution)/shard_map/project/pallas_call | solution.py:523
  34.5 0.0 collective-permute-done.6.refs_2_
  34.5 1.1 %project.5 = f32[8,16,4,8,128]{4,3,2,1,0:T(8,128)} custom-call(f32[64,8,128]{2,1,0:T(8,128)S(1)} %get-tuple-element.17.refs_0_, f32[16,8,512]{2,1,0:T(8,128)S(1)} %get-tuple-element.14.refs_2_.refs_1_, f32[16,8,512]{2,1,0:T(8,128)S(1)} %collective-permute-done.6.refs_2_, f32[8,16,4,8,128]{4,3,2,1,0:T(8,128)} %project.4.refs_3_), custom_call_target="tpu_custom_call", output_to_operand_aliasing={{}: (3, {})} | custom-call | flops 4194304 | bytes 1048576 | tf_op jit(solution)/shard_map/project/pallas_call | solution.py:523
  (5 shorter events, 0.0 us)
Async XLA Ops:
  0.6 6.0 %copy-start = (f32[1152,4,512]{2,1,0:T(4,128)S(1)}, f32[1152,4,512]{2,1,0:T(4,128)}, u32[]{:S(2)}) copy-start(f32[1152,4,512]{2,1,0:T(4,128)} %param.4) | copy-start | bytes 28311556
  3.6 12.3 %collective-permute-start = (f32[16,8,512]{2,1,0:T(8,128)S(1)}, f32[16,8,512]{2,1,0:T(8,128)S(1)}, u32[]{:S(2)}, u32[]{:S(2)}) collective-permute-start(f32[16,8,512]{2,1,0:T(8,128)S(1)} %get-tuple-element.12.refs_4_), channel_id=1, source_target_pairs={{0,16},{16,0},{1,17},{17,1},{2,18},{18,2},{3,19},{19,3},{4,20},{20... | collective-permute-start | bytes 786440 | tf_op jit(solution)/shard_map/ppermute | solution.py:543
  12.5 4.5 %collective-permute-start.1 = (f32[8,128]{1,0:T(8,128)S(1)}, f32[8,128]{1,0:T(8,128)S(1)}, u32[]{:S(2)}, u32[]{:S(2)}) collective-permute-start(f32[8,128]{1,0:T(8,128)S(1)} %get-tuple-element.15), channel_id=1, source_target_pairs={{0,16},{16,0},{1,17},{17,1},{2,18},{18,2},{3,19},{19,3},{4,20},{20... | collective-permute-start | bytes 12296 | tf_op jit(solution)/shard_map/ppermute | solution.py:543
  14.0 20.5 %collective-permute-start.6 = (f32[16,8,512]{2,1,0:T(8,128)S(1)}, f32[16,8,512]{2,1,0:T(8,128)S(1)}, u32[]{:S(2)}, u32[]{:S(2)}) collective-permute-start(f32[16,8,512]{2,1,0:T(8,128)S(1)} %get-tuple-element.18), channel_id=1, source_target_pairs={{0,16},{16,0},{1,17},{17,1},{2,18},{18,2},{3,19},{19,3},{4,20},{20... | collective-permute-start | bytes 786440 | tf_op jit(solution)/shard_map/ppermute | solution.py:543
  14.6 18.4 %collective-permute-start.7 = (f32[16,8,1024]{2,1,0:T(8,128)S(1)}, f32[16,8,1024]{2,1,0:T(8,128)S(1)}, u32[]{:S(2)}, u32[]{:S(2)}) collective-permute-start(f32[16,8,1024]{2,1,0:T(8,128)S(1)} %get-tuple-element.19), channel_id=1, source_target_pairs={{0,16},{16,0},{1,17},{17,1},{2,18},{18,2},{3,19},{19,3},{4,20},{20... | collective-permute-start | bytes 1572872 | tf_op jit(solution)/shard_map/ppermute | solution.py:543
  17.1 1.2 %collective-permute-start.2 = (f32[8,128]{1,0:T(8,128)S(1)}, f32[8,128]{1,0:T(8,128)S(1)}, u32[]{:S(2)}, u32[]{:S(2)}) collective-permute-start(f32[8,128]{1,0:T(8,128)S(1)} %join.1), channel_id=1, source_target_pairs={{0,1},{1,0},{2,3},{3,2},{4,5},{5,4},{6,7},{7,6},{8,9},{9,8},{10,11... | collective-permute-start | bytes 12296 | tf_op jit(solution)/shard_map/ppermute | solution.py:35
  18.2 3.6 %collective-permute-start.3 = (f32[8,128]{1,0:T(8,128)S(1)}, f32[8,128]{1,0:T(8,128)S(1)}, u32[]{:S(2)}, u32[]{:S(2)}) collective-permute-start(f32[8,128]{1,0:T(8,128)S(1)} %add.12), channel_id=1, source_target_pairs={{0,2},{2,0},{1,3},{3,1},{4,6},{6,4},{5,7},{7,5},{8,10},{10,8},{9,1... | collective-permute-start | bytes 12296 | tf_op jit(solution)/shard_map/ppermute | solution.py:35
  21.9 3.6 %collective-permute-start.4 = (f32[8,128]{1,0:T(8,128)S(1)}, f32[8,128]{1,0:T(8,128)S(1)}, u32[]{:S(2)}, u32[]{:S(2)}) collective-permute-start(f32[8,128]{1,0:T(8,128)S(1)} %add.13), channel_id=1, source_target_pairs={{0,4},{4,0},{1,5},{5,1},{2,6},{6,2},{3,7},{7,3},{8,12},{12,8},{9,1... | collective-permute-start | bytes 12296 | tf_op jit(solution)/shard_map/ppermute | solution.py:35
  25.5 4.5 %collective-permute-start.5 = (f32[8,128]{1,0:T(8,128)S(1)}, f32[8,128]{1,0:T(8,128)S(1)}, u32[]{:S(2)}, u32[]{:S(2)}) collective-permute-start(f32[8,128]{1,0:T(8,128)S(1)} %add.14), channel_id=1, source_target_pairs={{0,8},{8,0},{1,9},{9,1},{2,10},{10,2},{3,11},{11,3},{4,12},{12,4},... | collective-permute-start | bytes 12296 | tf_op jit(solution)/shard_map/ppermute | solution.py:35

commit v4 on v3

--- a/solution.py
+++ b/solution.py
@@ -373,16 +373,21 @@
 
 
 def gram_kernel(count, *refs):
-    refs[-1][...] = gram_sums(refs[:count])
-
-
-def gram_call(blocks, after):
+    refs[-2][...] = gram_sums(refs[:count])
+
+
+def gram_call(blocks, after, passed):
+    count = len(blocks)
     return pl.pallas_call(
-        lambda *refs: gram_kernel(len(blocks), *refs),
-        out_shape=jax.ShapeDtypeStruct((ROWS, LANES), jnp.float32),
-        in_specs=[pl.BlockSpec(memory_space=pltpu.VMEM)] * len(blocks)
-        + [pl.BlockSpec(memory_space=pl.ANY)],
-        out_specs=pl.BlockSpec(memory_space=pltpu.VMEM),
+        lambda *refs: gram_kernel(count, *refs),
+        out_shape=(
+            jax.ShapeDtypeStruct((ROWS, LANES), jnp.float32),
+            jax.ShapeDtypeStruct(passed.shape, passed.dtype),
+        ),
+        in_specs=[pl.BlockSpec(memory_space=pltpu.VMEM)] * count
+        + [pl.BlockSpec(memory_space=pl.ANY)] * 2,
+        out_specs=(pl.BlockSpec(memory_space=pltpu.VMEM), pl.BlockSpec(memory_space=pl.ANY)),
+        input_output_aliases={count + 1: 1},
         compiler_params=pltpu.CompilerParams(vmem_limit_bytes=VMEM_BYTES),
         cost_estimate=pl.CostEstimate(
             flops=sum(block.size for block in blocks) * 4 * NBLK,
@@ -390,7 +395,7 @@
             transcendentals=0,
         ),
         name="gram",
-    )(*blocks, after)
+    )(*blocks, after, passed)
 
 
 def join_kernel(own_ref, far_ref, out_ref):
@@ -498,45 +503,52 @@
                         flat[pl.ds(line, ROWS, stride=per), :] = value
 
 
-def project_kernel(slabs, at, inv_ref, own_ref, far_ref, *rest):
-    out_ref, held, sems = rest[-3:]
-    count = held.shape[0]
+def project_kernel(slabs, at, sizes, inv_ref, *refs):
+    out_ref, held, sems = refs[-3:]
     per = (2 * NBLK + PAD) * 2 * slabs
 
     def copy_of(i):
         return pltpu.make_async_copy(held.at[i, :, : 2 * NBLK], out_ref.at[:, :, at + i], sems.at[i])
 
-    def body(i, _):
-        flat = held.at[i].reshape(ROWS * per, LANES)
-        project_chunk(slabs, inv_ref, own_ref, far_ref, i * slabs * LANES, flat)
-        copy_of(i).start()
-        return 0
-
-    lax.fori_loop(0, count, body, 0)
-    for i in range(count):
+    done = 0
+    for piece, size in enumerate(sizes):
+        own_ref, far_ref = refs[2 * piece : 2 * piece + 2]
+
+        def body(i, _, own_ref=own_ref, far_ref=far_ref, done=done):
+            flat = held.at[done + i].reshape(ROWS * per, LANES)
+            project_chunk(slabs, inv_ref, own_ref, far_ref, i * slabs * LANES, flat)
+            copy_of(done + i).start()
+            return 0
+
+        lax.fori_loop(0, size, body, 0)
+        done += size
+    for i in range(done):
         copy_of(i).wait()
 
 
-def project_call(inv, own, far, modes, at, slabs, chunks):
-    count = own.shape[2] // (slabs * LANES)
+def project_call(inv, pairs, modes, at, slabs, chunks):
+    sizes = [own.shape[2] // (slabs * LANES) for own, _ in pairs]
+    count = sum(sizes)
     given = [] if modes is None else [modes]
+    arrays = [array for pair in pairs for array in pair]
+    values = sum(array.size for array in arrays)
     return pl.pallas_call(
-        lambda *refs: project_kernel(slabs, at, *refs),
+        lambda *refs: project_kernel(slabs, at, sizes, *refs),
         out_shape=jax.ShapeDtypeStruct((ROWS, 2 * NBLK, chunks, 2 * slabs, LANES), jnp.float32),
-        in_specs=[pl.BlockSpec(memory_space=pltpu.VMEM)] * 3
+        in_specs=[pl.BlockSpec(memory_space=pltpu.VMEM)] * (1 + len(arrays))
         + [pl.BlockSpec(memory_space=pltpu.HBM)] * len(given),
         out_specs=pl.BlockSpec(memory_space=pltpu.HBM),
-        input_output_aliases={3: 0} if given else {},
+        input_output_aliases={1 + len(arrays): 0} if given else {},
         scratch_shapes=[
             pltpu.VMEM((count, ROWS, 2 * NBLK + PAD, 2 * slabs, LANES), jnp.float32),
             pltpu.SemaphoreType.DMA((count,)),
         ],
         compiler_params=pltpu.CompilerParams(vmem_limit_bytes=VMEM_BYTES),
         cost_estimate=pl.CostEstimate(
-            flops=8 * own.size * NBLK, bytes_accessed=16 * own.size, transcendentals=0
+            flops=4 * values * NBLK, bytes_accessed=8 * values, transcendentals=0
         ),
         name="project",
-    )(inv, own, far, *given)
+    )(inv, *arrays, *given)
 
 
 def swap_bands(block):
@@ -548,21 +560,19 @@
     chunks = cells // LANES
     count = 2 * slabs * cells * lax.axis_size("space")
     given = (snapshots, quad_weights, freq_bins, block_starts)
-    pieces = (chunks - 2, 1) if chunks > 2 else (1,)
-    sends, owns, _ = spectra_call(*given, (1,))
-    fars = [swap_bands(sends[0])]
-    later, owns_later, (gram_send,) = spectra_call(*given, pieces, sends)
+    (send_a,), (own_a,), _ = spectra_call(*given, (1,))
+    far_a = swap_bands(send_a)
+    (send_b, send_c), (own_b, own_c), (gram_send,) = spectra_call(*given, (chunks - 2, 1), [send_a])
     far_gram = swap_bands(gram_send)
-    fars += [swap_bands(send) for send in later]
-    owns = [*owns, *owns_later]
-    total = join_call(gram_call(owns, fars[0]), far_gram)
+    far_b = swap_bands(send_b)
+    gram_own, send_c = gram_call([own_a, own_b, own_c], far_a, send_c)
+    far_c = swap_bands(send_c)
+    total = join_call(gram_own, far_gram)
     for level in range(lax.axis_size("space").bit_length() - 1):
         total = total + from_partner(total, "space", level)
     inv, fac = factor_call(total, count)
-    modes, at = None, 0
-    for size, own, far in zip((1, *pieces), owns, fars):
-        modes = project_call(inv, own, far, modes, at, slabs, chunks)
-        at += size
+    modes = project_call(inv, [(own_a, far_a), (own_b, far_b)], None, 0, slabs, chunks)
+    modes = project_call(inv, [(own_c, far_c)], modes, chunks - 1, slabs, chunks)
     modes = modes.reshape(ROWS, 2, NBLK, chunks, 2 * slabs, LANES)
     modes = modes.transpose(0, 1, 2, 4, 3, 5).reshape(ROWS, 2, NBLK, 2 * slabs, cells)
     factor = fac[:, :NBLK].reshape(ROWS, 2, NBLK, NBLK)
@@ -572,7 +582,7 @@
 def shards(snapshots, *others):
     fits = NFREQ == ROWS * lax.axis_size("band") == 2 * ROWS
     fits = fits and snapshots.shape[1] == SLABS // 2 and snapshots.shape[2] % LANES == 0
-    fits = fits and snapshots.shape[2] > LANES and snapshots.shape[0] % LANES == 0
+    fits = fits and snapshots.shape[2] > 2 * LANES and snapshots.shape[0] % LANES == 0
     return (two_bands if fits else any_bands)(snapshots, *others)
 
 

time: 35.7 us -> 34.2 us (0.958)
  Pallas kernels: 14.4 us -> 13.6 us
  waiting for transfers between devices: 8.27 us -> 7.6 us
    pallas_call x4 -> x3, Pallas kernels: 4.68 us -> 3.9 us  [the longest x2 2.84 us: project_call(): pl.pallas_call(lambda *refs: project_kernel(slabs, at, sizes, *refs), out...]
    ppermute x4, waiting for transfers between devices: 1.06 us -> 0.39 us  [swap_bands(): return lax.ppermute(block, 'band', [(0, 1), (1, 0)])]
  transfers between devices with their start and end apart: 8 -> 8, of which waited for: 5 -> 5; matrix products, arithmetic and copies ran while one was open for 0% -> 0% of each run, Pallas kernels for 29% -> 28%
where the time goes in v4:
time: 34.2 us; the launch traced here: 34.1 us
  Pallas kernels  13.6 us (40%)
  starting transfers between devices  12.1 us (35%)
  waiting for transfers between devices  7.6 us (22%)
  between operations  0.68 us (2%)
    pallas_call x2, Pallas kernels, spectra_call(): pl.pallas_call(lambda *refs: spectra_kernel(pieces, refs[4:4 + more], *re...  8.86 us
    ppermute x4, waiting for transfers between devices, from_partner(): return lax.ppermute(block, axis, route)  7.22 us
    ppermute x4, starting transfers between devices, swap_bands(): return lax.ppermute(block, 'band', [(0, 1), (1, 0)])  6.47 us
    ppermute x4, starting transfers between devices, from_partner(): return lax.ppermute(block, axis, route)  5.66 us
    pallas_call x2, Pallas kernels, project_call(): pl.pallas_call(lambda *refs: project_kernel(slabs, at, sizes, *refs), out...  2.84 us
    pallas_call x1, Pallas kernels, gram_call(): pl.pallas_call(lambda *refs: gram_kernel(count, *refs), out_shape=(jax.Sh...  1.06 us
    pallas_call x1, Pallas kernels, factor_call(): pl.pallas_call(lambda *refs: factor_kernel(count, *refs), out_shape=(jax....  0.89 us
  transfers between devices with their start and end apart: 8, of which 5 were waited for; matrix products, arithmetic and copies ran while one was open for 0% of the time, Pallas kernels for 28%

profile of v4, /device:TPU:0, one launch (start us, length us, event | category | flops | bytes accessed | tf_op | source)
XLA Modules:
  0.0 34.1 jit_solution(5276952375900154005)
XLA Ops:
  0.6 0.0 copy-start
  0.6 3.0 %spectra.2 = (f32[16,8,512]{2,1,0:T(8,128)S(1)}, f32[16,8,512]{2,1,0:T(8,128)S(1)}) custom-call(s32[16]{0:T(128)} %refs_0_.3, s32[8]{0:T(128)} %refs_1_.3, f32[4,512]{1,0:T(4,128)} %refs_2_.3, f32[1152,4,4,128]{3,2,1,0:T(4,128)} %bitcast.10), custom_call_target="tpu_custom_call" | custom-call | flops 905969664 | bytes 2883584 | tf_op jit(solution)/shard_map/spectra/pallas_call | solution.py:283
  3.6 3.0 %collective-permute-start = (f32[16,8,512]{2,1,0:T(8,128)S(1)}, f32[16,8,512]{2,1,0:T(8,128)S(1)}, u32[]{:S(2)}, u32[]{:S(2)}) collective-permute-start(f32[16,8,512]{2,1,0:T(8,128)S(1)} %get-tuple-element.14.refs_4_), channel_id=1, source_target_pairs={{0,16},{16,0},{1,17},{17,1},{2,18},{18,2},{3,19},{19,3},{4,20},{20... | collective-permute-start | bytes 786440 | tf_op jit(solution)/shard_map/ppermute | solution.py:555
  6.7 0.0 copy-done
  6.7 5.9 %spectra.3 = (f32[16,8,1024]{2,1,0:T(8,128)S(1)}, f32[16,8,512]{2,1,0:T(8,128)S(1)}, f32[16,8,1024]{2,1,0:T(8,128)S(1)}, f32[16,8,512]{2,1,0:T(8,128)S(1)}, f32[8,128]{1,0:T(8,128)S(1)}) custom-call(s32[16]{0:T(128)} %refs_0_.3, s32[8]{0:T(128)} %refs_1_.3, f32[4,512]{1,0:T(4,128)} %refs_2_.3, f32[1152,4,4,128]{3,2,1,0:T(4,128)S(1)} %bitcast.11, ...), custom_call_target="tpu_custom_call" | custom-call | flops 2717908992 | bytes 8650752 | tf_op jit(solution)/shard_map/spectra/pallas_call | solution.py:283
  12.5 1.4 %collective-permute-start.1 = (f32[8,128]{1,0:T(8,128)S(1)}, f32[8,128]{1,0:T(8,128)S(1)}, u32[]{:S(2)}, u32[]{:S(2)}) collective-permute-start(f32[8,128]{1,0:T(8,128)S(1)} %get-tuple-element.19), channel_id=1, source_target_pairs={{0,16},{16,0},{1,17},{17,1},{2,18},{18,2},{3,19},{19,3},{4,20},{20... | collective-permute-start | bytes 12296 | tf_op jit(solution)/shard_map/ppermute | solution.py:555
  14.0 0.7 %collective-permute-start.7 = (f32[16,8,1024]{2,1,0:T(8,128)S(1)}, f32[16,8,1024]{2,1,0:T(8,128)S(1)}, u32[]{:S(2)}, u32[]{:S(2)}) collective-permute-start(f32[16,8,1024]{2,1,0:T(8,128)S(1)} %get-tuple-element.23), channel_id=1, source_target_pairs={{0,16},{16,0},{1,17},{17,1},{2,18},{18,2},{3,19},{19,3},{4,20},{20... | collective-permute-start | bytes 1572872 | tf_op jit(solution)/shard_map/ppermute | solution.py:555
  14.6 0.0 collective-permute-done.refs_3_.refs_2_
  14.6 1.1 %gram.1 = (f32[8,128]{1,0:T(8,128)S(1)}, f32[16,8,512]{2,1,0:T(8,128)S(1)}) custom-call(f32[16,8,512]{2,1,0:T(8,128)S(1)} %get-tuple-element.13.refs_0_.refs_1_, f32[16,8,1024]{2,1,0:T(8,128)S(1)} %get-tuple-element.15.refs_1_.refs_3_, f32[16,8,512]{2,1,0:T(8,128)S(1)} %get-tuple-element.16.refs_2_.refs_1_, ...), custom_call_target="tpu_custom_call", output_to_operand_aliasing={{1}: (4, {})} | custom-call | flops 8388608 | bytes 1048576 | tf_op jit(solution)/shard_map/gram/pallas_call | solution.py:381
  15.7 1.3 %collective-permute-start.6 = (f32[16,8,512]{2,1,0:T(8,128)S(1)}, f32[16,8,512]{2,1,0:T(8,128)S(1)}, u32[]{:S(2)}, u32[]{:S(2)}) collective-permute-start(f32[16,8,512]{2,1,0:T(8,128)S(1)} %get-tuple-element.22), channel_id=1, source_target_pairs={{0,16},{16,0},{1,17},{17,1},{2,18},{18,2},{3,19},{19,3},{4,20},{20... | collective-permute-start | bytes 786440 | tf_op jit(solution)/shard_map/ppermute | solution.py:555
  17.1 0.0 collective-permute-done.1.far_ref
  17.1 0.0 collective-permute-start.2
  17.1 1.2 %collective-permute-done.2 = f32[8,128]{1,0:T(8,128)S(1)} collective-permute-done((f32[8,128]{1,0:T(8,128)S(1)}, f32[8,128]{1,0:T(8,128)S(1)}, u32[]{:S(2)}, u32[]{:S(2)}) %collective-permute-start.2) | collective-permute-done | bytes 4128 | tf_op jit(solution)/shard_map/ppermute | solution.py:35
  18.2 1.5 %collective-permute-start.3 = (f32[8,128]{1,0:T(8,128)S(1)}, f32[8,128]{1,0:T(8,128)S(1)}, u32[]{:S(2)}, u32[]{:S(2)}) collective-permute-start(f32[8,128]{1,0:T(8,128)S(1)} %add.12), channel_id=1, source_target_pairs={{0,2},{2,0},{1,3},{3,1},{4,6},{6,4},{5,7},{7,5},{8,10},{10,8},{9,1... | collective-permute-start | bytes 12296 | tf_op jit(solution)/shard_map/ppermute | solution.py:35
  19.7 2.1 %collective-permute-done.3 = f32[8,128]{1,0:T(8,128)S(1)} collective-permute-done((f32[8,128]{1,0:T(8,128)S(1)}, f32[8,128]{1,0:T(8,128)S(1)}, u32[]{:S(2)}, u32[]{:S(2)}) %collective-permute-start.3) | collective-permute-done | bytes 4128 | tf_op jit(solution)/shard_map/ppermute | solution.py:35
  21.8 1.6 %collective-permute-start.4 = (f32[8,128]{1,0:T(8,128)S(1)}, f32[8,128]{1,0:T(8,128)S(1)}, u32[]{:S(2)}, u32[]{:S(2)}) collective-permute-start(f32[8,128]{1,0:T(8,128)S(1)} %add.13), channel_id=1, source_target_pairs={{0,4},{4,0},{1,5},{5,1},{2,6},{6,2},{3,7},{7,3},{8,12},{12,8},{9,1... | collective-permute-start | bytes 12296 | tf_op jit(solution)/shard_map/ppermute | solution.py:35
  23.4 2.0 %collective-permute-done.4 = f32[8,128]{1,0:T(8,128)S(1)} collective-permute-done((f32[8,128]{1,0:T(8,128)S(1)}, f32[8,128]{1,0:T(8,128)S(1)}, u32[]{:S(2)}, u32[]{:S(2)}) %collective-permute-start.4) | collective-permute-done | bytes 4128 | tf_op jit(solution)/shard_map/ppermute | solution.py:35
  25.5 2.6 %collective-permute-start.5 = (f32[8,128]{1,0:T(8,128)S(1)}, f32[8,128]{1,0:T(8,128)S(1)}, u32[]{:S(2)}, u32[]{:S(2)}) collective-permute-start(f32[8,128]{1,0:T(8,128)S(1)} %add.14), channel_id=1, source_target_pairs={{0,8},{8,0},{1,9},{9,1},{2,10},{10,2},{3,11},{11,3},{4,12},{12,4},... | collective-permute-start | bytes 12296 | tf_op jit(solution)/shard_map/ppermute | solution.py:35
  28.0 1.9 %collective-permute-done.5 = f32[8,128]{1,0:T(8,128)S(1)} collective-permute-done((f32[8,128]{1,0:T(8,128)S(1)}, f32[8,128]{1,0:T(8,128)S(1)}, u32[]{:S(2)}, u32[]{:S(2)}) %collective-permute-start.5) | collective-permute-done | bytes 4128 | tf_op jit(solution)/shard_map/ppermute | solution.py:35
  30.0 0.9 %factor.1 = (f32[64,8,128]{2,1,0:T(8,128)S(1)}, f32[128,128]{1,0:T(8,128)}) custom-call(f32[8,128]{1,0:T(8,128)S(1)} %add.15.refs_0_), custom_call_target="tpu_custom_call" | custom-call | tf_op jit(solution)/shard_map/factor/pallas_call | solution.py:467
  30.8 0.0 collective-permute-done.7.refs_4_
  30.9 1.8 %project.2.refs_3_ = f32[8,16,4,8,128]{4,3,2,1,0:T(8,128)} custom-call(f32[64,8,128]{2,1,0:T(8,128)S(1)} %get-tuple-element.21.refs_0_, f32[16,8,512]{2,1,0:T(8,128)S(1)} %get-tuple-element.13.refs_0_.refs_1_, f32[16,8,512]{2,1,0:T(8,128)S(1)} %collective-permute-done.refs_3_.refs_2_, f32[16,8,1024]{2,1,0:T(8,128)S(1)} %get-tuple-element.15.refs_1_.refs_3_, ...), custom_call_target="tpu_custom_call" | custom-call | flops 12582912 | bytes 3145728 | tf_op jit(solution)/shard_map/project/pallas_call | solution.py:535
  32.6 0.4 %collective-permute-done.6.refs_2_ = f32[16,8,512]{2,1,0:T(8,128)S(1)} collective-permute-done((f32[16,8,512]{2,1,0:T(8,128)S(1)}, f32[16,8,512]{2,1,0:T(8,128)S(1)}, u32[]{:S(2)}, u32[]{:S(2)}) %collective-permute-start.6) | collective-permute-done | bytes 262176 | tf_op jit(solution)/shard_map/ppermute | solution.py:555
  33.0 1.1 %project.3 = f32[8,16,4,8,128]{4,3,2,1,0:T(8,128)} custom-call(f32[64,8,128]{2,1,0:T(8,128)S(1)} %get-tuple-element.21.refs_0_, f32[16,8,512]{2,1,0:T(8,128)S(1)} %get-tuple-element.16.refs_2_.refs_1_, f32[16,8,512]{2,1,0:T(8,128)S(1)} %collective-permute-done.6.refs_2_, f32[8,16,4,8,128]{4,3,2,1,0:T(8,128)} %project.2.refs_3_), custom_call_target="tpu_custom_call", output_to_operand_aliasing={{}: (3, {})} | custom-call | flops 4194304 | bytes 1048576 | tf_op jit(solution)/shard_map/project/pallas_call | solution.py:535
  (5 shorter events, 0.0 us)
Async XLA Ops:
  0.6 6.0 %copy-start = (f32[1152,4,512]{2,1,0:T(4,128)S(1)}, f32[1152,4,512]{2,1,0:T(4,128)}, u32[]{:S(2)}) copy-start(f32[1152,4,512]{2,1,0:T(4,128)} %param.4) | copy-start | bytes 28311556
  3.6 11.0 %collective-permute-start = (f32[16,8,512]{2,1,0:T(8,128)S(1)}, f32[16,8,512]{2,1,0:T(8,128)S(1)}, u32[]{:S(2)}, u32[]{:S(2)}) collective-permute-start(f32[16,8,512]{2,1,0:T(8,128)S(1)} %get-tuple-element.14.refs_4_), channel_id=1, source_target_pairs={{0,16},{16,0},{1,17},{17,1},{2,18},{18,2},{3,19},{19,3},{4,20},{20... | collective-permute-start | bytes 786440 | tf_op jit(solution)/shard_map/ppermute | solution.py:555
  12.5 4.5 %collective-permute-start.1 = (f32[8,128]{1,0:T(8,128)S(1)}, f32[8,128]{1,0:T(8,128)S(1)}, u32[]{:S(2)}, u32[]{:S(2)}) collective-permute-start(f32[8,128]{1,0:T(8,128)S(1)} %get-tuple-element.19), channel_id=1, source_target_pairs={{0,16},{16,0},{1,17},{17,1},{2,18},{18,2},{3,19},{19,3},{4,20},{20... | collective-permute-start | bytes 12296 | tf_op jit(solution)/shard_map/ppermute | solution.py:555
  14.0 16.9 %collective-permute-start.7 = (f32[16,8,1024]{2,1,0:T(8,128)S(1)}, f32[16,8,1024]{2,1,0:T(8,128)S(1)}, u32[]{:S(2)}, u32[]{:S(2)}) collective-permute-start(f32[16,8,1024]{2,1,0:T(8,128)S(1)} %get-tuple-element.23), channel_id=1, source_target_pairs={{0,16},{16,0},{1,17},{17,1},{2,18},{18,2},{3,19},{19,3},{4,20},{20... | collective-permute-start | bytes 1572872 | tf_op jit(solution)/shard_map/ppermute | solution.py:555
  15.7 17.3 %collective-permute-start.6 = (f32[16,8,512]{2,1,0:T(8,128)S(1)}, f32[16,8,512]{2,1,0:T(8,128)S(1)}, u32[]{:S(2)}, u32[]{:S(2)}) collective-permute-start(f32[16,8,512]{2,1,0:T(8,128)S(1)} %get-tuple-element.22), channel_id=1, source_target_pairs={{0,16},{16,0},{1,17},{17,1},{2,18},{18,2},{3,19},{19,3},{4,20},{20... | collective-permute-start | bytes 786440 | tf_op jit(solution)/shard_map/ppermute | solution.py:555
  17.1 1.2 %collective-permute-start.2 = (f32[8,128]{1,0:T(8,128)S(1)}, f32[8,128]{1,0:T(8,128)S(1)}, u32[]{:S(2)}, u32[]{:S(2)}) collective-permute-start(f32[8,128]{1,0:T(8,128)S(1)} %join.1), channel_id=1, source_target_pairs={{0,1},{1,0},{2,3},{3,2},{4,5},{5,4},{6,7},{7,6},{8,9},{9,8},{10,11... | collective-permute-start | bytes 12296 | tf_op jit(solution)/shard_map/ppermute | solution.py:35
  18.2 3.6 %collective-permute-start.3 = (f32[8,128]{1,0:T(8,128)S(1)}, f32[8,128]{1,0:T(8,128)S(1)}, u32[]{:S(2)}, u32[]{:S(2)}) collective-permute-start(f32[8,128]{1,0:T(8,128)S(1)} %add.12), channel_id=1, source_target_pairs={{0,2},{2,0},{1,3},{3,1},{4,6},{6,4},{5,7},{7,5},{8,10},{10,8},{9,1... | collective-permute-start | bytes 12296 | tf_op jit(solution)/shard_map/ppermute | solution.py:35
  21.8 3.6 %collective-permute-start.4 = (f32[8,128]{1,0:T(8,128)S(1)}, f32[8,128]{1,0:T(8,128)S(1)}, u32[]{:S(2)}, u32[]{:S(2)}) collective-permute-start(f32[8,128]{1,0:T(8,128)S(1)} %add.13), channel_id=1, source_target_pairs={{0,4},{4,0},{1,5},{5,1},{2,6},{6,2},{3,7},{7,3},{8,12},{12,8},{9,1... | collective-permute-start | bytes 12296 | tf_op jit(solution)/shard_map/ppermute | solution.py:35
  25.5 4.5 %collective-permute-start.5 = (f32[8,128]{1,0:T(8,128)S(1)}, f32[8,128]{1,0:T(8,128)S(1)}, u32[]{:S(2)}, u32[]{:S(2)}) collective-permute-start(f32[8,128]{1,0:T(8,128)S(1)} %add.14), channel_id=1, source_target_pairs={{0,8},{8,0},{1,9},{9,1},{2,10},{10,2},{3,11},{11,3},{4,12},{12,4},... | collective-permute-start | bytes 12296 | tf_op jit(solution)/shard_map/ppermute | solution.py:35

commit v5 on v4

--- a/solution.py
+++ b/solution.py
@@ -16,8 +16,6 @@
 LANES = 128
 ROWS = 8
 GROUPS = ((0, 1), (2, 3, 4), (5, 6, 7))
-UNROLL = True
-WINDOW = 3
 PAD = 1
 JOIN_FLOPS = 10**10
 VMEM_BYTES = 24 * 1024 * 1024
@@ -176,30 +174,31 @@
     return [jnp.sum(part, axis=1, keepdims=True) for part in parts]
 
 
-def coeff_chunk(flow_ref, total, base, high_ref, low_ref, fh_ref, fl_ref, acc_ref, slabs):
+def coeff_chunk(flow_ref, total, high_ref, low_ref, fh_ref, fl_ref, acc_ref, low, high, beside):
     apart = flow_ref.shape[0] // total
     per_block = 2 * NFREQ
     spans = reach(total)
     started = [False] * NBLK
+    slabs, wide = high - low, (high - low) * LANES
     shift, left = [None] * slabs, [0.0] * slabs
     for i, t0 in enumerate(range(0, total, BLOCK)):
         t1 = min(t0 + BLOCK, total)
         for l in range(slabs):
-            values = flow_ref[pl.ds(t0 * apart + base + l, t1 - t0, stride=apart), :]
+            values = flow_ref[pl.ds(t0 * apart + low + l, t1 - t0, stride=apart), :]
             if i == 0:
                 shift[l] = jnp.sum(values, axis=0, keepdims=True) * (1.0 / (t1 - t0))
             values = values - shift[l]
             left[l] += jnp.sum(values.reshape(-1, ROWS, LANES), axis=0)
-            high = values.astype(jnp.bfloat16)
+            upper = values.astype(jnp.bfloat16)
             cols = slice(l * LANES, (l + 1) * LANES)
-            fh_ref[t0:t1, cols] = high
-            fl_ref[t0:t1, cols] = (values - high.astype(jnp.float32)).astype(jnp.bfloat16)
+            fh_ref[t0:t1, cols] = upper
+            fl_ref[t0:t1, cols] = (values - upper.astype(jnp.float32)).astype(jnp.bfloat16)
     for i, t0 in enumerate(range(0, total, BLOCK)):
         t1 = min(t0 + BLOCK, total)
         hit = [j for j in range(NBLK) if spans[j][0] < t1 and spans[j][1] > t0]
         j0, j1 = min(hit), max(hit) + 1
         rows = slice(j0 * per_block, j1 * per_block)
-        xh, xl = fh_ref[t0:t1, :], fl_ref[t0:t1, :]
+        xh, xl = fh_ref[t0:t1, :wide], fl_ref[t0:t1, :wide]
         th, tl = high_ref[rows, t0:t1], low_ref[rows, t0:t1]
         part = jnp.dot(
             jnp.concatenate([th, tl, th], axis=1),
@@ -209,8 +208,12 @@
         for j in range(j0, j1):
             own = slice(j * per_block, (j + 1) * per_block)
             piece = part[(j - j0) * per_block : (j - j0 + 1) * per_block]
-            acc_ref[own, :] = acc_ref[own, :] + piece if started[j] else piece
+            acc_ref[own, :wide] = acc_ref[own, :wide] + piece if started[j] else piece
             started[j] = True
+        if beside:
+            beside.pop(0)()
+    while beside:
+        beside.pop(0)()
     left = [jnp.sum(rest, axis=0, keepdims=True) * (1.0 / total) for rest in left]
     return jnp.concatenate(left, axis=1)
 
@@ -220,68 +223,87 @@
         mean_part = sums[p] * left
         for j in range(NBLK):
             jp = 2 * j + p
-            piece = (acc_ref[jp * NFREQ : (jp + 1) * NFREQ, :] - mean_part) * root
+            piece = (acc_ref[jp * NFREQ : (jp + 1) * NFREQ, : left.shape[1]] - mean_part) * root
             send_ref[jp] = piece[:ROWS]
             own_ref[jp] = piece[ROWS:]
 
 
-def spectra_kernel(pieces, earlier, freq_hbm, start_hbm, weight_hbm, snap_ref, *rest):
-    first = len(earlier)
-    count, outs = sum(pieces), len(pieces)
-    total, chunks, slabs, _ = snap_ref.shape
-    sends, owns, rest = rest[:outs], rest[outs : 2 * outs], rest[2 * outs :]
+def spectra_kernel(units, earlier, freq_hbm, start_hbm, weight_hbm, snap_ref, *rest):
+    count = len(units)
+    total, _, slabs, _ = snap_ref.shape
+    send_ref, own_ref, *rest = rest
     if earlier:
+        kept_ref, high_ref, low_ref, sums_ref = earlier[1:]
         gram_ref, *rest = rest
-    freq_ref, start_ref, weight_ref, high_ref, low_ref, fh_ref, fl_ref, acc_ref, *rest = rest
-    small_sems = rest[0]
+    else:
+        kept_ref, high_ref, low_ref, sums_ref, *rest = rest
+    freq_ref, start_ref, weight_ref, fh_ref, fl_ref, acc_ref, small_sems, held, sems, *rest = rest
+    small = [(weight_hbm, weight_ref)]
+    if not earlier:
+        small += [(freq_hbm, freq_ref), (start_hbm, start_ref)]
     small = [
         pltpu.make_async_copy(source, target, small_sems.at[i])
-        for i, (source, target) in enumerate(
-            ((freq_hbm, freq_ref), (start_hbm, start_ref), (weight_hbm, weight_ref))
-        )
+        for i, (source, target) in enumerate(small)
     ]
     for copy in small:
         copy.start()
-    held, sems = rest[1:]
+    place = count - 1 if not earlier else 0
+    targets = [kept_ref if i == place else held.at[i - (i > place)] for i in range(count)]
     copies = [
-        pltpu.make_async_copy(snap_ref.at[:, first + i], held.at[i], sems.at[i]) for i in range(count)
+        pltpu.make_async_copy(snap_ref.at[:, chunk], targets[i], sems.at[i])
+        for i, (chunk, _, _) in enumerate(units)
+        if i != place or not earlier
     ]
-    for copy in copies[:WINDOW]:
+    for copy in copies:
         copy.start()
     for copy in small:
         copy.wait()
-    sums = fill_table(freq_ref, start_ref, high_ref, low_ref)
-    places = [(piece, at) for piece, size in enumerate(pieces) for at in range(size)]
-    for i, (piece, at) in enumerate(places):
-        weight = weight_ref[:, (first + i) * LANES : (first + i + 1) * LANES]
-        root = jnp.concatenate([jnp.sqrt(weight[l : l + 1, :]) for l in range(slabs)], axis=1)
-        copies[i].wait()
-        if i + WINDOW < count:
-            copies[i + WINDOW].start()
-        flat = held.at[i].reshape(total * slabs, LANES)
+    if earlier:
+        copies.insert(0, None)
+        sums = [sums_ref[p, :, :1] for p in range(2)]
+    else:
+        sums = fill_table(freq_ref, start_ref, high_ref, low_ref)
+        for p in range(2):
+            sums_ref[p] = jnp.broadcast_to(sums[p], (NFREQ, LANES))
+    beside = gram_steps(earlier[0], slice(None), rest[0], True) if earlier else []
+    at = 0
+    for i, (chunk, low, high) in enumerate(units):
+        weight = weight_ref[:, chunk * LANES : (chunk + 1) * LANES]
+        root = jnp.concatenate([jnp.sqrt(weight[l : l + 1, :]) for l in range(low, high)], axis=1)
+        if copies[i] is not None:
+            copies[i].wait()
+        flat = targets[i].reshape(total * slabs, LANES)
         left = coeff_chunk(
-            flat, total, 0, high_ref, low_ref, fh_ref, fl_ref, acc_ref, slabs
+            flat, total, high_ref, low_ref, fh_ref, fl_ref, acc_ref, low, high, beside
         )
-        cols = slice(at * slabs * LANES, (at + 1) * slabs * LANES)
-        store_chunk(acc_ref, left, sums, root, sends[piece].at[:, :, cols], owns[piece].at[:, :, cols])
+        cols = slice(at, at + (high - low) * LANES)
+        at = cols.stop
+        store_chunk(acc_ref, left, sums, root, send_ref.at[:, :, cols], own_ref.at[:, :, cols])
+        if earlier:
+            beside = gram_steps(send_ref, cols, rest[0], False)
     if earlier:
-        gram_ref[...] = gram_sums([*earlier, *sends])
-
-
-def spectra_call(snapshots, weights, freq_bins, block_starts, pieces, earlier=()):
+        for step in beside:
+            step()
+        gram_ref[...] = fold_lanes([rest[0][e] for e in range(len(ENTRIES))])
+
+
+def spectra_call(snapshots, weights, freq_bins, block_starts, units, earlier=()):
     total, slabs, cells = snapshots.shape
     by_chunk = snapshots.reshape(total, slabs, -1, LANES).transpose(0, 2, 1, 3)
-    cols = slabs * LANES
-    count, outs, more = sum(pieces), len(pieces), len(earlier)
-    shapes = [jax.ShapeDtypeStruct((2 * NBLK, ROWS, n * cols), jnp.float32) for n in pieces] * 2
+    cols, count, more = slabs * LANES, len(units), len(earlier)
+    values = sum(high - low for _, low, high in units) * LANES
+    shapes = [jax.ShapeDtypeStruct((2 * NBLK, ROWS, values), jnp.float32)] * 2
     if more:
         shapes.append(jax.ShapeDtypeStruct((ROWS, LANES), jnp.float32))
-    wide = -(-total // LANES) * LANES + LANES
+    else:
+        table = jax.ShapeDtypeStruct((2 * NBLK * NFREQ, total + LANES), jnp.bfloat16)
+        shapes.append(jax.ShapeDtypeStruct((total, slabs, LANES), jnp.float32))
+        shapes += [table, table, jax.ShapeDtypeStruct((2, NFREQ, LANES), jnp.float32)]
     small = [pltpu.with_memory_space_constraint(v, pltpu.HBM) for v in (freq_bins, block_starts, weights)]
     if not more:
         by_chunk = pltpu.with_memory_space_constraint(by_chunk, pltpu.HBM)
     given = pl.pallas_call(
-        lambda *refs: spectra_kernel(pieces, refs[4 : 4 + more], *refs[:4], *refs[4 + more :]),
+        lambda *refs: spectra_kernel(units, refs[4 : 4 + more], *refs[:4], *refs[4 + more :]),
         out_shape=tuple(shapes),
         in_specs=[pl.BlockSpec(memory_space=pltpu.HBM)] * 3
         + [pl.BlockSpec(memory_space=pltpu.VMEM if more else pltpu.HBM)]
@@ -291,24 +313,23 @@
             pltpu.SMEM(freq_bins.shape, jnp.int32),
             pltpu.SMEM(block_starts.shape, jnp.int32),
             pltpu.VMEM(weights.shape, jnp.float32),
-            pltpu.VMEM((2 * NBLK * NFREQ, wide), jnp.bfloat16),
-            pltpu.VMEM((2 * NBLK * NFREQ, wide), jnp.bfloat16),
             pltpu.VMEM((total, cols), jnp.bfloat16),
             pltpu.VMEM((total, cols), jnp.bfloat16),
             pltpu.VMEM((2 * NBLK * NFREQ, cols), jnp.float32),
             pltpu.SemaphoreType.DMA((3,)),
-            pltpu.VMEM((count, total, slabs, LANES), jnp.float32),
+            pltpu.VMEM((count - 1, total, slabs, LANES), jnp.float32),
             pltpu.SemaphoreType.DMA((count,)),
-        ],
+        ]
+        + ([pltpu.VMEM((len(ENTRIES), ROWS, LANES), jnp.float32)] if more else []),
         compiler_params=pltpu.CompilerParams(vmem_limit_bytes=VMEM_BYTES),
         cost_estimate=pl.CostEstimate(
-            flops=6 * 2 * NBLK * NFREQ * total * count * cols,
-            bytes_accessed=4 * (total + 2 * NBLK * NFREQ) * count * cols,
+            flops=6 * 2 * NBLK * NFREQ * total * values,
+            bytes_accessed=4 * (total + 2 * NBLK * NFREQ) * values,
             transcendentals=0,
         ),
         name="spectra",
     )(*small, by_chunk, *earlier)
-    return given[:outs], given[outs : 2 * outs], given[2 * outs :]
+    return given
 
 
 def lane_places(count):
@@ -348,46 +369,43 @@
     return total
 
 
-def gram_sums(blocks):
-    sums = {}
-    for group in GROUPS:
+def gram_steps(ref, cols, sums_ref, fresh):
+    def step(group):
+        start, stop, _ = cols.indices(ref.shape[2])
         keys = [key for key in ENTRIES if key[1] in group]
-        carry = tuple(jnp.zeros((ROWS, LANES), jnp.float32) for _ in keys)
-        for ref in blocks:
-
-            def body(k, carry, ref=ref, group=group, keys=keys):
-                cols = pl.ds(pl.multiple_of(k * LANES, LANES), LANES)
-                re = {b: ref[2 * b, :, cols] for b in range(group[0], NBLK)}
-                im = {b: ref[2 * b + 1, :, cols] for b in range(group[0], NBLK)}
-                out = []
-                for (kind, a, b), total in zip(keys, carry):
-                    if kind == 0:
-                        out.append(total + (re[a] * re[b] + im[a] * im[b]))
-                    else:
-                        out.append(total + (re[a] * im[b] - im[a] * re[b]))
-                return tuple(out)
-
-            carry = lax.fori_loop(0, ref.shape[2] // LANES, body, carry, unroll=UNROLL)
-        sums.update(zip(keys, carry))
-    return fold_lanes([sums[key] for key in ENTRIES])
+        totals = [None] * len(keys)
+        for k in range(start, stop, LANES):
+            re = {b: ref[2 * b, :, k : k + LANES] for b in range(group[0], NBLK)}
+            im = {b: ref[2 * b + 1, :, k : k + LANES] for b in range(group[0], NBLK)}
+            for i, (kind, a, b) in enumerate(keys):
+                if kind == 0:
+                    term = re[a] * re[b] + im[a] * im[b]
+                else:
+                    term = re[a] * im[b] - im[a] * re[b]
+                totals[i] = term if totals[i] is None else totals[i] + term
+        for key, total in zip(keys, totals):
+            e = ENTRIES.index(key)
+            sums_ref[e] = total if fresh else sums_ref[e] + total
+
+    return [lambda group=group: step(group) for group in GROUPS]
 
 
 def gram_kernel(count, *refs):
-    refs[-2][...] = gram_sums(refs[:count])
-
-
-def gram_call(blocks, after, passed):
+    out_ref, sums_ref = refs[-2:]
+    for i, ref in enumerate(refs[:count]):
+        for step in gram_steps(ref, slice(None), sums_ref, i == 0):
+            step()
+    out_ref[...] = fold_lanes([sums_ref[e] for e in range(len(ENTRIES))])
+
+
+def gram_call(blocks):
     count = len(blocks)
     return pl.pallas_call(
         lambda *refs: gram_kernel(count, *refs),
-        out_shape=(
-            jax.ShapeDtypeStruct((ROWS, LANES), jnp.float32),
-            jax.ShapeDtypeStruct(passed.shape, passed.dtype),
-        ),
-        in_specs=[pl.BlockSpec(memory_space=pltpu.VMEM)] * count
-        + [pl.BlockSpec(memory_space=pl.ANY)] * 2,
-        out_specs=(pl.BlockSpec(memory_space=pltpu.VMEM), pl.BlockSpec(memory_space=pl.ANY)),
-        input_output_aliases={count + 1: 1},
+        out_shape=jax.ShapeDtypeStruct((ROWS, LANES), jnp.float32),
+        in_specs=[pl.BlockSpec(memory_space=pltpu.VMEM)] * count,
+        out_specs=pl.BlockSpec(memory_space=pltpu.VMEM),
+        scratch_shapes=[pltpu.VMEM((len(ENTRIES), ROWS, LANES), jnp.float32)],
         compiler_params=pltpu.CompilerParams(vmem_limit_bytes=VMEM_BYTES),
         cost_estimate=pl.CostEstimate(
             flops=sum(block.size for block in blocks) * 4 * NBLK,
@@ -395,23 +413,23 @@
             transcendentals=0,
         ),
         name="gram",
-    )(*blocks, after, passed)
-
-
-def join_kernel(own_ref, far_ref, out_ref):
+    )(*blocks)
+
+
+def join_kernel(own_ref, far_ref, _, out_ref):
     out_ref[...] = own_ref[...] + far_ref[...]
 
 
-def join_call(own, far):
+def join_call(own, far, after):
     return pl.pallas_call(
         join_kernel,
         out_shape=jax.ShapeDtypeStruct(own.shape, own.dtype),
-        in_specs=[pl.BlockSpec(memory_space=pltpu.VMEM)] * 2,
+        in_specs=[pl.BlockSpec(memory_space=pltpu.VMEM)] * 2 + [pl.BlockSpec(memory_space=pl.ANY)],
         out_specs=pl.BlockSpec(memory_space=pltpu.VMEM),
         compiler_params=pltpu.CompilerParams(vmem_limit_bytes=VMEM_BYTES),
         cost_estimate=pl.CostEstimate(flops=JOIN_FLOPS, bytes_accessed=0, transcendentals=0),
         name="join",
-    )(own, far)
+    )(own, far, after)
 
 
 def factor_kernel(count, sum_ref, inv_ref, fac_ref):
@@ -477,14 +495,14 @@
     )(total)
 
 
-def project_chunk(slabs, inv_ref, own_ref, far_ref, first, flat):
+def project_chunk(slabs, inv_ref, spots, flat):
     band = lax.axis_index("band")
     per = flat.shape[0] // ROWS
-    for side, ref in enumerate((own_ref, far_ref)):
+    for side in range(2):
         base = (band if side == 0 else 1 - band) * slabs
-        for l0 in range(0, slabs, 2):
-            both = range(l0, l0 + 2)
-            cols = [pl.ds(pl.multiple_of(first + l * LANES, LANES), LANES) for l in both]
+        for l0, (refs, first) in zip(range(0, slabs, 2), spots):
+            ref = refs[side]
+            cols = [slice(first + i * LANES, first + (i + 1) * LANES) for i in range(2)]
             re = [[ref[2 * a, :, at] for a in range(NBLK)] for at in cols]
             im = [[ref[2 * a + 1, :, at] for a in range(NBLK)] for at in cols]
             for b in range(NBLK):
@@ -503,42 +521,29 @@
                         flat[pl.ds(line, ROWS, stride=per), :] = value
 
 
-def project_kernel(slabs, at, sizes, inv_ref, *refs):
+def project_kernel(slabs, pairs, inv_ref, *refs):
     out_ref, held, sems = refs[-3:]
     per = (2 * NBLK + PAD) * 2 * slabs
-
-    def copy_of(i):
-        return pltpu.make_async_copy(held.at[i, :, : 2 * NBLK], out_ref.at[:, :, at + i], sems.at[i])
-
-    done = 0
-    for piece, size in enumerate(sizes):
-        own_ref, far_ref = refs[2 * piece : 2 * piece + 2]
-
-        def body(i, _, own_ref=own_ref, far_ref=far_ref, done=done):
-            flat = held.at[done + i].reshape(ROWS * per, LANES)
-            project_chunk(slabs, inv_ref, own_ref, far_ref, i * slabs * LANES, flat)
-            copy_of(done + i).start()
-            return 0
-
-        lax.fori_loop(0, size, body, 0)
-        done += size
-    for i in range(done):
-        copy_of(i).wait()
-
-
-def project_call(inv, pairs, modes, at, slabs, chunks):
-    sizes = [own.shape[2] // (slabs * LANES) for own, _ in pairs]
-    count = sum(sizes)
-    given = [] if modes is None else [modes]
-    arrays = [array for pair in pairs for array in pair]
-    values = sum(array.size for array in arrays)
+    copies = []
+    for i, places in enumerate(pairs):
+        spots = [(refs[2 * which : 2 * which + 2], first) for which, first in places]
+        project_chunk(slabs, inv_ref, spots, held.at[i].reshape(ROWS * per, LANES))
+        copies.append(
+            pltpu.make_async_copy(held.at[i, :, : 2 * NBLK], out_ref.at[:, :, i], sems.at[i])
+        )
+        copies[i].start()
+    for copy in copies:
+        copy.wait()
+
+
+def project_call(inv, arrays, places, slabs):
+    count = len(places)
+    values = 2 * count * slabs * LANES * ROWS * 2 * NBLK
     return pl.pallas_call(
-        lambda *refs: project_kernel(slabs, at, sizes, *refs),
-        out_shape=jax.ShapeDtypeStruct((ROWS, 2 * NBLK, chunks, 2 * slabs, LANES), jnp.float32),
-        in_specs=[pl.BlockSpec(memory_space=pltpu.VMEM)] * (1 + len(arrays))
-        + [pl.BlockSpec(memory_space=pltpu.HBM)] * len(given),
+        lambda *refs: project_kernel(slabs, places, *refs),
+        out_shape=jax.ShapeDtypeStruct((ROWS, 2 * NBLK, count, 2 * slabs, LANES), jnp.float32),
+        in_specs=[pl.BlockSpec(memory_space=pltpu.VMEM)] * (1 + len(arrays)),
         out_specs=pl.BlockSpec(memory_space=pltpu.HBM),
-        input_output_aliases={1 + len(arrays): 0} if given else {},
         scratch_shapes=[
             pltpu.VMEM((count, ROWS, 2 * NBLK + PAD, 2 * slabs, LANES), jnp.float32),
             pltpu.SemaphoreType.DMA((count,)),
@@ -548,7 +553,7 @@
             flops=4 * values * NBLK, bytes_accessed=8 * values, transcendentals=0
         ),
         name="project",
-    )(inv, *arrays, *given)
+    )(inv, *arrays)
 
 
 def swap_bands(block):
@@ -560,19 +565,26 @@
     chunks = cells // LANES
     count = 2 * slabs * cells * lax.axis_size("space")
     given = (snapshots, quad_weights, freq_bins, block_starts)
-    (send_a,), (own_a,), _ = spectra_call(*given, (1,))
+    half = slabs // 2
+    early = [(0, 0, slabs), (1, 0, half)]
+    late = [(1, half, slabs)] + [(chunk, 0, slabs) for chunk in range(2, chunks)]
+    spots = []
+    for which, units in enumerate((early, late)):
+        pairs = [(chunk, l) for chunk, low, high in units for l in range(low, high, 2)]
+        spots += [(place, which, 2 * i * LANES) for i, place in enumerate(pairs)]
+    spots = [(which, first) for _, which, first in sorted(spots)]
+    spots = [spots[half * chunk : half * (chunk + 1)] for chunk in range(chunks)]
+    send_a, own_a, *left = spectra_call(*given, early)
     far_a = swap_bands(send_a)
-    (send_b, send_c), (own_b, own_c), (gram_send,) = spectra_call(*given, (chunks - 2, 1), [send_a])
+    send_b, own_b, gram_send = spectra_call(*given, late, [send_a, *left])
     far_gram = swap_bands(gram_send)
     far_b = swap_bands(send_b)
-    gram_own, send_c = gram_call([own_a, own_b, own_c], far_a, send_c)
-    far_c = swap_bands(send_c)
-    total = join_call(gram_own, far_gram)
+    gram_own = gram_call([own_a, own_b])
+    total = join_call(gram_own, far_gram, far_a)
     for level in range(lax.axis_size("space").bit_length() - 1):
         total = total + from_partner(total, "space", level)
     inv, fac = factor_call(total, count)
-    modes = project_call(inv, [(own_a, far_a), (own_b, far_b)], None, 0, slabs, chunks)
-    modes = project_call(inv, [(own_c, far_c)], modes, chunks - 1, slabs, chunks)
+    modes = project_call(inv, [own_a, far_a, own_b, far_b], spots, slabs)
     modes = modes.reshape(ROWS, 2, NBLK, chunks, 2 * slabs, LANES)
     modes = modes.transpose(0, 1, 2, 4, 3, 5).reshape(ROWS, 2, NBLK, 2 * slabs, cells)
     factor = fac[:, :NBLK].reshape(ROWS, 2, NBLK, NBLK)

time: 34.2 us -> 33.2 us (0.971)
  Pallas kernels: 13.6 us -> 13 us
    ppermute x4 -> x3, starting transfers between devices: 6.47 us -> 5.12 us  [swap_bands(): return lax.ppermute(block, 'band', [(0, 1), (1, 0)])]
    ppermute x4, starting transfers between devices: 5.66 us -> 6.98 us  [from_partner(): return lax.ppermute(block, axis, route)]
    ppermute x4, waiting for transfers between devices: 7.22 us -> 6 us  [from_partner(): return lax.ppermute(block, axis, route)]
    ppermute x4 -> x3, waiting for transfers between devices: 0.39 us -> 1.33 us  [swap_bands(): return lax.ppermute(block, 'band', [(0, 1), (1, 0)])]
    pallas_call x5 -> x4, Pallas kernels: 12.8 us -> 12.1 us  [the longest x2 9.08 us: spectra_call(): pl.pallas_call(lambda *refs: spectra_kernel(units, refs[4:4 + more], *ref...]
  transfers between devices with their start and end apart: 8 -> 7, of which waited for: 5 -> 5; matrix products, arithmetic and copies ran while one was open for 0% -> 0% of each run, Pallas kernels for 28% -> 22%
where the time goes in v5:
time: 33.2 us; the launch traced here: 33.1 us
  Pallas kernels  13 us (39%)
  starting transfers between devices  12.1 us (36%)
  waiting for transfers between devices  7.34 us (22%)
  between operations  0.67 us (2%)
    pallas_call x2, Pallas kernels, spectra_call(): pl.pallas_call(lambda *refs: spectra_kernel(units, refs[4:4 + more], *ref...  9.08 us
    ppermute x4, starting transfers between devices, from_partner(): return lax.ppermute(block, axis, route)  6.98 us
    ppermute x4, waiting for transfers between devices, from_partner(): return lax.ppermute(block, axis, route)  6 us
    ppermute x3, starting transfers between devices, swap_bands(): return lax.ppermute(block, 'band', [(0, 1), (1, 0)])  5.12 us
    pallas_call x1, Pallas kernels, project_call(): pl.pallas_call(lambda *refs: project_kernel(slabs, places, *refs), out_sh...  1.94 us
    ppermute x3, waiting for transfers between devices, swap_bands(): return lax.ppermute(block, 'band', [(0, 1), (1, 0)])  1.33 us
    pallas_call x1, Pallas kernels, gram_call(): pl.pallas_call(lambda *refs: gram_kernel(count, *refs), out_shape=jax.Sha...  1.05 us
    pallas_call x1, Pallas kernels, factor_call(): pl.pallas_call(lambda *refs: factor_kernel(count, *refs), out_shape=(jax....  0.89 us
  transfers between devices with their start and end apart: 7, of which 5 were waited for; matrix products, arithmetic and copies ran while one was open for 0% of the time, Pallas kernels for 22%

profile of v5, /device:TPU:0, one launch (start us, length us, event | category | flops | bytes accessed | tf_op | source)
XLA Modules:
  0.0 33.1 jit_solution(15414061878780978502)
XLA Ops:
  0.6 0.0 copy-start
  0.6 3.9 %spectra.2 = (f32[16,8,768]{2,1,0:T(8,128)S(1)}, f32[16,8,768]{2,1,0:T(8,128)S(1)}, f32[1152,4,128]{2,1,0:T(4,128)S(1)}, bf16[256,1280]{1,0:T(8,128)(2,1)S(1)}, ...) custom-call(s32[16]{0:T(128)} %refs_0_.3, s32[8]{0:T(128)} %refs_1_.3, f32[4,512]{1,0:T(4,128)} %refs_2_.3, ...), custom_call_target="tpu_custom_call" | custom-call | flops 1358954496 | bytes 4325376 | tf_op jit(solution)/shard_map/spectra/pallas_call | solution.py:305
  4.5 3.0 %collective-permute-start.1 = (f32[16,8,768]{2,1,0:T(8,128)S(1)}, f32[16,8,768]{2,1,0:T(8,128)S(1)}, u32[]{:S(2)}, u32[]{:S(2)}) collective-permute-start(f32[16,8,768]{2,1,0:T(8,128)S(1)} %get-tuple-element.14.refs_4_), channel_id=1, source_target_pairs={{0,16},{16,0},{1,17},{17,1},{2,18},{18,2},{3,19},{19,3},{4,20},{20... | collective-permute-start | bytes 1179656 | tf_op jit(solution)/shard_map/ppermute | solution.py:560
  7.5 0.0 copy-done
  7.5 5.2 %spectra.3 = (f32[16,8,1280]{2,1,0:T(8,128)S(1)}, f32[16,8,1280]{2,1,0:T(8,128)S(1)}, f32[8,128]{1,0:T(8,128)S(1)}) custom-call(s32[16]{0:T(128)} %refs_0_.3, s32[8]{0:T(128)} %refs_1_.3, f32[4,512]{1,0:T(4,128)} %refs_2_.3, f32[1152,4,4,128]{3,2,1,0:T(4,128)S(1)} %bitcast.11, f32[16,8,768]{2,1,0:T(8,128)S(1)} %get-tuple-element.14.refs_4_, ...), custom_call_target="tpu_custom_call" | custom-call | flops 2264924160 | bytes 7208960 | tf_op jit(solution)/shard_map/spectra/pallas_call | solution.py:305
  12.8 1.3 %collective-permute-start = (f32[8,128]{1,0:T(8,128)S(1)}, f32[8,128]{1,0:T(8,128)S(1)}, u32[]{:S(2)}, u32[]{:S(2)}) collective-permute-start(f32[8,128]{1,0:T(8,128)S(1)} %get-tuple-element.20), channel_id=1, source_target_pairs={{0,16},{16,0},{1,17},{17,1},{2,18},{18,2},{3,19},{19,3},{4,20},{20... | collective-permute-start | bytes 12296 | tf_op jit(solution)/shard_map/ppermute | solution.py:560
  14.0 0.8 %collective-permute-start.6 = (f32[16,8,1280]{2,1,0:T(8,128)S(1)}, f32[16,8,1280]{2,1,0:T(8,128)S(1)}, u32[]{:S(2)}, u32[]{:S(2)}) collective-permute-start(f32[16,8,1280]{2,1,0:T(8,128)S(1)} %get-tuple-element.23), channel_id=1, source_target_pairs={{0,16},{16,0},{1,17},{17,1},{2,18},{18,2},{3,19},{19,3},{4,20},{20... | collective-permute-start | bytes 1966088 | tf_op jit(solution)/shard_map/ppermute | solution.py:560
  14.9 1.1 %gram.1.own_ref = f32[8,128]{1,0:T(8,128)S(1)} custom-call(f32[16,8,768]{2,1,0:T(8,128)S(1)} %get-tuple-element.13.refs_0_.refs_1_, f32[16,8,1280]{2,1,0:T(8,128)S(1)} %get-tuple-element.19.refs_1_.refs_3_), custom_call_target="tpu_custom_call" | custom-call | flops 8388608 | bytes 1048576 | tf_op jit(solution)/shard_map/gram/pallas_call | solution.py:403
  15.9 1.3 %collective-permute-done.far_ref = f32[8,128]{1,0:T(8,128)S(1)} collective-permute-done((f32[8,128]{1,0:T(8,128)S(1)}, f32[8,128]{1,0:T(8,128)S(1)}, u32[]{:S(2)}, u32[]{:S(2)}) %collective-permute-start) | collective-permute-done | bytes 4128 | tf_op jit(solution)/shard_map/ppermute | solution.py:560
  17.2 0.0 collective-permute-done.1._.refs_2_
  17.2 0.0 collective-permute-start.2
  17.3 1.2 %collective-permute-done.2 = f32[8,128]{1,0:T(8,128)S(1)} collective-permute-done((f32[8,128]{1,0:T(8,128)S(1)}, f32[8,128]{1,0:T(8,128)S(1)}, u32[]{:S(2)}, u32[]{:S(2)}) %collective-permute-start.2) | collective-permute-done | bytes 4128 | tf_op jit(solution)/shard_map/ppermute | solution.py:33
  18.4 1.9 %collective-permute-start.3 = (f32[8,128]{1,0:T(8,128)S(1)}, f32[8,128]{1,0:T(8,128)S(1)}, u32[]{:S(2)}, u32[]{:S(2)}) collective-permute-start(f32[8,128]{1,0:T(8,128)S(1)} %add.12), channel_id=1, source_target_pairs={{0,2},{2,0},{1,3},{3,1},{4,6},{6,4},{5,7},{7,5},{8,10},{10,8},{9,1... | collective-permute-start | bytes 12296 | tf_op jit(solution)/shard_map/ppermute | solution.py:33
  20.4 1.7 %collective-permute-done.3 = f32[8,128]{1,0:T(8,128)S(1)} collective-permute-done((f32[8,128]{1,0:T(8,128)S(1)}, f32[8,128]{1,0:T(8,128)S(1)}, u32[]{:S(2)}, u32[]{:S(2)}) %collective-permute-start.3) | collective-permute-done | bytes 4128 | tf_op jit(solution)/shard_map/ppermute | solution.py:33
  22.0 2.0 %collective-permute-start.4 = (f32[8,128]{1,0:T(8,128)S(1)}, f32[8,128]{1,0:T(8,128)S(1)}, u32[]{:S(2)}, u32[]{:S(2)}) collective-permute-start(f32[8,128]{1,0:T(8,128)S(1)} %add.13), channel_id=1, source_target_pairs={{0,4},{4,0},{1,5},{5,1},{2,6},{6,2},{3,7},{7,3},{8,12},{12,8},{9,1... | collective-permute-start | bytes 12296 | tf_op jit(solution)/shard_map/ppermute | solution.py:33
  24.0 1.6 %collective-permute-done.4 = f32[8,128]{1,0:T(8,128)S(1)} collective-permute-done((f32[8,128]{1,0:T(8,128)S(1)}, f32[8,128]{1,0:T(8,128)S(1)}, u32[]{:S(2)}, u32[]{:S(2)}) %collective-permute-start.4) | collective-permute-done | bytes 4128 | tf_op jit(solution)/shard_map/ppermute | solution.py:33
  25.6 3.0 %collective-permute-start.5 = (f32[8,128]{1,0:T(8,128)S(1)}, f32[8,128]{1,0:T(8,128)S(1)}, u32[]{:S(2)}, u32[]{:S(2)}) collective-permute-start(f32[8,128]{1,0:T(8,128)S(1)} %add.14), channel_id=1, source_target_pairs={{0,8},{8,0},{1,9},{9,1},{2,10},{10,2},{3,11},{11,3},{4,12},{12,4},... | collective-permute-start | bytes 12296 | tf_op jit(solution)/shard_map/ppermute | solution.py:33
  28.7 1.6 %collective-permute-done.5 = f32[8,128]{1,0:T(8,128)S(1)} collective-permute-done((f32[8,128]{1,0:T(8,128)S(1)}, f32[8,128]{1,0:T(8,128)S(1)}, u32[]{:S(2)}, u32[]{:S(2)}) %collective-permute-start.5) | collective-permute-done | bytes 4128 | tf_op jit(solution)/shard_map/ppermute | solution.py:33
  30.3 0.9 %factor.1 = (f32[64,8,128]{2,1,0:T(8,128)S(1)}, f32[128,128]{1,0:T(8,128)}) custom-call(f32[8,128]{1,0:T(8,128)S(1)} %add.15.refs_0_), custom_call_target="tpu_custom_call" | custom-call | tf_op jit(solution)/shard_map/factor/pallas_call | solution.py:485
  31.1 0.0 collective-permute-done.6.refs_4_
  31.1 1.9 %project.1 = f32[8,16,4,8,128]{4,3,2,1,0:T(8,128)} custom-call(f32[64,8,128]{2,1,0:T(8,128)S(1)} %get-tuple-element.22.refs_0_, f32[16,8,768]{2,1,0:T(8,128)S(1)} %get-tuple-element.13.refs_0_.refs_1_, f32[16,8,768]{2,1,0:T(8,128)S(1)} %collective-permute-done.1._.refs_2_, f32[16,8,1280]{2,1,0:T(8,128)S(1)} %get-tuple-element.19.refs_1_.refs_3_, ...), custom_call_target="tpu_custom_call" | custom-call | flops 16777216 | bytes 4194304 | tf_op jit(solution)/shard_map/project/pallas_call | solution.py:542
  (5 shorter events, 0.0 us)
Async XLA Ops:
  0.6 6.9 %copy-start = (f32[1152,4,512]{2,1,0:T(4,128)S(1)}, f32[1152,4,512]{2,1,0:T(4,128)}, u32[]{:S(2)}) copy-start(f32[1152,4,512]{2,1,0:T(4,128)} %param.4) | copy-start | bytes 28311556
  4.5 12.7 %collective-permute-start.1 = (f32[16,8,768]{2,1,0:T(8,128)S(1)}, f32[16,8,768]{2,1,0:T(8,128)S(1)}, u32[]{:S(2)}, u32[]{:S(2)}) collective-permute-start(f32[16,8,768]{2,1,0:T(8,128)S(1)} %get-tuple-element.14.refs_4_), channel_id=1, source_target_pairs={{0,16},{16,0},{1,17},{17,1},{2,18},{18,2},{3,19},{19,3},{4,20},{20... | collective-permute-start | bytes 1179656 | tf_op jit(solution)/shard_map/ppermute | solution.py:560
  12.8 4.5 %collective-permute-start = (f32[8,128]{1,0:T(8,128)S(1)}, f32[8,128]{1,0:T(8,128)S(1)}, u32[]{:S(2)}, u32[]{:S(2)}) collective-permute-start(f32[8,128]{1,0:T(8,128)S(1)} %get-tuple-element.20), channel_id=1, source_target_pairs={{0,16},{16,0},{1,17},{17,1},{2,18},{18,2},{3,19},{19,3},{4,20},{20... | collective-permute-start | bytes 12296 | tf_op jit(solution)/shard_map/ppermute | solution.py:560
  14.0 17.1 %collective-permute-start.6 = (f32[16,8,1280]{2,1,0:T(8,128)S(1)}, f32[16,8,1280]{2,1,0:T(8,128)S(1)}, u32[]{:S(2)}, u32[]{:S(2)}) collective-permute-start(f32[16,8,1280]{2,1,0:T(8,128)S(1)} %get-tuple-element.23), channel_id=1, source_target_pairs={{0,16},{16,0},{1,17},{17,1},{2,18},{18,2},{3,19},{19,3},{4,20},{20... | collective-permute-start | bytes 1966088 | tf_op jit(solution)/shard_map/ppermute | solution.py:560
  17.2 1.2 %collective-permute-start.2 = (f32[8,128]{1,0:T(8,128)S(1)}, f32[8,128]{1,0:T(8,128)S(1)}, u32[]{:S(2)}, u32[]{:S(2)}) collective-permute-start(f32[8,128]{1,0:T(8,128)S(1)} %join.1), channel_id=1, source_target_pairs={{0,1},{1,0},{2,3},{3,2},{4,5},{5,4},{6,7},{7,6},{8,9},{9,8},{10,11... | collective-permute-start | bytes 12296 | tf_op jit(solution)/shard_map/ppermute | solution.py:33
  18.4 3.6 %collective-permute-start.3 = (f32[8,128]{1,0:T(8,128)S(1)}, f32[8,128]{1,0:T(8,128)S(1)}, u32[]{:S(2)}, u32[]{:S(2)}) collective-permute-start(f32[8,128]{1,0:T(8,128)S(1)} %add.12), channel_id=1, source_target_pairs={{0,2},{2,0},{1,3},{3,1},{4,6},{6,4},{5,7},{7,5},{8,10},{10,8},{9,1... | collective-permute-start | bytes 12296 | tf_op jit(solution)/shard_map/ppermute | solution.py:33
  22.0 3.6 %collective-permute-start.4 = (f32[8,128]{1,0:T(8,128)S(1)}, f32[8,128]{1,0:T(8,128)S(1)}, u32[]{:S(2)}, u32[]{:S(2)}) collective-permute-start(f32[8,128]{1,0:T(8,128)S(1)} %add.13), channel_id=1, source_target_pairs={{0,4},{4,0},{1,5},{5,1},{2,6},{6,2},{3,7},{7,3},{8,12},{12,8},{9,1... | collective-permute-start | bytes 12296 | tf_op jit(solution)/shard_map/ppermute | solution.py:33
  25.6 4.6 %collective-permute-start.5 = (f32[8,128]{1,0:T(8,128)S(1)}, f32[8,128]{1,0:T(8,128)S(1)}, u32[]{:S(2)}, u32[]{:S(2)}) collective-permute-start(f32[8,128]{1,0:T(8,128)S(1)} %add.14), channel_id=1, source_target_pairs={{0,8},{8,0},{1,9},{9,1},{2,10},{10,2},{3,11},{11,3},{4,12},{12,4},... | collective-permute-start | bytes 12296 | tf_op jit(solution)/shard_map/ppermute | solution.py:33

commit v6 on v5

--- a/solution.py
+++ b/solution.py
@@ -254,7 +254,7 @@
         for i, (chunk, _, _) in enumerate(units)
         if i != place or not earlier
     ]
-    for copy in copies:
+    for copy in copies if earlier else copies[:1]:
         copy.start()
     for copy in small:
         copy.wait()
@@ -265,6 +265,8 @@
         sums = fill_table(freq_ref, start_ref, high_ref, low_ref)
         for p in range(2):
             sums_ref[p] = jnp.broadcast_to(sums[p], (NFREQ, LANES))
+        for copy in copies[1:]:
+            copy.start()
     beside = gram_steps(earlier[0], slice(None), rest[0], True) if earlier else []
     at = 0
     for i, (chunk, low, high) in enumerate(units):

time: 33.2 us -> 33.2 us (level)
  no operation moved by 1% of the time
where the time goes in v6:
time: 33.2 us; the launch traced here: 33.1 us
  Pallas kernels  12.9 us (39%)
  starting transfers between devices  12.1 us (36%)
  waiting for transfers between devices  7.35 us (22%)
  between operations  0.67 us (2%)
    pallas_call x2, Pallas kernels, spectra_call(): pl.pallas_call(lambda *refs: spectra_kernel(units, refs[4:4 + more], *ref...  9.07 us
    ppermute x4, starting transfers between devices, from_partner(): return lax.ppermute(block, axis, route)  6.97 us
    ppermute x4, waiting for transfers between devices, from_partner(): return lax.ppermute(block, axis, route)  6.01 us
    ppermute x3, starting transfers between devices, swap_bands(): return lax.ppermute(block, 'band', [(0, 1), (1, 0)])  5.12 us
    pallas_call x1, Pallas kernels, project_call(): pl.pallas_call(lambda *refs: project_kernel(slabs, places, *refs), out_sh...  1.94 us
    ppermute x3, waiting for transfers between devices, swap_bands(): return lax.ppermute(block, 'band', [(0, 1), (1, 0)])  1.34 us
    pallas_call x1, Pallas kernels, gram_call(): pl.pallas_call(lambda *refs: gram_kernel(count, *refs), out_shape=jax.Sha...  1.05 us
    pallas_call x1, Pallas kernels, factor_call(): pl.pallas_call(lambda *refs: factor_kernel(count, *refs), out_shape=(jax....  0.89 us
  transfers between devices with their start and end apart: 7, of which 5 were waited for; matrix products, arithmetic and copies ran while one was open for 0% of the time, Pallas kernels for 22%

profile of v6, /device:TPU:0, one launch (start us, length us, event | category | flops | bytes accessed | tf_op | source)
XLA Modules:
  0.0 33.1 jit_solution(14313170370005320445)
XLA Ops:
  0.6 0.0 copy-start
  0.6 3.9 %spectra.2 = (f32[16,8,768]{2,1,0:T(8,128)S(1)}, f32[16,8,768]{2,1,0:T(8,128)S(1)}, f32[1152,4,128]{2,1,0:T(4,128)S(1)}, bf16[256,1280]{1,0:T(8,128)(2,1)S(1)}, ...) custom-call(s32[16]{0:T(128)} %refs_0_.3, s32[8]{0:T(128)} %refs_1_.3, f32[4,512]{1,0:T(4,128)} %refs_2_.3, ...), custom_call_target="tpu_custom_call" | custom-call | flops 1358954496 | bytes 4325376 | tf_op jit(solution)/shard_map/spectra/pallas_call | solution.py:307
  4.5 3.0 %collective-permute-start.1 = (f32[16,8,768]{2,1,0:T(8,128)S(1)}, f32[16,8,768]{2,1,0:T(8,128)S(1)}, u32[]{:S(2)}, u32[]{:S(2)}) collective-permute-start(f32[16,8,768]{2,1,0:T(8,128)S(1)} %get-tuple-element.14.refs_4_), channel_id=1, source_target_pairs={{0,16},{16,0},{1,17},{17,1},{2,18},{18,2},{3,19},{19,3},{4,20},{20... | collective-permute-start | bytes 1179656 | tf_op jit(solution)/shard_map/ppermute | solution.py:562
  7.5 0.0 copy-done
  7.5 5.2 %spectra.3 = (f32[16,8,1280]{2,1,0:T(8,128)S(1)}, f32[16,8,1280]{2,1,0:T(8,128)S(1)}, f32[8,128]{1,0:T(8,128)S(1)}) custom-call(s32[16]{0:T(128)} %refs_0_.3, s32[8]{0:T(128)} %refs_1_.3, f32[4,512]{1,0:T(4,128)} %refs_2_.3, f32[1152,4,4,128]{3,2,1,0:T(4,128)S(1)} %bitcast.11, f32[16,8,768]{2,1,0:T(8,128)S(1)} %get-tuple-element.14.refs_4_, ...), custom_call_target="tpu_custom_call" | custom-call | flops 2264924160 | bytes 7208960 | tf_op jit(solution)/shard_map/spectra/pallas_call | solution.py:307
  12.8 1.3 %collective-permute-start = (f32[8,128]{1,0:T(8,128)S(1)}, f32[8,128]{1,0:T(8,128)S(1)}, u32[]{:S(2)}, u32[]{:S(2)}) collective-permute-start(f32[8,128]{1,0:T(8,128)S(1)} %get-tuple-element.20), channel_id=1, source_target_pairs={{0,16},{16,0},{1,17},{17,1},{2,18},{18,2},{3,19},{19,3},{4,20},{20... | collective-permute-start | bytes 12296 | tf_op jit(solution)/shard_map/ppermute | solution.py:562
  14.0 0.8 %collective-permute-start.6 = (f32[16,8,1280]{2,1,0:T(8,128)S(1)}, f32[16,8,1280]{2,1,0:T(8,128)S(1)}, u32[]{:S(2)}, u32[]{:S(2)}) collective-permute-start(f32[16,8,1280]{2,1,0:T(8,128)S(1)} %get-tuple-element.23), channel_id=1, source_target_pairs={{0,16},{16,0},{1,17},{17,1},{2,18},{18,2},{3,19},{19,3},{4,20},{20... | collective-permute-start | bytes 1966088 | tf_op jit(solution)/shard_map/ppermute | solution.py:562
  14.9 1.1 %gram.1.own_ref = f32[8,128]{1,0:T(8,128)S(1)} custom-call(f32[16,8,768]{2,1,0:T(8,128)S(1)} %get-tuple-element.13.refs_0_.refs_1_, f32[16,8,1280]{2,1,0:T(8,128)S(1)} %get-tuple-element.19.refs_1_.refs_3_), custom_call_target="tpu_custom_call" | custom-call | flops 8388608 | bytes 1048576 | tf_op jit(solution)/shard_map/gram/pallas_call | solution.py:405
  15.9 1.3 %collective-permute-done.far_ref = f32[8,128]{1,0:T(8,128)S(1)} collective-permute-done((f32[8,128]{1,0:T(8,128)S(1)}, f32[8,128]{1,0:T(8,128)S(1)}, u32[]{:S(2)}, u32[]{:S(2)}) %collective-permute-start) | collective-permute-done | bytes 4128 | tf_op jit(solution)/shard_map/ppermute | solution.py:562
  17.2 0.0 collective-permute-done.1._.refs_2_
  17.2 0.0 collective-permute-start.2
  17.3 1.2 %collective-permute-done.2 = f32[8,128]{1,0:T(8,128)S(1)} collective-permute-done((f32[8,128]{1,0:T(8,128)S(1)}, f32[8,128]{1,0:T(8,128)S(1)}, u32[]{:S(2)}, u32[]{:S(2)}) %collective-permute-start.2) | collective-permute-done | bytes 4128 | tf_op jit(solution)/shard_map/ppermute | solution.py:33
  18.4 1.9 %collective-permute-start.3 = (f32[8,128]{1,0:T(8,128)S(1)}, f32[8,128]{1,0:T(8,128)S(1)}, u32[]{:S(2)}, u32[]{:S(2)}) collective-permute-start(f32[8,128]{1,0:T(8,128)S(1)} %add.12), channel_id=1, source_target_pairs={{0,2},{2,0},{1,3},{3,1},{4,6},{6,4},{5,7},{7,5},{8,10},{10,8},{9,1... | collective-permute-start | bytes 12296 | tf_op jit(solution)/shard_map/ppermute | solution.py:33
  20.4 1.7 %collective-permute-done.3 = f32[8,128]{1,0:T(8,128)S(1)} collective-permute-done((f32[8,128]{1,0:T(8,128)S(1)}, f32[8,128]{1,0:T(8,128)S(1)}, u32[]{:S(2)}, u32[]{:S(2)}) %collective-permute-start.3) | collective-permute-done | bytes 4128 | tf_op jit(solution)/shard_map/ppermute | solution.py:33
  22.0 2.0 %collective-permute-start.4 = (f32[8,128]{1,0:T(8,128)S(1)}, f32[8,128]{1,0:T(8,128)S(1)}, u32[]{:S(2)}, u32[]{:S(2)}) collective-permute-start(f32[8,128]{1,0:T(8,128)S(1)} %add.13), channel_id=1, source_target_pairs={{0,4},{4,0},{1,5},{5,1},{2,6},{6,2},{3,7},{7,3},{8,12},{12,8},{9,1... | collective-permute-start | bytes 12296 | tf_op jit(solution)/shard_map/ppermute | solution.py:33
  24.1 1.6 %collective-permute-done.4 = f32[8,128]{1,0:T(8,128)S(1)} collective-permute-done((f32[8,128]{1,0:T(8,128)S(1)}, f32[8,128]{1,0:T(8,128)S(1)}, u32[]{:S(2)}, u32[]{:S(2)}) %collective-permute-start.4) | collective-permute-done | bytes 4128 | tf_op jit(solution)/shard_map/ppermute | solution.py:33
  25.6 3.0 %collective-permute-start.5 = (f32[8,128]{1,0:T(8,128)S(1)}, f32[8,128]{1,0:T(8,128)S(1)}, u32[]{:S(2)}, u32[]{:S(2)}) collective-permute-start(f32[8,128]{1,0:T(8,128)S(1)} %add.14), channel_id=1, source_target_pairs={{0,8},{8,0},{1,9},{9,1},{2,10},{10,2},{3,11},{11,3},{4,12},{12,4},... | collective-permute-start | bytes 12296 | tf_op jit(solution)/shard_map/ppermute | solution.py:33
  28.7 1.6 %collective-permute-done.5 = f32[8,128]{1,0:T(8,128)S(1)} collective-permute-done((f32[8,128]{1,0:T(8,128)S(1)}, f32[8,128]{1,0:T(8,128)S(1)}, u32[]{:S(2)}, u32[]{:S(2)}) %collective-permute-start.5) | collective-permute-done | bytes 4128 | tf_op jit(solution)/shard_map/ppermute | solution.py:33
  30.3 0.9 %factor.1 = (f32[64,8,128]{2,1,0:T(8,128)S(1)}, f32[128,128]{1,0:T(8,128)}) custom-call(f32[8,128]{1,0:T(8,128)S(1)} %add.15.refs_0_), custom_call_target="tpu_custom_call" | custom-call | tf_op jit(solution)/shard_map/factor/pallas_call | solution.py:487
  31.1 0.0 collective-permute-done.6.refs_4_
  31.1 1.9 %project.1 = f32[8,16,4,8,128]{4,3,2,1,0:T(8,128)} custom-call(f32[64,8,128]{2,1,0:T(8,128)S(1)} %get-tuple-element.22.refs_0_, f32[16,8,768]{2,1,0:T(8,128)S(1)} %get-tuple-element.13.refs_0_.refs_1_, f32[16,8,768]{2,1,0:T(8,128)S(1)} %collective-permute-done.1._.refs_2_, f32[16,8,1280]{2,1,0:T(8,128)S(1)} %get-tuple-element.19.refs_1_.refs_3_, ...), custom_call_target="tpu_custom_call" | custom-call | flops 16777216 | bytes 4194304 | tf_op jit(solution)/shard_map/project/pallas_call | solution.py:544
  (5 shorter events, 0.0 us)
Async XLA Ops:
  0.6 6.9 %copy-start = (f32[1152,4,512]{2,1,0:T(4,128)S(1)}, f32[1152,4,512]{2,1,0:T(4,128)}, u32[]{:S(2)}) copy-start(f32[1152,4,512]{2,1,0:T(4,128)} %param.4) | copy-start | bytes 28311556
  4.5 12.7 %collective-permute-start.1 = (f32[16,8,768]{2,1,0:T(8,128)S(1)}, f32[16,8,768]{2,1,0:T(8,128)S(1)}, u32[]{:S(2)}, u32[]{:S(2)}) collective-permute-start(f32[16,8,768]{2,1,0:T(8,128)S(1)} %get-tuple-element.14.refs_4_), channel_id=1, source_target_pairs={{0,16},{16,0},{1,17},{17,1},{2,18},{18,2},{3,19},{19,3},{4,20},{20... | collective-permute-start | bytes 1179656 | tf_op jit(solution)/shard_map/ppermute | solution.py:562
  12.8 4.5 %collective-permute-start = (f32[8,128]{1,0:T(8,128)S(1)}, f32[8,128]{1,0:T(8,128)S(1)}, u32[]{:S(2)}, u32[]{:S(2)}) collective-permute-start(f32[8,128]{1,0:T(8,128)S(1)} %get-tuple-element.20), channel_id=1, source_target_pairs={{0,16},{16,0},{1,17},{17,1},{2,18},{18,2},{3,19},{19,3},{4,20},{20... | collective-permute-start | bytes 12296 | tf_op jit(solution)/shard_map/ppermute | solution.py:562
  14.0 17.1 %collective-permute-start.6 = (f32[16,8,1280]{2,1,0:T(8,128)S(1)}, f32[16,8,1280]{2,1,0:T(8,128)S(1)}, u32[]{:S(2)}, u32[]{:S(2)}) collective-permute-start(f32[16,8,1280]{2,1,0:T(8,128)S(1)} %get-tuple-element.23), channel_id=1, source_target_pairs={{0,16},{16,0},{1,17},{17,1},{2,18},{18,2},{3,19},{19,3},{4,20},{20... | collective-permute-start | bytes 1966088 | tf_op jit(solution)/shard_map/ppermute | solution.py:562
  17.2 1.2 %collective-permute-start.2 = (f32[8,128]{1,0:T(8,128)S(1)}, f32[8,128]{1,0:T(8,128)S(1)}, u32[]{:S(2)}, u32[]{:S(2)}) collective-permute-start(f32[8,128]{1,0:T(8,128)S(1)} %join.1), channel_id=1, source_target_pairs={{0,1},{1,0},{2,3},{3,2},{4,5},{5,4},{6,7},{7,6},{8,9},{9,8},{10,11... | collective-permute-start | bytes 12296 | tf_op jit(solution)/shard_map/ppermute | solution.py:33
  18.4 3.6 %collective-permute-start.3 = (f32[8,128]{1,0:T(8,128)S(1)}, f32[8,128]{1,0:T(8,128)S(1)}, u32[]{:S(2)}, u32[]{:S(2)}) collective-permute-start(f32[8,128]{1,0:T(8,128)S(1)} %add.12), channel_id=1, source_target_pairs={{0,2},{2,0},{1,3},{3,1},{4,6},{6,4},{5,7},{7,5},{8,10},{10,8},{9,1... | collective-permute-start | bytes 12296 | tf_op jit(solution)/shard_map/ppermute | solution.py:33
  22.0 3.6 %collective-permute-start.4 = (f32[8,128]{1,0:T(8,128)S(1)}, f32[8,128]{1,0:T(8,128)S(1)}, u32[]{:S(2)}, u32[]{:S(2)}) collective-permute-start(f32[8,128]{1,0:T(8,128)S(1)} %add.13), channel_id=1, source_target_pairs={{0,4},{4,0},{1,5},{5,1},{2,6},{6,2},{3,7},{7,3},{8,12},{12,8},{9,1... | collective-permute-start | bytes 12296 | tf_op jit(solution)/shard_map/ppermute | solution.py:33
  25.6 4.6 %collective-permute-start.5 = (f32[8,128]{1,0:T(8,128)S(1)}, f32[8,128]{1,0:T(8,128)S(1)}, u32[]{:S(2)}, u32[]{:S(2)}) collective-permute-start(f32[8,128]{1,0:T(8,128)S(1)} %add.14), channel_id=1, source_target_pairs={{0,8},{8,0},{1,9},{9,1},{2,10},{10,2},{3,11},{11,3},{4,12},{12,4},... | collective-permute-start | bytes 12296 | tf_op jit(solution)/shard_map/ppermute | solution.py:33
